TPU v7x, 128 devices: a whole 4x4x4 slice. The times are simulated.
128 devices in a mesh: row: 16 (over x_hi, y, core), col: 8 (over z, x_lo).
Axes of the slice: x: 4 (x_hi: 2, x_lo: 2; x = x_hi * 2 + x_lo), y: 4, z: 4, core: 2. Of those that a mesh axis runs over, the one named last changes fastest.
Arguments:
- blocks: bfloat16 [640, 24, 128, 128], P(('row', 'col')), may hold values from -0.8984375 to 0.8984375
- pattern: int32 [640, 24], P(('row', 'col')), may hold values from 0 to 639, as said below
- owner: int32 [15360, 1], P(('row', 'col')), may hold values from 0 to 127; in each aligned block of 120 rows (0 to 119, 120 to 239, ...) at most 2 rows name the same one
Outputs:
- owned_blocks: bfloat16 [32768, 128, 128], P(('row', 'col'))
- owned_ids: int32 [32768], P(('row', 'col'))
Inputs may be any that keep to these rules, and one draw needn't show every extreme that they name: `pattern`: the 24 indices of a block row are distinct, and each names a block row held by the device of that row or by one of its eight neighbours on the periodic 16 by 8 device grid. Among the blocks of one device's block rows, at most 2 name the same owner; some owner receives exactly 2 from some device.
All inputs are finite; a program needn't handle non-finite values.
Results may differ from a plain program's by a relative error of at most 0.001.
Values may be sent and summed in bfloat16 or wider, within the bound.
No kernel may reach another device: no remote copies, remote signals or barrier semaphores. Data moves between devices by JAX's collectives and lax.ppermute only.
A program may use at most 192 MiB of HBM per device.

v0:
```python
import jax
import jax.numpy as jnp
from jax import lax
from jax.sharding import PartitionSpec as P


def with_halo(shard, sides, width):
    for axis, dim in sides:
        devices, length = (lax.axis_size(axis), shard.shape[dim])
        up = [(i, (i + 1) % devices) for i in range(devices)]
        down = [(j, i) for i, j in up]
        last = lax.slice_in_dim(shard, length - width, length, axis=dim)
        first = lax.slice_in_dim(shard, 0, width, axis=dim)
        before = lax.ppermute(last, axis, up)
        after = lax.ppermute(first, axis, down)
        shard = jnp.concatenate([before, shard, after], axis=dim)
    return shard


def shards(blocks, pattern, owner):
    rows_here = blocks.shape[0]
    stored = blocks.shape[1]
    order_size = blocks.shape[2]
    count_row = lax.axis_size("row")
    count_col = lax.axis_size("col")
    devices = count_row * count_col
    grid_row = lax.axis_index("row")
    grid_col = lax.axis_index("col")
    device_here = grid_row * count_col + grid_col
    framed, framed_cols = (
        with_halo(blocks[None, None], (("row", 0), ("col", 1)), 1),
        with_halo(pattern[None, None], (("row", 0), ("col", 1)), 1),
    )
    pool_blocks = framed.reshape(9 * rows_here * stored, order_size, order_size)
    pool_cols = framed_cols.reshape(9 * rows_here, stored)

    def locate(global_rows):
        holder = global_rows // rows_here
        local_row = global_rows % rows_here
        delta_row = (holder // count_col - grid_row + count_row) % count_row
        delta_col = (holder % count_col - grid_col + count_col) % count_col
        frame_row = jnp.where(delta_row == 0, 1, jnp.where(delta_row == 1, 2, 0))
        frame_col = jnp.where(delta_col == 0, 1, jnp.where(delta_col == 1, 2, 0))
        return (frame_row * 3 + frame_col) * rows_here + local_row

    def one_row(row_local):
        row_cols = pattern[row_local]
        pool_rows = locate(row_cols)
        inner_cols = pool_cols[pool_rows]
        matches = inner_cols[:, None, :] == row_cols[None, :, None]
        found = jnp.any(matches, axis=2)
        where_slot = jnp.argmax(matches, axis=2)
        picked = pool_blocks[pool_rows[:, None] * stored + where_slot]
        picked = jnp.where(found[:, :, None, None], picked, jnp.zeros_like(picked))
        summed = jnp.einsum(
            "axy,auyz->uxz", blocks[row_local], picked, preferred_element_type=jnp.float32
        )
        return summed.astype(jnp.bfloat16)

    products = lax.map(one_row, jnp.arange(rows_here, dtype=jnp.int32))
    capacity = max(2, rows_here * stored // devices + 1)
    owners = owner.reshape(rows_here * stored)
    one_hot = (owners[:, None] == jnp.arange(devices, dtype=jnp.int32)[None, :]).astype(jnp.int32)
    running = jnp.cumsum(one_hot, axis=0) - 1
    rank = jnp.sum(running * one_hot, axis=1)
    target = owners * capacity + rank
    block_ids = device_here * rows_here * stored + jnp.arange(rows_here * stored, dtype=jnp.int32)
    outgoing = jnp.zeros((devices * capacity, order_size, order_size), jnp.bfloat16)
    outgoing = outgoing.at[target].set(products.reshape(rows_here * stored, order_size, order_size))
    outgoing_ids = jnp.full((devices * capacity,), -1, jnp.int32).at[target].set(block_ids)
    arrived, arrived_ids = (
        lax.all_to_all(
            outgoing.reshape(devices, capacity, order_size, order_size),
            ("row", "col"),
            split_axis=0,
            concat_axis=0,
            tiled=True,
        ),
        lax.all_to_all(
            outgoing_ids.reshape(devices, capacity),
            ("row", "col"),
            split_axis=0,
            concat_axis=0,
            tiled=True,
        ),
    )
    return (
        arrived.reshape(devices * capacity, order_size, order_size),
        arrived_ids.reshape(devices * capacity),
    )


def solution(mesh):
    in_specs = (
        P(("row", "col"), None, None, None),
        P(("row", "col"), None),
        P(("row", "col"), None),
    )
    out_specs = (P(("row", "col"), None, None), P(("row", "col")))
    return jax.shard_map(shards, mesh=mesh, in_specs=in_specs, out_specs=out_specs, check_vma=False)
```

profile of v0, /device:TPU:0, one launch (start us, length us, event | category | flops | bytes accessed | tf_op | source)
XLA Modules:
  0.0 1076.0 jit_solution(7837824925565544468)
XLA Ops:
  0.7 5.3 collective-permute-start.5
  6.1 43.6 %collective-permute-done.4 = bf16[1,1,5,24,128,128]{5,4,3,2,1,0:T(8,128)(2,1)S(1)} collective-permute-done((bf16[1,1,5,24,128,128]{5,4,3,2,1,0:T(8,128)(2,1)}, bf16[1,1,5,24,128,128]{5,4,3,2,1,0:T(8,128)(2,1)S(1)}, u32[]{:S(2)}, u32[]{:S(2)}) %collective-permute-start.4) | collective-permute-done | bytes 3932192 | tf_op jit(solution)/shard_map/ppermute | solution.py:14
  49.7 8.4 pad_maximum_fusion.1
  58.1 1.6 collective-permute-start.6
  59.7 3.6 collective-permute-start.7
  63.2 5.4 collective-permute-start.1
  69.0 499.8 %collective-permute-done = s32[1,1,5,24]{3,2,1,0:T(8,128)S(1)} collective-permute-done((s32[1,1,5,24]{3,2,1,0:T(8,128)S(1)}, s32[1,1,5,24]{3,2,1,0:T(8,128)S(1)}, u32[]{:S(2)}, u32[]{:S(2)}) %collective-permute-start) | collective-permute-done | bytes 512 | tf_op jit(solution)/shard_map/ppermute | solution.py:14
  568.9 1.6 collective-permute-start.2
  570.5 2.6 collective-permute-start.3
  573.1 0.9 scatter_custom_fusion.1
  574.0 0.8 all_to_all.10
  574.8 5.8 all-to-all-start.1
  580.7 24.7 %pad_maximum_fusion = bf16[3,3,5,24,128,128]{5,4,3,2,1,0:T(8,128)(2,1)} fusion(bf16[3,1,5,24,128,128]{5,4,3,2,1,0:T(8,128)(2,1)} %collective-permute-done.7, bf16[1,1,5,24,128,128]{5,4,3,2,1,0:T(8,128)(2,1)} %copy-done.1, bf16[1,1,5,24,128,128]{5,4,3,2,1,0:T(8,128)(2,1)} %bitcast.83, bf16[1,1,5,24,128,128]{5,4,3,2,1,0:T(8,128)(2,1)} %copy-done, ...), kind=kLoop, calls=%fused_computation.74 | loop fusion | flops 70778880 | bytes 70778880 | tf_op jit(solution)/shard_map/concatenate | solution.py:16
  605.4 313.2 %while.13 = (s32[]{:T(128)}, bf16[5,24,128,128]{2,3,1,0:T(8,128)(2,1)}, s32[5]{0:T(128)S(1)}, s32[5,24]{1,0:T(8,128)S(1)}, s32[]{:T(128)}, /*index=5*/s32[]{:T(1...) while((s32[]{:T(128)}, ...), condition=%wide.region_5.6_spmd, body=%wide.region_2.5_spmd.sunk | while | flops 2425890816 | bytes 95982776 | solution.py:60
  605.4 0.7 dynamic_slice.37
  608.1 0.6 gather_fusion
  608.7 1.6 compare_reduce_fusion.4
  610.4 22.5 %gather_fusion.1 = bf16[576,128,128]{2,1,0:T(8,128)(2,1)} fusion(bf16[1080,128,128]{2,1,0:T(8,128)(2,1)} %get-tuple-element.275, s32[1024]{0:T(1024)S(1)} %pad_clamp_fusion.5), kind=kCustom, calls=%fused_computation.1.clone.1 | custom fusion | bytes 37751040 | tf_op jit(solution)/shard_map/while/body/eval_jaxpr/gather | solution.py:53
  632.9 24.7 %copy.18 = bf16[24,24,128,128]{2,3,0,1:T(8,128)(2,1)} copy(bf16[24,24,128,128]{3,2,1,0:T(8,128)(2,1)} %bitcast.77) | data formatting | bytes 37748736 | tf_op jit(solution)/shard_map/while/body/eval_jaxpr/gather | solution.py:53
  658.2 10.0 fusion.48
  668.3 0.6 dynamic_slice.37
  671.5 1.6 compare_reduce_fusion.4
  673.2 21.3 %gather_fusion.1 = bf16[576,128,128]{2,1,0:T(8,128)(2,1)} fusion(bf16[1080,128,128]{2,1,0:T(8,128)(2,1)} %get-tuple-element.275, s32[1024]{0:T(1024)S(1)} %pad_clamp_fusion.5), kind=kCustom, calls=%fused_computation.1.clone.1 | custom fusion | bytes 37751040 | tf_op jit(solution)/shard_map/while/body/eval_jaxpr/gather | solution.py:53
  694.6 24.7 %copy.18 = bf16[24,24,128,128]{2,3,0,1:T(8,128)(2,1)} copy(bf16[24,24,128,128]{3,2,1,0:T(8,128)(2,1)} %bitcast.77) | data formatting | bytes 37748736 | tf_op jit(solution)/shard_map/while/body/eval_jaxpr/gather | solution.py:53
  719.9 10.0 fusion.48
  729.9 0.6 dynamic_slice.37
  733.2 1.6 compare_reduce_fusion.4
  734.9 23.2 %gather_fusion.1 = bf16[576,128,128]{2,1,0:T(8,128)(2,1)} fusion(bf16[1080,128,128]{2,1,0:T(8,128)(2,1)} %get-tuple-element.275, s32[1024]{0:T(1024)S(1)} %pad_clamp_fusion.5), kind=kCustom, calls=%fused_computation.1.clone.1 | custom fusion | bytes 37751040 | tf_op jit(solution)/shard_map/while/body/eval_jaxpr/gather | solution.py:53
  758.1 24.7 %copy.18 = bf16[24,24,128,128]{2,3,0,1:T(8,128)(2,1)} copy(bf16[24,24,128,128]{3,2,1,0:T(8,128)(2,1)} %bitcast.77) | data formatting | bytes 37748736 | tf_op jit(solution)/shard_map/while/body/eval_jaxpr/gather | solution.py:53
  783.4 10.0 fusion.48
  793.4 0.6 dynamic_slice.37
  796.7 1.6 compare_reduce_fusion.4
  798.4 22.8 %gather_fusion.1 = bf16[576,128,128]{2,1,0:T(8,128)(2,1)} fusion(bf16[1080,128,128]{2,1,0:T(8,128)(2,1)} %get-tuple-element.275, s32[1024]{0:T(1024)S(1)} %pad_clamp_fusion.5), kind=kCustom, calls=%fused_computation.1.clone.1 | custom fusion | bytes 37751040 | tf_op jit(solution)/shard_map/while/body/eval_jaxpr/gather | solution.py:53
  821.2 24.7 %copy.18 = bf16[24,24,128,128]{2,3,0,1:T(8,128)(2,1)} copy(bf16[24,24,128,128]{3,2,1,0:T(8,128)(2,1)} %bitcast.77) | data formatting | bytes 37748736 | tf_op jit(solution)/shard_map/while/body/eval_jaxpr/gather | solution.py:53
  846.5 10.0 fusion.48
  856.6 0.6 dynamic_slice.37
  859.8 1.6 compare_reduce_fusion.4
  861.5 21.8 %gather_fusion.1 = bf16[576,128,128]{2,1,0:T(8,128)(2,1)} fusion(bf16[1080,128,128]{2,1,0:T(8,128)(2,1)} %get-tuple-element.275, s32[1024]{0:T(1024)S(1)} %pad_clamp_fusion.5), kind=kCustom, calls=%fused_computation.1.clone.1 | custom fusion | bytes 37751040 | tf_op jit(solution)/shard_map/while/body/eval_jaxpr/gather | solution.py:53
  883.3 24.7 %copy.18 = bf16[24,24,128,128]{2,3,0,1:T(8,128)(2,1)} copy(bf16[24,24,128,128]{3,2,1,0:T(8,128)(2,1)} %bitcast.77) | data formatting | bytes 37748736 | tf_op jit(solution)/shard_map/while/body/eval_jaxpr/gather | solution.py:53
  908.6 10.0 fusion.48
  918.7 6.3 copy.13
  924.9 5.5 broadcast_in_dim.62
  930.5 19.1 %scatter_fusion = bf16[256,128,128]{2,1,0:T(8,128)(2,1)} fusion(bf16[256,128,128]{2,1,0:T(8,128)(2,1)} %broadcast_in_dim.62, s32[120]{0:T(128)S(1)} %copy-done.5, bf16[120,128,128]{2,1,0:T(8,128)(2,1)} %copy.13), kind=kCustom, calls=%fused_computation.2 | custom fusion | bytes 11796960 | tf_op jit(solution)/shard_map/scatter | solution.py:69
  949.5 13.2 %all-to-all-start = ((bf16[128,2,128,128]{3,2,1,0:T(8,128)(2,1)}), bf16[128,2,128,128]{3,2,1,0:T(8,128)(2,1)}, u32[]{:S(2)}, u32[]{:S(2)}) async-start(bf16[128,2,128,128]{3,2,1,0:T(8,128)(2,1)} %bitcast.79), calls=%async_computation | async-start | bytes 16777216 | tf_op jit(solution)/shard_map/all_to_all | solution.py:72
  963.2 1.6 reduce.29
  964.9 0.7 reshape.314
  965.6 99.9 %all-to-all-done = bf16[128,2,128,128]{3,2,1,0:T(8,128)(2,1)} async-done(((bf16[128,2,128,128]{3,2,1,0:T(8,128)(2,1)}), bf16[128,2,128,128]{3,2,1,0:T(8,128)(2,1)}, u32[]{:S(2)}, u32[]{:S(2)}) %all-to-all-start) | async-done | bytes 8388640 | tf_op jit(solution)/shard_map/all_to_all | solution.py:72
  1065.4 10.5 copy.29
  (76 shorter events, 7.9 us)
Async XLA Ops:
  0.6 62.6 %copy-start.2 = (s32[5,24]{1,0:T(8,128)S(1)}, s32[5,24]{1,0:T(8,128)}, u32[]{:S(2)}) copy-start(s32[5,24]{1,0:T(8,128)} %param.6) | copy-start | bytes 1444
  0.6 67.9 %copy-start.3 = (s32[120,1]{0,1:T(1,128)S(1)}, s32[120,1]{0,1:T(1,128)}, u32[]{:S(2)}) copy-start(s32[120,1]{0,1:T(1,128)} %param.7) | copy-start | bytes 1444
  0.6 49.0 %collective-permute-start.4 = (bf16[1,1,5,24,128,128]{5,4,3,2,1,0:T(8,128)(2,1)}, bf16[1,1,5,24,128,128]{5,4,3,2,1,0:T(8,128)(2,1)S(1)}, u32[]{:S(2)}, u32[]{:S(2)}) collective-permute-start(bf16[1,1,5,24,128,128]{5,4,3,2,1,0:T(8,128)(2,1)} %bitcast.80), channel_id=1, source_target_pairs={{0,8},{8,16},{16,24},{24,32},{32,40},{40,48},{48,56},{56,64},{64,7... | collective-permute-start | bytes 11796488 | tf_op jit(solution)/shard_map/ppermute | solution.py:14
  0.7 48.9 %collective-permute-start.5 = (bf16[1,1,5,24,128,128]{5,4,3,2,1,0:T(8,128)(2,1)}, bf16[1,1,5,24,128,128]{5,4,3,2,1,0:T(8,128)(2,1)S(1)}, u32[]{:S(2)}, u32[]{:S(2)}) collective-permute-start(bf16[1,1,5,24,128,128]{5,4,3,2,1,0:T(8,128)(2,1)} %bitcast.81), channel_id=1, source_target_pairs={{8,0},{16,8},{24,16},{32,24},{40,32},{48,40},{56,48},{64,56},{72,6... | collective-permute-start | bytes 11796488 | tf_op jit(solution)/shard_map/ppermute | solution.py:15
  49.7 8.4 copy-start
  49.7 8.4 copy-start.1
  58.1 522.6 %collective-permute-start.6 = (bf16[3,1,5,24,128,128]{5,4,3,2,1,0:T(8,128)(2,1)}, bf16[3,1,5,24,128,128]{5,4,3,2,1,0:T(8,128)(2,1)}, u32[]{:S(2)}, u32[]{:S(2)}) collective-permute-start(bf16[3,1,5,24,128,128]{5,4,3,2,1,0:T(8,128)(2,1)} %pad_maximum_fusion.1), channel_id=1, source_target_pairs={{0,1},{1,2},{2,3},{3,4},{4,5},{5,6},{6,7},{7,0},{8,9},{9,10},{10,1... | collective-permute-start | bytes 35389448 | tf_op jit(solution)/shard_map/ppermute | solution.py:14
  59.7 521.1 %collective-permute-start.7 = (bf16[3,1,5,24,128,128]{5,4,3,2,1,0:T(8,128)(2,1)}, bf16[3,1,5,24,128,128]{5,4,3,2,1,0:T(8,128)(2,1)}, u32[]{:S(2)}, u32[]{:S(2)}) collective-permute-start(bf16[3,1,5,24,128,128]{5,4,3,2,1,0:T(8,128)(2,1)} %pad_maximum_fusion.1), channel_id=1, source_target_pairs={{1,0},{2,1},{3,2},{4,3},{5,4},{6,5},{7,6},{0,7},{9,8},{10,9},{11,1... | collective-permute-start | bytes 35389448 | tf_op jit(solution)/shard_map/ppermute | solution.py:15
  63.2 505.7 %collective-permute-start = (s32[1,1,5,24]{3,2,1,0:T(8,128)S(1)}, s32[1,1,5,24]{3,2,1,0:T(8,128)S(1)}, u32[]{:S(2)}, u32[]{:S(2)}) collective-permute-start(s32[1,1,5,24]{3,2,1,0:T(8,128)S(1)} %bitcast.85), channel_id=1, source_target_pairs={{0,8},{8,16},{16,24},{24,32},{32,40},{40,48},{48,56},{56,64},{64,7... | collective-permute-start | bytes 1448 | tf_op jit(solution)/shard_map/ppermute | solution.py:14
  63.2 505.7 %collective-permute-start.1 = (s32[1,1,5,24]{3,2,1,0:T(8,128)S(1)}, s32[1,1,5,24]{3,2,1,0:T(8,128)S(1)}, u32[]{:S(2)}, u32[]{:S(2)}) collective-permute-start(s32[1,1,5,24]{3,2,1,0:T(8,128)S(1)} %bitcast.86), channel_id=1, source_target_pairs={{8,0},{16,8},{24,16},{32,24},{40,32},{48,40},{56,48},{64,56},{72,6... | collective-permute-start | bytes 1448 | tf_op jit(solution)/shard_map/ppermute | solution.py:15
  69.0 511.7 %copy-start.4 = (s32[120]{0:T(128)}, s32[120]{0:T(128)S(1)}, u32[]{:S(2)}) copy-start(s32[120]{0:T(128)S(1)} %fusion.35) | copy-start | bytes 1444
  568.9 11.8 %collective-permute-start.2 = (s32[3,1,5,24]{3,2,1,0:T(8,128)S(1)}, s32[3,1,5,24]{3,2,1,0:T(8,128)S(1)}, u32[]{:S(2)}, u32[]{:S(2)}) collective-permute-start(s32[3,1,5,24]{3,2,1,0:T(8,128)S(1)} %pad_add_fusion.1), channel_id=1, source_target_pairs={{0,1},{1,2},{2,3},{3,4},{4,5},{5,6},{6,7},{7,0},{8,9},{9,10},{10,1... | collective-permute-start | bytes 4328 | tf_op jit(solution)/shard_map/ppermute | solution.py:14
  570.5 10.2 collective-permute-start.3
  574.8 374.7 %all-to-all-start.1 = ((s32[128,1,2]{2,1,0:T(1,128)}), s32[128,1,2]{2,1,0:T(1,128)}, u32[]{:S(2)}, u32[]{:S(2)}) async-start(s32[128,1,2]{2,1,0:T(1,128)} %bitcast.22), calls=%async_computation.1 | async-start | bytes 131072 | tf_op jit(solution)/shard_map/all_to_all | solution.py:79
  918.6 11.8 %copy-start.5 = (s32[120]{0:T(128)S(1)}, s32[120]{0:T(128)}, u32[]{:S(2)}) copy-start(s32[120]{0:T(128)} %copy-done.4) | copy-start | bytes 1444
  949.5 115.9 %all-to-all-start = ((bf16[128,2,128,128]{3,2,1,0:T(8,128)(2,1)}), bf16[128,2,128,128]{3,2,1,0:T(8,128)(2,1)}, u32[]{:S(2)}, u32[]{:S(2)}) async-start(bf16[128,2,128,128]{3,2,1,0:T(8,128)(2,1)} %bitcast.79), calls=%async_computation | async-start | bytes 16777216 | tf_op jit(solution)/shard_map/all_to_all | solution.py:72
where the time goes:
time: 1080 us
  waiting for transfers between devices  643 us (60%)
  local copies, waits for them, and re-layouts  286 us (26%)
  matrix products  50.1 us (5%)
  other arithmetic  46.7 us (4%)
  starting transfers between devices  39.1 us (4%)
    ppermute x4, waiting for transfers between devices, with_halo(): before = lax.ppermute(last, axis, up)  543 us
    gather x10, local copies, waits for them, and re-layouts, one_row(): picked = pool_blocks[pool_rows[:, None] * stored + where_slot]  235 us
    all_to_all x1, waiting for transfers between devices, shards(): lax.all_to_all(outgoing.reshape(devices, capacity, order_size, order_size...  99.9 us
    dot_general x5, matrix products, one_row(): jnp.einsum('axy,auyz->uxz', blocks[row_local], picked, preferred_element_...  50.1 us
    concatenate x4, other arithmetic, with_halo(): shard = jnp.concatenate([before, shard, after], axis=dim)  33.1 us
  transfers between devices with their start and end apart: 10, of which 3 were waited for; matrix products, arithmetic and copies ran while one was open for 34% of the time, Pallas kernels for 0%

commit v1 on v0

v1 whole, which is shorter than its diff:
```python
import jax
import jax.numpy as jnp
from jax import lax
from jax.experimental import pallas as pl
from jax.experimental.pallas import tpu as pltpu
from jax.sharding import PartitionSpec as P

AXES = ("row", "col")
UNROLL = 24


def at_wrap(r, rows):
    half = rows // 2
    return r in (0, half - 1, half, rows - 1)


def permutations(rows, cols):
    def build(target):
        pairs = []
        for r in range(rows):
            for c in range(cols):
                tr, tc = target(r, c)
                pairs.append((r * cols + c, (tr % rows) * cols + tc % cols))
        return pairs

    def beside(r):
        return r + 1 if r % 2 else r - 1

    def along(c):
        return c + 2 if c % 2 == 0 else c - 2

    return {
        "pair": build(lambda r, c: (r, c ^ 1)),
        "skip": build(lambda r, c: (r, along(c))),
        "far": build(lambda r, c: (r, c - 1 if c % 2 == 0 else c + 1)),
        "core": build(lambda r, c: (r ^ 1, c)),
        "beside": build(lambda r, c: (beside(r), c)),
        "a": build(lambda r, c: (beside(r), c ^ 1) if at_wrap(r, rows) else (beside(r), c)),
        "b": build(lambda r, c: (r, c ^ 1) if at_wrap(r, rows) else (beside(r), c)),
        "c": build(lambda r, c: (r, along(c)) if at_wrap(r, rows) else (beside(r), c)),
    }


def pick(name, flag, a, b):
    def body(flag_ref, a_ref, b_ref, out_ref, sem):
        @pl.when(flag_ref[0] != 0)
        def _():
            copy = pltpu.make_async_copy(a_ref, out_ref, sem)
            copy.start()
            copy.wait()

        @pl.when(flag_ref[0] == 0)
        def _():
            copy = pltpu.make_async_copy(b_ref, out_ref, sem)
            copy.start()
            copy.wait()

    return pl.pallas_call(
        body,
        out_shape=jax.ShapeDtypeStruct(a.shape, a.dtype),
        in_specs=[pl.BlockSpec(memory_space=pltpu.SMEM)] + [pl.BlockSpec(memory_space=pl.ANY)] * 2,
        out_specs=pl.BlockSpec(memory_space=pltpu.VMEM),
        scratch_shapes=[pltpu.SemaphoreType.DMA],
        cost_estimate=pl.CostEstimate(flops=0, bytes_accessed=2 * a.size * 2, transcendentals=0),
        name=name,
    )(flag, a, b)


def add_entries(count_ref, list_ref, left_ref, pool, acc):
    def group(g, _):
        for q in range(UNROLL):
            code = list_ref[g * UNROLL + q]
            slot = code & 127
            block = (code >> 7) & 1023
            acc[slot] += jnp.dot(
                left_ref[code >> 17], pool[block], preferred_element_type=jnp.float32
            )
        return 0

    lax.fori_loop(0, (count_ref[0] + UNROLL - 1) // UNROLL, group, 0)


def load_pool(chunks, pool, sems):
    copies, start = [], 0
    for n, chunk in enumerate(chunks):
        size = chunk.shape[0]
        copies.append(pltpu.make_async_copy(chunk, pool.at[pl.ds(start, size)], sems.at[n]))
        start += size
    for copy in copies:
        copy.start()
    return copies


def accumulate(name, count, entries, left, chunks, acc):
    n = len(chunks)
    size = sum(chunk.shape[0] for chunk in chunks)
    order = left.shape[-1]
    slots = left.shape[0] + 8
    fresh = acc is None

    def body(*refs):
        count_ref, list_ref, left_ref = refs[:3]
        chunk_refs = refs[3 : 3 + n]
        out, total, pool, sems = refs[-4:]
        copies = load_pool(chunk_refs, pool, sems)
        if fresh:
            total[...] = jnp.zeros(total.shape, total.dtype)
        else:
            fetch = pltpu.make_async_copy(refs[3 + n], total, sems.at[n])
            fetch.start()
            copies.append(fetch)
        for copy in copies:
            copy.wait()
        add_entries(count_ref, list_ref, left_ref, pool, total)
        store = pltpu.make_async_copy(total, out, sems.at[n])
        store.start()
        store.wait()

    smem = pl.BlockSpec(memory_space=pltpu.SMEM)
    vmem = pl.BlockSpec(memory_space=pltpu.VMEM)
    anywhere = pl.BlockSpec(memory_space=pl.ANY)
    args = [count, entries, left, *chunks] + ([] if fresh else [acc])
    return pl.pallas_call(
        body,
        out_shape=jax.ShapeDtypeStruct((slots, order, order), jnp.float32),
        in_specs=[smem, smem, vmem] + [anywhere] * (n + (not fresh)),
        out_specs=anywhere,
        scratch_shapes=[
            pltpu.VMEM((slots, order, order), jnp.float32),
            pltpu.VMEM((size, order, order), jnp.bfloat16),
            pltpu.SemaphoreType.DMA((n + 1,)),
        ],
        input_output_aliases={} if fresh else {3 + n: 0},
        compiler_params=pltpu.CompilerParams(vmem_limit_bytes=36 << 20),
        cost_estimate=pl.CostEstimate(
            flops=size * 3 * order**3, bytes_accessed=size * order * order * 2 + 20 * 2**20, transcendentals=0
        ),
        name=name,
    )(*args)


def finish(name, count, entries, left, chunks, acc, inverse):
    n = len(chunks)
    size = sum(chunk.shape[0] for chunk in chunks)
    order = left.shape[-1]
    slots = inverse.shape[0]
    part = 16

    def body(*refs):
        count_ref, list_ref, inverse_ref, left_ref = refs[:4]
        chunk_refs = refs[4 : 4 + n]
        acc_ref, out, total, pool, stage, sems, out_sems = refs[4 + n :]
        copies = load_pool(chunk_refs, pool, sems)
        fetch = pltpu.make_async_copy(acc_ref, total, sems.at[n])
        fetch.start()
        for copy in copies:
            copy.wait()
        fetch.wait()
        add_entries(count_ref, list_ref, left_ref, pool, total)

        def piece(p):
            return pltpu.make_async_copy(
                stage.at[pl.ds(p * part, part)], out.at[pl.ds(p * part, part)], out_sems.at[p]
            )

        def fill(p, _):
            for q in range(part):
                s = p * part + q
                t = inverse_ref[s]
                value = total[jnp.maximum(t, 0)]
                stage[s] = jnp.where(t >= 0, value, 0.0).astype(jnp.bfloat16)
            piece(p).start()
            return 0

        lax.fori_loop(0, slots // part, fill, 0)

        def drain(p, _):
            piece(p).wait()
            return 0

        lax.fori_loop(0, slots // part, drain, 0)

    smem = pl.BlockSpec(memory_space=pltpu.SMEM)
    vmem = pl.BlockSpec(memory_space=pltpu.VMEM)
    anywhere = pl.BlockSpec(memory_space=pl.ANY)
    return pl.pallas_call(
        body,
        out_shape=jax.ShapeDtypeStruct((slots, order, order), jnp.bfloat16),
        in_specs=[smem] * 3 + [vmem] + [anywhere] * (n + 1),
        out_specs=anywhere,
        scratch_shapes=[
            pltpu.VMEM(acc.shape, jnp.float32),
            pltpu.VMEM((size, order, order), jnp.bfloat16),
            pltpu.VMEM((slots, order, order), jnp.bfloat16),
            pltpu.SemaphoreType.DMA((n + 1,)),
            pltpu.SemaphoreType.DMA((slots // part,)),
        ],
        compiler_params=pltpu.CompilerParams(vmem_limit_bytes=40 << 20),
        cost_estimate=pl.CostEstimate(
            flops=size * 3 * order**3, bytes_accessed=30 * 2**20, transcendentals=0
        ),
        name=name,
    )(count, entries, inverse, left, *chunks, acc)


def shards(blocks, pattern, owner):
    held, stored, order = blocks.shape[:3]
    rows, cols = lax.axis_size("row"), lax.axis_size("col")
    devices = rows * cols
    r, c = lax.axis_index("row"), lax.axis_index("col")
    here = r * cols + c
    perms = permutations(rows, cols)
    half = rows // 2
    wrap = (r == 0) | (r == half - 1) | (r == half) | (r == rows - 1)
    flag = wrap.astype(jnp.int32).reshape(1)
    items = held * stored

    token = [None]

    def send(x, which):
        if token[0] is not None:
            x, _ = lax.optimization_barrier((x, token[0]))
        return lax.ppermute(x, AXES, perms[which])

    def wait(x):
        if token[0] is None:
            token[0] = x
        else:
            token[0], _ = lax.optimization_barrier((x, token[0]))

    pattern_col = jnp.stack([pattern, lax.ppermute(pattern, AXES, perms["pair"]), lax.ppermute(pattern, AXES, perms["far"])])
    pattern_core = lax.ppermute(pattern_col, AXES, perms["core"])
    pattern_y = lax.ppermute(pattern_col, AXES, perms["beside"])
    pattern_a = jnp.where(wrap, pattern_y[1], pattern_y[0])
    pattern_b = jnp.where(wrap, pattern_y[0], pattern_y[1])
    patterns = jnp.stack([*pattern_col, *pattern_core, pattern_a, pattern_b, pattern_y[2]])
    pair = c ^ 1
    far = jnp.where(c % 2 == 0, c - 1 + cols, c + 1) % cols
    beside = jnp.where(r % 2 == 1, r + 1, r - 1 + rows) % rows
    holders = jnp.stack(
        [r * cols + c, r * cols + pair, r * cols + far]
        + [(r ^ 1) * cols + c, (r ^ 1) * cols + pair, (r ^ 1) * cols + far]
        + [
            beside * cols + jnp.where(wrap, pair, c),
            beside * cols + jnp.where(wrap, c, pair),
            beside * cols + far,
        ]
    )
    row_ids = holders[:, None] * held + jnp.arange(held, dtype=jnp.int32)[None, :]
    numbers = jnp.arange(stored, dtype=jnp.int32)
    same_row = row_ids[:, :, None, None] == pattern[None, None]
    left_of = jnp.sum(jnp.where(same_row, numbers, 0), axis=-1)
    has_row = jnp.any(same_row, axis=-1)
    same_col = patterns[:, :, :, None, None] == pattern[None, None, None]
    slot_of = jnp.sum(jnp.where(same_col, numbers, 0), axis=-1)
    has_col = jnp.any(same_col, axis=-1)
    row_base = jnp.arange(held, dtype=jnp.int32) * stored
    valid = has_row[:, :, None, :] & has_col
    codes = ((left_of + row_base)[:, :, None, :] << 17) | (slot_of + row_base)
    valid = valid.reshape(9, held, stored * held)
    codes = codes.reshape(9, held, stored * held)
    block_number = jnp.repeat(numbers, held)

    slot_index = {"O": 0, "X": 1, "Z": 2, "DO": 3, "DX": 4, "DZ": 5, "A": 6, "B": 7, "C": 8}

    def tables(keys):
        ok = jnp.stack([valid[slot_index[s], k] for s, k in keys]).reshape(-1)
        code = jnp.stack(
            [codes[slot_index[s], k] | ((block_number + n * stored) << 7) for n, (s, k) in enumerate(keys)]
        ).reshape(-1)
        total = ok.shape[0]
        length = -(-total // UNROLL) * UNROLL
        place = jnp.where(ok, jnp.cumsum(ok.astype(jnp.int32)) - 1, -1)
        hit = place[None, :] == jnp.arange(length, dtype=jnp.int32)[:, None]
        count = jnp.sum(ok.astype(jnp.int32)).reshape(1)
        listed = jnp.sum(jnp.where(hit, code[None, :], 0), axis=1)
        listed = jnp.where(jnp.arange(length) < count, listed, items)
        return count, listed

    owners = owner.reshape(items)
    number = jnp.arange(items, dtype=jnp.int32)
    earlier = (owners[:, None] == owners[None, :]) & (number[None, :] < number[:, None])
    rank = jnp.sum(earlier.astype(jnp.int32), axis=1)
    capacity = max(2, items // devices + 1)
    target = owners * capacity + rank
    landed = target[None, :] == jnp.arange(devices * capacity, dtype=jnp.int32)[:, None]
    inverse = jnp.sum(jnp.where(landed, number[None, :] + 1, 0), axis=1) - 1
    outgoing_ids = jnp.where(inverse >= 0, here * items + inverse, -1)
    arrived_ids = lax.all_to_all(
        outgoing_ids.reshape(devices, capacity), AXES, split_axis=0, concat_axis=0, tiled=True
    )

    left = blocks.reshape(items, order, order)
    got = {name: [None] * held for name in ("X", "Z", "DX", "DZ", "A", "B", "C")}
    for k in range(2):
        got["X"][k] = send(blocks[k], "pair")
        got["A"][k] = send(blocks[k], "a")
    got["DO"] = send(left, "core")

    def run(name, keys, acc):
        chunks, used, skip = [], [], 0
        for s, k in keys:
            if s in ("O", "DO"):
                if k == 0:
                    chunks.append(left if s == "O" else got["DO"])
            else:
                chunks.append(got[s][k])
        count, listed = tables(keys)
        return accumulate(name, count, listed, left, chunks, acc)

    every = range(held)
    acc = run("own", [("O", k) for k in every], None)
    for k in every:
        wait(got["A"][k])
        wait(got["X"][k])
        if k + 2 < held:
            got["X"][k + 2] = send(blocks[k + 2], "pair")
            got["A"][k + 2] = send(blocks[k + 2], "a")
        got["Z"][k] = send(got["X"][k], "skip")
        got["B"][k] = send(pick("pick_b", flag, got["A"][k], got["X"][k]), "b")
        got["DX"][k] = send(got["X"][k], "core")
        if k == 0:
            acc = run("core", [("DO", j) for j in every], acc)
        else:
            wait(got["Z"][k - 1])
            got["C"][k - 1] = send(pick("pick_c", flag, got["A"][k - 1], got["Z"][k - 1]), "c")
            got["DZ"][k - 1] = send(got["Z"][k - 1], "core")
        if k == 2:
            acc = run("first", [("X", 0), ("X", 1), ("A", 0), ("A", 1), ("DX", 0), ("DX", 1), ("Z", 0), ("B", 0)], acc)
        if k == 4:
            acc = run(
                "second",
                [("X", 2), ("X", 3), ("A", 2), ("A", 3), ("DX", 2), ("DX", 3), ("Z", 1), ("Z", 2)]
                + [("DZ", 0), ("DZ", 1), ("B", 1), ("B", 2), ("C", 0)],
                acc,
            )
    last = held - 1
    wait(got["Z"][last])
    got["C"][last] = send(pick("pick_c", flag, got["A"][last], got["Z"][last]), "c")
    got["DZ"][last] = send(got["Z"][last], "core")
    acc = run(
        "third",
        [("X", 4), ("A", 4), ("DX", 4), ("Z", 3), ("Z", 4), ("DZ", 2), ("DZ", 3), ("B", 3), ("C", 1), ("C", 2)],
        acc,
    )
    keys = [("B", 4), ("C", 3), ("C", 4), ("DZ", 4)]
    count, listed = tables(keys)
    outgoing = finish("finish", count, listed, left, [got[s][k] for s, k in keys], acc, inverse)
    arrived = lax.all_to_all(outgoing, AXES, split_axis=0, concat_axis=0, tiled=True)
    return arrived, arrived_ids.reshape(devices * capacity)


def solution(mesh):
    in_specs = (P(AXES, None, None, None), P(AXES, None), P(AXES, None))
    out_specs = (P(AXES, None, None), P(AXES))
    return jax.shard_map(shards, mesh=mesh, in_specs=in_specs, out_specs=out_specs, check_vma=False)
```

time: 1080 us -> 399 us (0.37)
  waiting for transfers between devices: 643 us -> 192 us
  local copies, waits for them, and re-layouts: 286 us -> 39.6 us
  Pallas kernels: 0 us -> 75.6 us
  matrix products: 50.1 us -> 0 us
  other arithmetic: 46.7 us -> 30.3 us
  starting transfers between devices: 39.1 us -> 52.1 us
    ppermute x8 -> x40, waiting for transfers between devices: 543 us -> 91.9 us  [the longest x36 81.7 us: send(): return lax.ppermute(x, AXES, perms[which])]
    gather x15 -> x0, local copies, waits for them, and re-layouts: 238 us -> none  [the longest x10 235 us: one_row(): picked = pool_blocks[pool_rows[:, None] * stored + where_slot]]
    pallas_call x0 -> x16, Pallas kernels: none -> 75.6 us  [the longest x5 45.7 us: accumulate(): pl.pallas_call(body, out_shape=jax.ShapeDtypeStruct((slots, order, order)...]
    dot_general x5 -> x0, matrix products: 50.1 us -> none  [one_row(): jnp.einsum('axy,auyz->uxz', blocks[row_local], picked, preferred_element_...]
    concatenate x4 -> x0, other arithmetic: 33.1 us -> none  [with_halo(): shard = jnp.concatenate([before, shard, after], axis=dim)]
    scatter x2 -> x0, local copies, waits for them, and re-layouts: 20 us -> none  [the longest x1 19.1 us: shards(): outgoing.at[target]]
    ppermute x8 -> x40, starting transfers between devices: 20.1 us -> 36.5 us  [the longest x36 29.7 us: send(): return lax.ppermute(x, AXES, perms[which])]
    reduce_sum x1 -> x16, other arithmetic: 0.17 us -> 12.4 us  [the longest x6 4.16 us: tables(): count = jnp.sum(ok.astype(jnp.int32)).reshape(1)]
  transfers between devices with their start and end apart: 10 -> 42, of which waited for: 3 -> 15; matrix products, arithmetic and copies ran while one was open for 34% -> 13% of each run, Pallas kernels for 0% -> 19%
where the time goes in v1:
time: 399 us; the launch traced here: 392 us
  waiting for transfers between devices  192 us (48%)
  Pallas kernels  75.6 us (19%)
  starting transfers between devices  52.1 us (13%)
  local copies, waits for them, and re-layouts  39.6 us (10%)
  other arithmetic  30.3 us (8%)
    all_to_all x1, waiting for transfers between devices, shards(): lax.all_to_all(outgoing, AXES, split_axis=0, concat_axis=0, tiled=True)  99.9 us
    ppermute x36, waiting for transfers between devices, send(): return lax.ppermute(x, AXES, perms[which])  81.7 us
    pallas_call x5, Pallas kernels, accumulate(): pl.pallas_call(body, out_shape=jax.ShapeDtypeStruct((slots, order, order)...  45.7 us
    ppermute x36, starting transfers between devices, send(): return lax.ppermute(x, AXES, perms[which])  29.7 us
    pallas_call x10, Pallas kernels, pick(): pl.pallas_call(body, out_shape=jax.ShapeDtypeStruct(a.shape, a.dtype), in...  20.5 us
    unnamed x95, local copies, waits for them, and re-layouts  19.1 us
    pallas_call x1, Pallas kernels, finish(): pl.pallas_call(body, out_shape=jax.ShapeDtypeStruct((slots, order, order)...  9.47 us
    ppermute x1, waiting for transfers between devices, shards(): pattern_y = lax.ppermute(pattern_col, AXES, perms['beside'])  8.97 us
  transfers between devices with their start and end apart: 42, of which 15 were waited for; matrix products, arithmetic and copies ran while one was open for 13% of the time, Pallas kernels for 19%

profile of v1, /device:TPU:0, one launch (start us, length us, event | category | flops | bytes accessed | tf_op | source)
XLA Modules:
  0.0 391.6 jit_solution(10016062401768059399)
XLA Ops:
  0.6 1.7 collective-permute-start
  2.3 4.0 %collective-permute-start.1 = (s32[5,24]{1,0:T(8,128)}, s32[5,24]{1,0:T(8,128)S(1)}, u32[]{:S(2)}, u32[]{:S(2)}) collective-permute-start(s32[5,24]{1,0:T(8,128)} %param.4), channel_id=1, source_target_pairs={{0,7},{1,2},{2,1},{3,4},{4,3},{5,6},{6,5},{7,0},{8,15},{9,10},{10,... | collective-permute-start | bytes 1448 | tf_op jit(solution)/shard_map/ppermute | solution.py:231
  6.3 4.1 %slice_bitcast_fusion = (bf16[24,128,128]{2,1,0:T(8,128)(2,1)}, bf16[24,128,128]{2,1,0:T(8,128)(2,1)}, bf16[24,128,128]{2,1,0:T(8,128)(2,1)}, bf16[24,128,128]{2,1,0:T(8,128)(2,1)}, bf16[24,128,128]{2,1,0:T(8,128)(2,1)}) fusion(bf16[5,24,128,128]{3,2,1,0:T(8,128)(2,1)} %param.3), kind=kLoop, calls=%fused_computation.15 | loop fusion | bytes 7864320 | tf_op jit(solution)/shard_map/squeeze | solution.py:296
  10.4 4.6 %collective-permute-start.5 = (bf16[24,128,128]{2,1,0:T(8,128)(2,1)}, bf16[24,128,128]{2,1,0:T(8,128)(2,1)S(1)}, u32[]{:S(2)}, u32[]{:S(2)}) collective-permute-start(bf16[24,128,128]{2,1,0:T(8,128)(2,1)} %get-tuple-element.63), channel_id=1, source_target_pairs={{0,121},{1,120},{2,123},{3,122},{4,125},{5,124},{6,127},{7,126},{8... | collective-permute-start | bytes 2359304 | tf_op jit(solution)/shard_map/ppermute | solution.py:223
  16.1 6.9 %all-to-all-start.1 = ((s32[128,1,2]{2,1,0:T(1,128)}), s32[128,1,2]{2,1,0:T(1,128)}, u32[]{:S(2)}, u32[]{:S(2)}) async-start(s32[128,1,2]{2,1,0:T(1,128)} %bitcast.128), calls=%async_computation.1 | async-start | bytes 131072 | tf_op jit(solution)/shard_map/all_to_all | solution.py:289
  34.1 4.1 %collective-permute-start.23 = (bf16[24,128,128]{2,1,0:T(8,128)(2,1)}, bf16[24,128,128]{2,1,0:T(8,128)(2,1)S(1)}, u32[]{:S(2)}, u32[]{:S(2)}) collective-permute-start(bf16[24,128,128]{2,1,0:T(8,128)(2,1)} %get-tuple-element.62), channel_id=1, source_target_pairs={{0,121},{1,120},{2,123},{3,122},{4,125},{5,124},{6,127},{7,126},{8... | collective-permute-start | bytes 2359304 | tf_op jit(solution)/shard_map/ppermute | solution.py:223
  40.5 9.0 %collective-permute-done.3 = s32[3,5,24]{2,1,0:T(8,128)S(1)} collective-permute-done((s32[3,5,24]{2,1,0:T(8,128)S(1)}, s32[3,5,24]{2,1,0:T(8,128)S(1)}, u32[]{:S(2)}, u32[]{:S(2)}) %collective-permute-start.3) | collective-permute-done | bytes 1472 | tf_op jit(solution)/shard_map/ppermute | solution.py:233
  49.5 4.0 %fusion = s32[9,5,24,5]{2,3,1,0:T(8,128)S(1)} fusion(s32[5,24]{1,0:T(8,128)S(1)} %copy-done.27, s32[9,5,24]{2,1,0:T(8,128)S(1)} %constant_dynamic-update-slice_fusion), kind=kLoop, calls=%fused_computation.8 | loop fusion | flops 383400 | bytes 26400 | tf_op jit(solution)/shard_map/reduce_sum | solution.py:255
  53.5 4.1 %compare_reduce_fusion = pred[9,5,24,5]{2,3,1,0:T(8,128)(4,1)S(1)} fusion(s32[5,24]{1,0:T(8,128)S(1)} %copy-done.27, s32[9,5,24]{2,1,0:T(8,128)S(1)} %constant_dynamic-update-slice_fusion), kind=kLoop, calls=%fused_computation.7 | loop fusion | flops 253800 | bytes 10200 | tf_op jit(solution)/shard_map/reduce_or | solution.py:256
  59.7 1.3 reduce_sum.149
  62.9 1.3 fusion.11
  64.2 1.3 fusion.15
  70.4 2.0 pick_b.9
  74.2 2.2 collective-permute-start.6
  76.5 2.9 collective-permute-start.26
  79.4 12.3 %collective-permute-done.38.refs_10_ = bf16[24,128,128]{2,1,0:T(8,128)(2,1)} collective-permute-done((bf16[24,128,128]{2,1,0:T(8,128)(2,1)}, bf16[24,128,128]{2,1,0:T(8,128)(2,1)}, u32[]{:S(2)}, u32[]{:S(2)}) %collective-permute-start.38) | collective-permute-done | bytes 786464 | tf_op jit(solution)/shard_map/ppermute | solution.py:223
  92.9 2.0 pick_b.7
  95.5 4.0 %collective-permute-start.12 = (bf16[24,128,128]{2,1,0:T(8,128)(2,1)}, bf16[24,128,128]{2,1,0:T(8,128)(2,1)}, u32[]{:S(2)}, u32[]{:S(2)}) collective-permute-start(bf16[24,128,128]{2,1,0:T(8,128)(2,1)} %get-tuple-element.35), channel_id=1, source_target_pairs={{0,1},{1,0},{2,3},{3,2},{4,5},{5,4},{6,7},{7,6},{8,9},{9,8},{10,11... | collective-permute-start | bytes 2359304 | tf_op jit(solution)/shard_map/ppermute | solution.py:223
  99.4 3.0 collective-permute-done.6.b_ref.refs_3_
  103.9 2.1 pick_c.9
  105.9 7.3 %collective-permute-done.24.b_ref.refs_9_ = bf16[24,128,128]{2,1,0:T(8,128)(2,1)} collective-permute-done((bf16[24,128,128]{2,1,0:T(8,128)(2,1)S(1)}, bf16[24,128,128]{2,1,0:T(8,128)(2,1)}, u32[]{:S(2)}, u32[]{:S(2)}) %collective-permute-start.24) | collective-permute-done | bytes 786464 | tf_op jit(solution)/shard_map/ppermute | solution.py:223
  114.0 2.1 pick_b.8
  116.0 11.0 %collective-permute-done.33.refs_13_ = bf16[24,128,128]{2,1,0:T(8,128)(2,1)} collective-permute-done((bf16[24,128,128]{2,1,0:T(8,128)(2,1)}, bf16[24,128,128]{2,1,0:T(8,128)(2,1)}, u32[]{:S(2)}, u32[]{:S(2)}) %collective-permute-start.33) | collective-permute-done | bytes 786464 | tf_op jit(solution)/shard_map/ppermute | solution.py:223
  131.3 7.9 %collective-permute-done.34.refs_14_ = bf16[24,128,128]{2,1,0:T(8,128)(2,1)S(1)} collective-permute-done((bf16[24,128,128]{2,1,0:T(8,128)(2,1)}, bf16[24,128,128]{2,1,0:T(8,128)(2,1)S(1)}, u32[]{:S(2)}, u32[]{:S(2)}) %collective-permute-start.34) | collective-permute-done | bytes 786464 | tf_op jit(solution)/shard_map/ppermute | solution.py:223
  143.5 8.2 %collective-permute-done.19.b_ref.refs_10_ = bf16[24,128,128]{2,1,0:T(8,128)(2,1)} collective-permute-done((bf16[24,128,128]{2,1,0:T(8,128)(2,1)}, bf16[24,128,128]{2,1,0:T(8,128)(2,1)}, u32[]{:S(2)}, u32[]{:S(2)}) %collective-permute-start.19) | collective-permute-done | bytes 786464 | tf_op jit(solution)/shard_map/ppermute | solution.py:223
  152.5 2.1 pick_c.7
  154.6 2.0 pick_b.6
  156.7 3.1 collective-permute-start.7
  162.1 9.6 %collective-permute-done.13.b_ref.refs_6_ = bf16[24,128,128]{2,1,0:T(8,128)(2,1)S(1)} collective-permute-done((bf16[24,128,128]{2,1,0:T(8,128)(2,1)}, bf16[24,128,128]{2,1,0:T(8,128)(2,1)S(1)}, u32[]{:S(2)}, u32[]{:S(2)}) %collective-permute-start.13) | collective-permute-done | bytes 786464 | tf_op jit(solution)/shard_map/ppermute | solution.py:223
  172.5 2.1 pick_c.8
  174.6 12.0 %collective-permute-done.25.refs_11_ = bf16[24,128,128]{2,1,0:T(8,128)(2,1)} collective-permute-done((bf16[24,128,128]{2,1,0:T(8,128)(2,1)}, bf16[24,128,128]{2,1,0:T(8,128)(2,1)}, u32[]{:S(2)}, u32[]{:S(2)}) %collective-permute-start.25) | collective-permute-done | bytes 786464 | tf_op jit(solution)/shard_map/ppermute | solution.py:223
  188.4 8.7 %collective-permute-done.15.b_ref.refs_7_ = bf16[24,128,128]{2,1,0:T(8,128)(2,1)} collective-permute-done((bf16[24,128,128]{2,1,0:T(8,128)(2,1)S(1)}, bf16[24,128,128]{2,1,0:T(8,128)(2,1)}, u32[]{:S(2)}, u32[]{:S(2)}) %collective-permute-start.15) | collective-permute-done | bytes 786464 | tf_op jit(solution)/shard_map/ppermute | solution.py:223
  198.4 2.1 pick_c.5
  200.5 2.0 pick_b.5
  202.5 2.0 pick_c.6
  205.6 1.7 collective-permute-start.9
  207.6 2.1 copy-done.1
  209.7 6.2 %own.1.refs_4_ = f32[128,128,128]{2,1,0:T(8,128)S(1)} custom-call(s32[1]{0:T(128)} %bitcast.120.refs_0_, s32[600]{0:T(1024)S(1)} %fusion.9.refs_1_, bf16[120,128,128]{2,1,0:T(8,128)(2,1)S(1)} %bitcast.337, bf16[120,128,128]{2,1,0:T(8,128)(2,1)S(1)} %bitcast.338), custom_call_target="tpu_custom_call" | custom-call | flops 754974720 | bytes 24903680 | tf_op jit(solution)/shard_map/own/pallas_call | solution.py:123
  216.6 5.7 %core.1.refs_11_ = f32[128,128,128]{2,1,0:T(8,128)S(1)} custom-call(s32[1]{0:T(128)} %bitcast.107.refs_0_, s32[600]{0:T(1024)S(1)} %fusion.8.refs_1_, bf16[120,128,128]{2,1,0:T(8,128)(2,1)S(1)} %bitcast.339, bf16[120,128,128]{2,1,0:T(8,128)(2,1)} %collective-permute-done.39.refs_3_, f32[128,128,128]{2,1,0:T(8,128)S(1)} %own.1.refs_4_), custom_call_target="tpu_custom_call", output_to_operand_aliasing={{}: (4, {})} | custom-call | flops 754974720 | bytes 24903680 | tf_op jit(solution)/shard_map/core/pallas_call | solution.py:123
  222.4 6.9 %first.1.refs_16_ = f32[128,128,128]{2,1,0:T(8,128)S(1)} custom-call(s32[1]{0:T(128)} %bitcast.91.refs_0_, s32[960]{0:T(1024)S(1)} %fusion.7.refs_1_, bf16[120,128,128]{2,1,0:T(8,128)(2,1)S(1)} %bitcast.340, bf16[24,128,128]{2,1,0:T(8,128)(2,1)S(1)} %copy-done.14, bf16[24,128,128]{2,1,0:T(8,128)(2,1)S(1)} %copy-done.16, ...), custom_call_target="tpu_custom_call", output_to_operand_aliasing={{}: (11, {})} | custom-call | flops 1207959552 | bytes 27262976 | tf_op jit(solution)/shard_map/first/pallas_call | solution.py:123
  229.3 3.4 copy-done
  232.7 13.9 %second.1.refs_13_ = f32[128,128,128]{2,1,0:T(8,128)} custom-call(s32[1]{0:T(128)} %bitcast.67.refs_0_, s32[1560]{0:T(1024)S(1)} %fusion.6.refs_1_, bf16[120,128,128]{2,1,0:T(8,128)(2,1)S(1)} %bitcast.341, bf16[24,128,128]{2,1,0:T(8,128)(2,1)} %collective-permute-done.6.b_ref.refs_3_, ...), custom_call_target="tpu_custom_call", output_to_operand_aliasing={{}: (16, {})} | custom-call | flops 1962934272 | bytes 31195136 | tf_op jit(solution)/shard_map/second/pallas_call | solution.py:123
  246.7 12.9 %third.1.refs_8_ = f32[128,128,128]{2,1,0:T(8,128)} custom-call(s32[1]{0:T(128)} %bitcast.41.refs_0_, s32[1200]{0:T(1024)S(1)} %fusion.5.refs_1_, bf16[120,128,128]{2,1,0:T(8,128)(2,1)S(1)} %bitcast.342, bf16[24,128,128]{2,1,0:T(8,128)(2,1)S(1)} %copy-done.20, bf16[24,128,128]{2,1,0:T(8,128)(2,1)S(1)} %copy-done.8, ...), custom_call_target="tpu_custom_call", output_to_operand_aliasing={{}: (13, {})} | custom-call | flops 1509949440 | bytes 28835840 | tf_op jit(solution)/shard_map/third/pallas_call | solution.py:123
  259.7 9.5 %finish.1 = bf16[256,128,128]{2,1,0:T(8,128)(2,1)} custom-call(s32[1]{0:T(128)} %bitcast.16.refs_0_, s32[480]{0:T(512)S(1)} %fusion.10.refs_1_, s32[256]{0:T(256)S(1)} %get-tuple-element.181.refs_2_, bf16[120,128,128]{2,1,0:T(8,128)(2,1)S(1)} %bitcast.343, bf16[24,128,128]{2,1,0:T(8,128)(2,1)S(1)} %collective-permute-done.9.refs_4_, ...), custom_call_target="tpu_custom_call" | custom-call | flops 603979776 | bytes 31457280 | tf_op jit(solution)/shard_map/finish/pallas_call | solution.py:186
  269.1 8.7 %all-to-all-start = ((bf16[256,128,128]{2,1,0:T(8,128)(2,1)}), bf16[256,128,128]{2,1,0:T(8,128)(2,1)}, u32[]{:S(2)}, u32[]{:S(2)}) async-start(bf16[256,128,128]{2,1,0:T(8,128)(2,1)} %finish.1), calls=%async_computation | async-start | bytes 16777216 | tf_op jit(solution)/shard_map/all_to_all | solution.py:349
  278.4 1.6 reduce.21
  280.8 99.9 %all-to-all-done = bf16[256,128,128]{2,1,0:T(8,128)(2,1)} async-done(((bf16[256,128,128]{2,1,0:T(8,128)(2,1)}), bf16[256,128,128]{2,1,0:T(8,128)(2,1)}, u32[]{:S(2)}, u32[]{:S(2)}) %all-to-all-start) | async-done | bytes 8388640 | tf_op jit(solution)/shard_map/all_to_all | solution.py:349
  380.6 10.5 %copy.24 = bf16[256,128,128]{2,1,0:T(8,128)(2,1)} copy(bf16[256,128,128]{2,1,0:T(8,128)(2,1)} %all-to-all-done) | data formatting | bytes 16777216
  (295 shorter events, 47.0 us)
Async XLA Ops:
  0.6 33.4 %collective-permute-start = (s32[5,24]{1,0:T(8,128)}, s32[5,24]{1,0:T(8,128)S(1)}, u32[]{:S(2)}, u32[]{:S(2)}) collective-permute-start(s32[5,24]{1,0:T(8,128)} %param.4), channel_id=1, source_target_pairs={{0,1},{1,0},{2,3},{3,2},{4,5},{5,4},{6,7},{7,6},{8,9},{9,8},{10,11... | collective-permute-start | bytes 1448 | tf_op jit(solution)/shard_map/ppermute | solution.py:231
  2.3 35.9 %collective-permute-start.1 = (s32[5,24]{1,0:T(8,128)}, s32[5,24]{1,0:T(8,128)S(1)}, u32[]{:S(2)}, u32[]{:S(2)}) collective-permute-start(s32[5,24]{1,0:T(8,128)} %param.4), channel_id=1, source_target_pairs={{0,7},{1,2},{2,1},{3,4},{4,3},{5,6},{6,5},{7,0},{8,15},{9,10},{10,... | collective-permute-start | bytes 1448 | tf_op jit(solution)/shard_map/ppermute | solution.py:231
  10.4 58.9 %collective-permute-start.4 = (bf16[24,128,128]{2,1,0:T(8,128)(2,1)}, bf16[24,128,128]{2,1,0:T(8,128)(2,1)S(1)}, u32[]{:S(2)}, u32[]{:S(2)}) collective-permute-start(bf16[24,128,128]{2,1,0:T(8,128)(2,1)} %get-tuple-element.63), channel_id=1, source_target_pairs={{0,1},{1,0},{2,3},{3,2},{4,5},{5,4},{6,7},{7,6},{8,9},{9,8},{10,11... | collective-permute-start | bytes 2359304 | tf_op jit(solution)/shard_map/ppermute | solution.py:223
  10.4 58.9 %collective-permute-start.5 = (bf16[24,128,128]{2,1,0:T(8,128)(2,1)}, bf16[24,128,128]{2,1,0:T(8,128)(2,1)S(1)}, u32[]{:S(2)}, u32[]{:S(2)}) collective-permute-start(bf16[24,128,128]{2,1,0:T(8,128)(2,1)} %get-tuple-element.63), channel_id=1, source_target_pairs={{0,121},{1,120},{2,123},{3,122},{4,125},{5,124},{6,127},{7,126},{8... | collective-permute-start | bytes 2359304 | tf_op jit(solution)/shard_map/ppermute | solution.py:223
  15.0 59.2 %collective-permute-start.10 = (bf16[24,128,128]{2,1,0:T(8,128)(2,1)}, bf16[24,128,128]{2,1,0:T(8,128)(2,1)S(1)}, u32[]{:S(2)}, u32[]{:S(2)}) collective-permute-start(bf16[24,128,128]{2,1,0:T(8,128)(2,1)} %get-tuple-element.62), channel_id=1, source_target_pairs={{0,1},{1,0},{2,3},{3,2},{4,5},{5,4},{6,7},{7,6},{8,9},{9,8},{10,11... | collective-permute-start | bytes 2359304 | tf_op jit(solution)/shard_map/ppermute | solution.py:223
  16.1 253.0 %all-to-all-start.1 = ((s32[128,1,2]{2,1,0:T(1,128)}), s32[128,1,2]{2,1,0:T(1,128)}, u32[]{:S(2)}, u32[]{:S(2)}) async-start(s32[128,1,2]{2,1,0:T(1,128)} %bitcast.128), calls=%async_computation.1 | async-start | bytes 131072 | tf_op jit(solution)/shard_map/all_to_all | solution.py:289
  34.1 42.4 %collective-permute-start.23 = (bf16[24,128,128]{2,1,0:T(8,128)(2,1)}, bf16[24,128,128]{2,1,0:T(8,128)(2,1)S(1)}, u32[]{:S(2)}, u32[]{:S(2)}) collective-permute-start(bf16[24,128,128]{2,1,0:T(8,128)(2,1)} %get-tuple-element.62), channel_id=1, source_target_pairs={{0,121},{1,120},{2,123},{3,122},{4,125},{5,124},{6,127},{7,126},{8... | collective-permute-start | bytes 2359304 | tf_op jit(solution)/shard_map/ppermute | solution.py:223
  38.3 1.3 collective-permute-start.2
  39.5 10.0 %collective-permute-start.3 = (s32[3,5,24]{2,1,0:T(8,128)S(1)}, s32[3,5,24]{2,1,0:T(8,128)S(1)}, u32[]{:S(2)}, u32[]{:S(2)}) collective-permute-start(s32[3,5,24]{2,1,0:T(8,128)S(1)} %pad_add_fusion), channel_id=1, source_target_pairs={{0,120},{1,121},{2,122},{3,123},{4,124},{5,125},{6,126},{7,127},{8... | collective-permute-start | bytes 4328 | tf_op jit(solution)/shard_map/ppermute | solution.py:233
  65.6 37.7 %copy-start.33 = (s32[1,120]{1,0:T(1,128)S(1)}, s32[1,120]{1,0:T(1,128)}, u32[]{:S(2)}) copy-start(s32[1,120]{1,0:T(1,128)} %get-tuple-element.121) | copy-start | bytes 1444
  72.5 56.2 %copy-start.28 = (s32[1,120]{1,0:T(1,128)S(1)}, s32[1,120]{1,0:T(1,128)}, u32[]{:S(2)}) copy-start(s32[1,120]{1,0:T(1,128)} %get-tuple-element.115) | copy-start | bytes 1444
  72.5 56.2 %copy-start.29 = (s32[1,120]{1,0:T(1,128)S(1)}, s32[1,120]{1,0:T(1,128)}, u32[]{:S(2)}) copy-start(s32[1,120]{1,0:T(1,128)} %get-tuple-element.94) | copy-start | bytes 1444
  72.5 56.1 %copy-start.30 = (s32[1,120]{1,0:T(1,128)S(1)}, s32[1,120]{1,0:T(1,128)}, u32[]{:S(2)}) copy-start(s32[1,120]{1,0:T(1,128)} %get-tuple-element.128) | copy-start | bytes 1444
  72.5 56.1 %copy-start.31 = (s32[1,120]{1,0:T(1,128)S(1)}, s32[1,120]{1,0:T(1,128)}, u32[]{:S(2)}) copy-start(s32[1,120]{1,0:T(1,128)} %get-tuple-element.133) | copy-start | bytes 1444
  72.5 19.2 %collective-permute-start.38 = (bf16[24,128,128]{2,1,0:T(8,128)(2,1)}, bf16[24,128,128]{2,1,0:T(8,128)(2,1)}, u32[]{:S(2)}, u32[]{:S(2)}) collective-permute-start(bf16[24,128,128]{2,1,0:T(8,128)(2,1)} %pick_b.9), channel_id=1, source_target_pairs={{0,1},{1,0},{2,3},{3,2},{4,5},{5,4},{6,7},{7,6},{8,16},{9,17},{10,... | collective-permute-start | bytes 2359304 | tf_op jit(solution)/shard_map/ppermute | solution.py:223
  73.7 18.4 %collective-permute-start.30 = (bf16[24,128,128]{2,1,0:T(8,128)(2,1)}, bf16[24,128,128]{2,1,0:T(8,128)(2,1)S(1)}, u32[]{:S(2)}, u32[]{:S(2)}) collective-permute-start(bf16[24,128,128]{2,1,0:T(8,128)(2,1)} %copy-done.13), channel_id=1, source_target_pairs={{0,2},{1,7},{2,4},{3,1},{4,6},{5,3},{6,0},{7,5},{8,10},{9,15},{10,... | collective-permute-start | bytes 2359304 | tf_op jit(solution)/shard_map/ppermute | solution.py:223
  74.1 20.8 %collective-permute-start.36 = (bf16[24,128,128]{2,1,0:T(8,128)(2,1)}, bf16[24,128,128]{2,1,0:T(8,128)(2,1)}, u32[]{:S(2)}, u32[]{:S(2)}) collective-permute-start(bf16[24,128,128]{2,1,0:T(8,128)(2,1)} %copy-done.13), channel_id=1, source_target_pairs={{0,8},{1,9},{2,10},{3,11},{4,12},{5,13},{6,14},{7,15},{8,0},{9,1},... | collective-permute-start | bytes 2359304 | tf_op jit(solution)/shard_map/ppermute | solution.py:223
  74.2 28.2 %collective-permute-start.6 = (bf16[24,128,128]{2,1,0:T(8,128)(2,1)}, bf16[24,128,128]{2,1,0:T(8,128)(2,1)}, u32[]{:S(2)}, u32[]{:S(2)}) collective-permute-start(bf16[24,128,128]{2,1,0:T(8,128)(2,1)} %get-tuple-element.32), channel_id=1, source_target_pairs={{0,1},{1,0},{2,3},{3,2},{4,5},{5,4},{6,7},{7,6},{8,9},{9,8},{10,11... | collective-permute-start | bytes 2359304 | tf_op jit(solution)/shard_map/ppermute | solution.py:223
  76.5 26.6 %collective-permute-start.26 = (bf16[24,128,128]{2,1,0:T(8,128)(2,1)}, bf16[24,128,128]{2,1,0:T(8,128)(2,1)S(1)}, u32[]{:S(2)}, u32[]{:S(2)}) collective-permute-start(bf16[24,128,128]{2,1,0:T(8,128)(2,1)} %get-tuple-element.32), channel_id=1, source_target_pairs={{0,121},{1,120},{2,123},{3,122},{4,125},{5,124},{6,127},{7,126},{8... | collective-permute-start | bytes 2359304 | tf_op jit(solution)/shard_map/ppermute | solution.py:223
  91.7 3.7 collective-permute-start.37
  92.1 21.2 %collective-permute-start.24 = (bf16[24,128,128]{2,1,0:T(8,128)(2,1)S(1)}, bf16[24,128,128]{2,1,0:T(8,128)(2,1)}, u32[]{:S(2)}, u32[]{:S(2)}) collective-permute-start(bf16[24,128,128]{2,1,0:T(8,128)(2,1)S(1)} %collective-permute-done.10.b_ref.refs_4_), channel_id=1, source_target_pairs={{0,2},{1,7},{2,4},{3,1},{4,6},{5,3},{6,0},{7,5},{8,10},{9,15},{10,... | collective-permute-start | bytes 2359304 | tf_op jit(solution)/shard_map/ppermute | solution.py:223
  94.9 112.6 %collective-permute-start.39 = (bf16[120,128,128]{2,1,0:T(8,128)(2,1)}, bf16[120,128,128]{2,1,0:T(8,128)(2,1)}, u32[]{:S(2)}, u32[]{:S(2)}) collective-permute-start(bf16[120,128,128]{2,1,0:T(8,128)(2,1)} %bitcast.336), channel_id=1, source_target_pairs={{0,8},{1,9},{2,10},{3,11},{4,12},{5,13},{6,14},{7,15},{8,0},{9,1},... | collective-permute-start | bytes 11796488 | tf_op jit(solution)/shard_map/ppermute | solution.py:223
  95.5 32.6 %collective-permute-start.12 = (bf16[24,128,128]{2,1,0:T(8,128)(2,1)}, bf16[24,128,128]{2,1,0:T(8,128)(2,1)}, u32[]{:S(2)}, u32[]{:S(2)}) collective-permute-start(bf16[24,128,128]{2,1,0:T(8,128)(2,1)} %get-tuple-element.35), channel_id=1, source_target_pairs={{0,1},{1,0},{2,3},{3,2},{4,5},{5,4},{6,7},{7,6},{8,9},{9,8},{10,11... | collective-permute-start | bytes 2359304 | tf_op jit(solution)/shard_map/ppermute | solution.py:223
  102.4 25.6 %collective-permute-start.11 = (bf16[24,128,128]{2,1,0:T(8,128)(2,1)}, bf16[24,128,128]{2,1,0:T(8,128)(2,1)S(1)}, u32[]{:S(2)}, u32[]{:S(2)}) collective-permute-start(bf16[24,128,128]{2,1,0:T(8,128)(2,1)} %get-tuple-element.35), channel_id=1, source_target_pairs={{0,121},{1,120},{2,123},{3,122},{4,125},{5,124},{6,127},{7,126},{8... | collective-permute-start | bytes 2359304 | tf_op jit(solution)/shard_map/ppermute | solution.py:223
  103.0 24.0 %collective-permute-start.33 = (bf16[24,128,128]{2,1,0:T(8,128)(2,1)}, bf16[24,128,128]{2,1,0:T(8,128)(2,1)}, u32[]{:S(2)}, u32[]{:S(2)}) collective-permute-start(bf16[24,128,128]{2,1,0:T(8,128)(2,1)} %pick_b.7), channel_id=1, source_target_pairs={{0,1},{1,0},{2,3},{3,2},{4,5},{5,4},{6,7},{7,6},{8,16},{9,17},{10,... | collective-permute-start | bytes 2359304 | tf_op jit(solution)/shard_map/ppermute | solution.py:223
  113.3 16.5 %collective-permute-start.35 = (bf16[24,128,128]{2,1,0:T(8,128)(2,1)}, bf16[24,128,128]{2,1,0:T(8,128)(2,1)S(1)}, u32[]{:S(2)}, u32[]{:S(2)}) collective-permute-start(bf16[24,128,128]{2,1,0:T(8,128)(2,1)} %pick_c.9), channel_id=1, source_target_pairs={{0,2},{1,7},{2,4},{3,1},{4,6},{5,3},{6,0},{7,5},{8,16},{9,17},{10,... | collective-permute-start | bytes 2359304 | tf_op jit(solution)/shard_map/ppermute | solution.py:223
  127.0 12.2 %collective-permute-start.34 = (bf16[24,128,128]{2,1,0:T(8,128)(2,1)}, bf16[24,128,128]{2,1,0:T(8,128)(2,1)S(1)}, u32[]{:S(2)}, u32[]{:S(2)}) collective-permute-start(bf16[24,128,128]{2,1,0:T(8,128)(2,1)} %pick_b.8), channel_id=1, source_target_pairs={{0,1},{1,0},{2,3},{3,2},{4,5},{5,4},{6,7},{7,6},{8,16},{9,17},{10,... | collective-permute-start | bytes 2359304 | tf_op jit(solution)/shard_map/ppermute | solution.py:223
  128.0 12.1 %collective-permute-start.32 = (bf16[24,128,128]{2,1,0:T(8,128)(2,1)}, bf16[24,128,128]{2,1,0:T(8,128)(2,1)}, u32[]{:S(2)}, u32[]{:S(2)}) collective-permute-start(bf16[24,128,128]{2,1,0:T(8,128)(2,1)} %collective-permute-done.24.b_ref.refs_9_), channel_id=1, source_target_pairs={{0,8},{1,9},{2,10},{3,11},{4,12},{5,13},{6,14},{7,15},{8,0},{9,1},... | collective-permute-start | bytes 2359304 | tf_op jit(solution)/shard_map/ppermute | solution.py:223
  128.1 12.6 %collective-permute-start.31 = (bf16[24,128,128]{2,1,0:T(8,128)(2,1)S(1)}, bf16[24,128,128]{2,1,0:T(8,128)(2,1)}, u32[]{:S(2)}, u32[]{:S(2)}) collective-permute-start(bf16[24,128,128]{2,1,0:T(8,128)(2,1)S(1)} %copy-done.18), channel_id=1, source_target_pairs={{0,8},{1,9},{2,10},{3,11},{4,12},{5,13},{6,14},{7,15},{8,0},{9,1},... | collective-permute-start | bytes 2359304 | tf_op jit(solution)/shard_map/ppermute | solution.py:223
  130.7 21.0 %collective-permute-start.19 = (bf16[24,128,128]{2,1,0:T(8,128)(2,1)}, bf16[24,128,128]{2,1,0:T(8,128)(2,1)}, u32[]{:S(2)}, u32[]{:S(2)}) collective-permute-start(bf16[24,128,128]{2,1,0:T(8,128)(2,1)} %collective-permute-done.6.b_ref.refs_3_), channel_id=1, source_target_pairs={{0,2},{1,7},{2,4},{3,1},{4,6},{5,3},{6,0},{7,5},{8,10},{9,15},{10,... | collective-permute-start | bytes 2359304 | tf_op jit(solution)/shard_map/ppermute | solution.py:223
  140.1 16.6 %collective-permute-start.28 = (bf16[24,128,128]{2,1,0:T(8,128)(2,1)}, bf16[24,128,128]{2,1,0:T(8,128)(2,1)}, u32[]{:S(2)}, u32[]{:S(2)}) collective-permute-start(bf16[24,128,128]{2,1,0:T(8,128)(2,1)} %collective-permute-done.6.b_ref.refs_3_), channel_id=1, source_target_pairs={{0,8},{1,9},{2,10},{3,11},{4,12},{5,13},{6,14},{7,15},{8,0},{9,1},... | collective-permute-start | bytes 2359304 | tf_op jit(solution)/shard_map/ppermute | solution.py:223
  140.1 19.7 %collective-permute-start.29 = (bf16[24,128,128]{2,1,0:T(8,128)(2,1)}, bf16[24,128,128]{2,1,0:T(8,128)(2,1)}, u32[]{:S(2)}, u32[]{:S(2)}) collective-permute-start(bf16[24,128,128]{2,1,0:T(8,128)(2,1)} %collective-permute-done.12.b_ref.refs_4_), channel_id=1, source_target_pairs={{0,8},{1,9},{2,10},{3,11},{4,12},{5,13},{6,14},{7,15},{8,0},{9,1},... | collective-permute-start | bytes 2359304 | tf_op jit(solution)/shard_map/ppermute | solution.py:223
  140.6 19.7 %collective-permute-start.8 = (bf16[24,128,128]{2,1,0:T(8,128)(2,1)}, bf16[24,128,128]{2,1,0:T(8,128)(2,1)S(1)}, u32[]{:S(2)}, u32[]{:S(2)}) collective-permute-start(bf16[24,128,128]{2,1,0:T(8,128)(2,1)} %get-tuple-element.33), channel_id=1, source_target_pairs={{0,1},{1,0},{2,3},{3,2},{4,5},{5,4},{6,7},{7,6},{8,9},{9,8},{10,11... | collective-permute-start | bytes 2359304 | tf_op jit(solution)/shard_map/ppermute | solution.py:223
  151.7 20.1 %collective-permute-start.13 = (bf16[24,128,128]{2,1,0:T(8,128)(2,1)}, bf16[24,128,128]{2,1,0:T(8,128)(2,1)S(1)}, u32[]{:S(2)}, u32[]{:S(2)}) collective-permute-start(bf16[24,128,128]{2,1,0:T(8,128)(2,1)} %collective-permute-done.12.b_ref.refs_4_), channel_id=1, source_target_pairs={{0,2},{1,7},{2,4},{3,1},{4,6},{5,3},{6,0},{7,5},{8,10},{9,15},{10,... | collective-permute-start | bytes 2359304 | tf_op jit(solution)/shard_map/ppermute | solution.py:223
  156.7 29.9 %collective-permute-start.7 = (bf16[24,128,128]{2,1,0:T(8,128)(2,1)}, bf16[24,128,128]{2,1,0:T(8,128)(2,1)S(1)}, u32[]{:S(2)}, u32[]{:S(2)}) collective-permute-start(bf16[24,128,128]{2,1,0:T(8,128)(2,1)} %get-tuple-element.33), channel_id=1, source_target_pairs={{0,121},{1,120},{2,123},{3,122},{4,125},{5,124},{6,127},{7,126},{8... | collective-permute-start | bytes 2359304 | tf_op jit(solution)/shard_map/ppermute | solution.py:223
  159.8 26.8 %collective-permute-start.25 = (bf16[24,128,128]{2,1,0:T(8,128)(2,1)}, bf16[24,128,128]{2,1,0:T(8,128)(2,1)}, u32[]{:S(2)}, u32[]{:S(2)}) collective-permute-start(bf16[24,128,128]{2,1,0:T(8,128)(2,1)} %pick_c.7), channel_id=1, source_target_pairs={{0,2},{1,7},{2,4},{3,1},{4,6},{5,3},{6,0},{7,5},{8,16},{9,17},{10,... | collective-permute-start | bytes 2359304 | tf_op jit(solution)/shard_map/ppermute | solution.py:223
  160.4 40.1 %copy-start.19 = (bf16[24,128,128]{2,1,0:T(8,128)(2,1)}, bf16[24,128,128]{2,1,0:T(8,128)(2,1)S(1)}, u32[]{:S(2)}) copy-start(bf16[24,128,128]{2,1,0:T(8,128)(2,1)S(1)} %collective-permute-done.8.b_ref.refs_3_) | copy-start | bytes 2359300
  160.4 26.2 %collective-permute-start.22 = (bf16[24,128,128]{2,1,0:T(8,128)(2,1)}, bf16[24,128,128]{2,1,0:T(8,128)(2,1)}, u32[]{:S(2)}, u32[]{:S(2)}) collective-permute-start(bf16[24,128,128]{2,1,0:T(8,128)(2,1)} %pick_b.6), channel_id=1, source_target_pairs={{0,1},{1,0},{2,3},{3,2},{4,5},{5,4},{6,7},{7,6},{8,16},{9,17},{10,... | collective-permute-start | bytes 2359304 | tf_op jit(solution)/shard_map/ppermute | solution.py:223
  171.7 25.4 %collective-permute-start.15 = (bf16[24,128,128]{2,1,0:T(8,128)(2,1)S(1)}, bf16[24,128,128]{2,1,0:T(8,128)(2,1)}, u32[]{:S(2)}, u32[]{:S(2)}) collective-permute-start(bf16[24,128,128]{2,1,0:T(8,128)(2,1)S(1)} %collective-permute-done.8.b_ref.refs_3_), channel_id=1, source_target_pairs={{0,2},{1,7},{2,4},{3,1},{4,6},{5,3},{6,0},{7,5},{8,10},{9,15},{10,... | collective-permute-start | bytes 2359304 | tf_op jit(solution)/shard_map/ppermute | solution.py:223
  186.5 19.0 %collective-permute-start.27 = (bf16[24,128,128]{2,1,0:T(8,128)(2,1)}, bf16[24,128,128]{2,1,0:T(8,128)(2,1)}, u32[]{:S(2)}, u32[]{:S(2)}) collective-permute-start(bf16[24,128,128]{2,1,0:T(8,128)(2,1)} %pick_c.8), channel_id=1, source_target_pairs={{0,2},{1,7},{2,4},{3,1},{4,6},{5,3},{6,0},{7,5},{8,16},{9,17},{10,... | collective-permute-start | bytes 2359304 | tf_op jit(solution)/shard_map/ppermute | solution.py:223
  186.6 19.0 %collective-permute-start.20 = (bf16[24,128,128]{2,1,0:T(8,128)(2,1)}, bf16[24,128,128]{2,1,0:T(8,128)(2,1)}, u32[]{:S(2)}, u32[]{:S(2)}) collective-permute-start(bf16[24,128,128]{2,1,0:T(8,128)(2,1)} %collective-permute-done.19.b_ref.refs_10_), channel_id=1, source_target_pairs={{0,8},{1,9},{2,10},{3,11},{4,12},{5,13},{6,14},{7,15},{8,0},{9,1},... | collective-permute-start | bytes 2359304 | tf_op jit(solution)/shard_map/ppermute | solution.py:223
  186.6 20.7 %collective-permute-start.21 = (bf16[24,128,128]{2,1,0:T(8,128)(2,1)S(1)}, bf16[24,128,128]{2,1,0:T(8,128)(2,1)}, u32[]{:S(2)}, u32[]{:S(2)}) collective-permute-start(bf16[24,128,128]{2,1,0:T(8,128)(2,1)S(1)} %collective-permute-done.13.b_ref.refs_6_), channel_id=1, source_target_pairs={{0,8},{1,9},{2,10},{3,11},{4,12},{5,13},{6,14},{7,15},{8,0},{9,1},... | collective-permute-start | bytes 2359304 | tf_op jit(solution)/shard_map/ppermute | solution.py:223
  197.1 49.6 %collective-permute-start.18 = (bf16[24,128,128]{2,1,0:T(8,128)(2,1)S(1)}, bf16[24,128,128]{2,1,0:T(8,128)(2,1)}, u32[]{:S(2)}, u32[]{:S(2)}) collective-permute-start(bf16[24,128,128]{2,1,0:T(8,128)(2,1)S(1)} %collective-permute-done.8.b_ref.refs_3_), channel_id=1, source_target_pairs={{0,8},{1,9},{2,10},{3,11},{4,12},{5,13},{6,14},{7,15},{8,0},{9,1},... | collective-permute-start | bytes 2359304 | tf_op jit(solution)/shard_map/ppermute | solution.py:223
  205.5 54.1 %collective-permute-start.14 = (bf16[24,128,128]{2,1,0:T(8,128)(2,1)}, bf16[24,128,128]{2,1,0:T(8,128)(2,1)S(1)}, u32[]{:S(2)}, u32[]{:S(2)}) collective-permute-start(bf16[24,128,128]{2,1,0:T(8,128)(2,1)} %pick_c.5), channel_id=1, source_target_pairs={{0,2},{1,7},{2,4},{3,1},{4,6},{5,3},{6,0},{7,5},{8,16},{9,17},{10,... | collective-permute-start | bytes 2359304 | tf_op jit(solution)/shard_map/ppermute | solution.py:223
  205.6 54.1 %collective-permute-start.9 = (bf16[24,128,128]{2,1,0:T(8,128)(2,1)}, bf16[24,128,128]{2,1,0:T(8,128)(2,1)S(1)}, u32[]{:S(2)}, u32[]{:S(2)}) collective-permute-start(bf16[24,128,128]{2,1,0:T(8,128)(2,1)} %pick_b.5), channel_id=1, source_target_pairs={{0,1},{1,0},{2,3},{3,2},{4,5},{5,4},{6,7},{7,6},{8,16},{9,17},{10,... | collective-permute-start | bytes 2359304 | tf_op jit(solution)/shard_map/ppermute | solution.py:223
  207.3 52.4 %collective-permute-start.16 = (bf16[24,128,128]{2,1,0:T(8,128)(2,1)}, bf16[24,128,128]{2,1,0:T(8,128)(2,1)S(1)}, u32[]{:S(2)}, u32[]{:S(2)}) collective-permute-start(bf16[24,128,128]{2,1,0:T(8,128)(2,1)} %pick_c.6), channel_id=1, source_target_pairs={{0,2},{1,7},{2,4},{3,1},{4,6},{5,3},{6,0},{7,5},{8,16},{9,17},{10,... | collective-permute-start | bytes 2359304 | tf_op jit(solution)/shard_map/ppermute | solution.py:223
  207.5 52.1 %collective-permute-start.17 = (bf16[24,128,128]{2,1,0:T(8,128)(2,1)}, bf16[24,128,128]{2,1,0:T(8,128)(2,1)S(1)}, u32[]{:S(2)}, u32[]{:S(2)}) collective-permute-start(bf16[24,128,128]{2,1,0:T(8,128)(2,1)} %collective-permute-done.15.b_ref.refs_7_), channel_id=1, source_target_pairs={{0,8},{1,9},{2,10},{3,11},{4,12},{5,13},{6,14},{7,15},{8,0},{9,1},... | collective-permute-start | bytes 2359304 | tf_op jit(solution)/shard_map/ppermute | solution.py:223
  269.1 111.5 %all-to-all-start = ((bf16[256,128,128]{2,1,0:T(8,128)(2,1)}), bf16[256,128,128]{2,1,0:T(8,128)(2,1)}, u32[]{:S(2)}, u32[]{:S(2)}) async-start(bf16[256,128,128]{2,1,0:T(8,128)(2,1)} %finish.1), calls=%async_computation | async-start | bytes 16777216 | tf_op jit(solution)/shard_map/all_to_all | solution.py:349
  (39 other events, 710.7 us)

commit v2 on v1

v2 whole, which is shorter than its diff:
```python
import jax
import jax.numpy as jnp
from jax import lax
from jax.experimental import pallas as pl
from jax.experimental.pallas import tpu as pltpu
from jax.sharding import PartitionSpec as P

AXES = ("row", "col")
UNROLL = 24


def at_wrap(r, rows):
    half = rows // 2
    return r in (0, half - 1, half, rows - 1)


def permutations(rows, cols):
    def build(target):
        pairs = []
        for r in range(rows):
            for c in range(cols):
                reached = target(r, c)
                if reached is None:
                    continue
                tr, tc = reached
                pairs.append((r * cols + c, (tr % rows) * cols + tc % cols))
        return pairs

    def beside(r):
        return r + 1 if r % 2 else r - 1

    def along(c):
        return c + 2 if c % 2 == 0 else c - 2

    def only(wrapped, target):
        return build(lambda r, c: target(r, c) if at_wrap(r, rows) == wrapped else None)

    def other(c):
        return c - 1 if c % 2 == 0 else c + 1

    def back(c):
        return c - 2 if c % 2 == 0 else c + 2

    return {
        "pair": build(lambda r, c: (r, c ^ 1)),
        "along": build(lambda r, c: (r, along(c))),
        "far": build(lambda r, c: (r, other(c))),
        "core": build(lambda r, c: (r ^ 1, c)),
        "beside": build(lambda r, c: (beside(r), c)),
        "cross": build(lambda r, c: (beside(r), c ^ 1) if at_wrap(r, rows) else (beside(r), c)),
        "inner_beside": only(False, lambda r, c: (beside(r), c)),
        "wrap_pair": only(True, lambda r, c: (r, c ^ 1)),
        "wrap_back": only(True, lambda r, c: (r, back(c))),
        "wrap_cross": only(True, lambda r, c: (beside(r), c ^ 1)),
    }


def add_entries(count_ref, list_ref, left_ref, pool, acc):
    def group(g, _):
        for q in range(UNROLL):
            code = list_ref[g * UNROLL + q]
            slot = code & 127
            block = (code >> 7) & 1023
            acc[slot] += jnp.dot(
                left_ref[code >> 17], pool[block], preferred_element_type=jnp.float32
            )
        return 0

    lax.fori_loop(0, (count_ref[0] + UNROLL - 1) // UNROLL, group, 0)


def load_pool(flag_ref, refs, chunks, pool, sems):
    refs, copies, start = list(refs), [], 0
    for n, chunk in enumerate(chunks):
        size = chunk[-1].shape[0]
        into = pool.at[pl.ds(start, size)]
        if len(chunk) == 1:
            copies.append(pltpu.make_async_copy(refs.pop(0), into, sems.at[n]))
            copies[-1].start()
        else:
            at_cut = pltpu.make_async_copy(refs.pop(0).at[pl.ds(chunk[1], size)], into, sems.at[n])
            elsewhere = pltpu.make_async_copy(refs.pop(0), into, sems.at[n])
            pl.when(flag_ref[0] != 0)(at_cut.start)
            pl.when(flag_ref[0] == 0)(elsewhere.start)
            copies.append(elsewhere)
        start += size
    return copies


def arrays_of(chunks):
    return [one for chunk in chunks for one in chunk if not isinstance(one, int)]


def accumulate(name, flag, count, entries, left, chunks, acc):
    arrays = arrays_of(chunks)
    n, size = len(arrays), sum(chunk[-1].shape[0] for chunk in chunks)
    order = left.shape[-1]
    slots = left.shape[0] + 8
    fresh = acc is None

    def body(*refs):
        flag_ref, count_ref, list_ref, left_hbm = refs[:4]
        out, total, left_ref, pool, sems = refs[-5:]
        fetch_left = pltpu.make_async_copy(left_hbm, left_ref, sems.at[n + 1])
        fetch_left.start()
        copies = load_pool(flag_ref, refs[4 : 4 + n], chunks, pool, sems)
        if fresh:
            total[...] = jnp.zeros(total.shape, total.dtype)
        else:
            fetch = pltpu.make_async_copy(refs[4 + n], total, sems.at[n])
            fetch.start()
            copies.append(fetch)
        for copy in [fetch_left, *copies]:
            copy.wait()
        add_entries(count_ref, list_ref, left_ref, pool, total)
        store = pltpu.make_async_copy(total, out, sems.at[n])
        store.start()
        store.wait()

    smem = pl.BlockSpec(memory_space=pltpu.SMEM)
    anywhere = pl.BlockSpec(memory_space=pl.ANY)
    args = [flag, count, entries, left, *arrays] + ([] if fresh else [acc])
    return pl.pallas_call(
        body,
        out_shape=jax.ShapeDtypeStruct((slots, order, order), jnp.float32),
        in_specs=[smem] * 3 + [anywhere] * (1 + n + (not fresh)),
        out_specs=anywhere,
        scratch_shapes=[
            pltpu.VMEM((slots, order, order), jnp.float32),
            pltpu.VMEM(left.shape, jnp.bfloat16),
            pltpu.VMEM((size, order, order), jnp.bfloat16),
            pltpu.SemaphoreType.DMA((n + 2,)),
        ],
        input_output_aliases={} if fresh else {4 + n: 0},
        compiler_params=pltpu.CompilerParams(vmem_limit_bytes=36 << 20),
        cost_estimate=pl.CostEstimate(flops=8 << 30, bytes_accessed=32 << 20, transcendentals=0),
        name=name,
    )(*args)


def finish(name, flag, count, entries, left, chunks, acc, inverse):
    arrays = arrays_of(chunks)
    n, size = len(arrays), sum(chunk[-1].shape[0] for chunk in chunks)
    order = left.shape[-1]
    slots = inverse.shape[0]
    part = 16

    def body(*refs):
        flag_ref, count_ref, list_ref, inverse_ref, left_hbm = refs[:5]
        acc_ref, out, total, left_ref, pool, stage, sems, out_sems = refs[5 + n :]
        fetch_left = pltpu.make_async_copy(left_hbm, left_ref, sems.at[n + 1])
        fetch_left.start()
        copies = load_pool(flag_ref, refs[5 : 5 + n], chunks, pool, sems)
        fetch = pltpu.make_async_copy(acc_ref, total, sems.at[n])
        fetch.start()
        for copy in [fetch_left, *copies, fetch]:
            copy.wait()
        add_entries(count_ref, list_ref, left_ref, pool, total)

        def piece(p):
            return pltpu.make_async_copy(
                stage.at[pl.ds(p * part, part)], out.at[pl.ds(p * part, part)], out_sems.at[p]
            )

        def fill(p, _):
            for q in range(part):
                s = p * part + q
                t = inverse_ref[s]
                value = total[jnp.maximum(t, 0)]
                stage[s] = jnp.where(t >= 0, value, 0.0).astype(jnp.bfloat16)
            piece(p).start()
            return 0

        lax.fori_loop(0, slots // part, fill, 0)

        def drain(p, _):
            piece(p).wait()
            return 0

        lax.fori_loop(0, slots // part, drain, 0)

    smem = pl.BlockSpec(memory_space=pltpu.SMEM)
    anywhere = pl.BlockSpec(memory_space=pl.ANY)
    return pl.pallas_call(
        body,
        out_shape=jax.ShapeDtypeStruct((slots, order, order), jnp.bfloat16),
        in_specs=[smem] * 4 + [anywhere] * (n + 2),
        out_specs=anywhere,
        scratch_shapes=[
            pltpu.VMEM(acc.shape, jnp.float32),
            pltpu.VMEM(left.shape, jnp.bfloat16),
            pltpu.VMEM((size, order, order), jnp.bfloat16),
            pltpu.VMEM((slots, order, order), jnp.bfloat16),
            pltpu.SemaphoreType.DMA((n + 2,)),
            pltpu.SemaphoreType.DMA((slots // part,)),
        ],
        compiler_params=pltpu.CompilerParams(vmem_limit_bytes=40 << 20),
        cost_estimate=pl.CostEstimate(flops=0, bytes_accessed=1 << 18, transcendentals=0),
        name=name,
    )(flag, count, entries, inverse, left, *arrays, acc)


def shards(blocks, pattern, owner):
    held, stored, order = blocks.shape[:3]
    rows, cols = lax.axis_size("row"), lax.axis_size("col")
    devices = rows * cols
    r, c = lax.axis_index("row"), lax.axis_index("col")
    here = r * cols + c
    perms = permutations(rows, cols)
    half = rows // 2
    wrap = (r == 0) | (r == half - 1) | (r == half) | (r == rows - 1)
    items = held * stored
    left = blocks.reshape(items, order, order)

    flag = [wrap.astype(jnp.int32).reshape(1)]
    got = {}

    def after(x):
        x, flag[0] = lax.optimization_barrier((x, flag[0]))
        return x

    def wait(*keys):
        for key in keys:
            got[key] = after(got[key])

    def send(x, which):
        return lax.ppermute(after(x), AXES, perms[which])

    pair = c ^ 1
    far = jnp.where(c % 2 == 0, c - 1 + cols, c + 1) % cols
    beside = jnp.where(r % 2 == 1, r + 1, r - 1 + rows) % rows
    holders = {
        "O": here,
        "X": r * cols + pair,
        "Z": r * cols + far,
        "DO": (r ^ 1) * cols + c,
        "DX": (r ^ 1) * cols + pair,
        "DZ": (r ^ 1) * cols + far,
        "A": beside * cols + jnp.where(wrap, pair, c),
        "B": beside * cols + jnp.where(wrap, c, pair),
        "C": beside * cols + far,
    }
    numbers = jnp.arange(stored, dtype=jnp.int32)
    own_slots = jnp.arange(items, dtype=jnp.int32).reshape(held, stored)

    def codes_of(patterns, ids, first):
        into = jnp.max(jnp.where(ids[:, None, None] == pattern[None], own_slots[None], -1), axis=-1)
        to = jnp.max(jnp.where(patterns[:, :, None, None] == pattern[None, None], own_slots[None, None], -1), axis=-1)
        into = into[:, None, :]
        block = (first[:, None] + numbers[None, :])[:, :, None]
        code = (into << 17) | (block << 7) | to
        return jnp.where((into >= 0) & (to >= 0), code, -1).reshape(patterns.shape[0], items)

    def listing(codes):
        codes = codes.reshape(-1)
        total = codes.shape[0]
        length = -(-total // UNROLL) * UNROLL
        ok = codes >= 0
        place = jnp.where(ok, jnp.cumsum(ok.astype(jnp.int32)) - 1, -1)
        count = jnp.sum(ok.astype(jnp.int32)).reshape(1)
        order_of = jnp.arange(length, dtype=jnp.int32)
        listed = jnp.sum(jnp.where(place[None, :] == order_of[:, None], codes[None, :], 0), axis=1)
        return count, jnp.where(order_of < count, listed, items)

    cuts = [(0, 3), (3, 5)]
    whole = (0, held)

    def rows_of(key):
        slot, p = key
        lo, hi = whole if p is None else cuts[p]
        return [(slot, k) for k in range(lo, hi)]

    calls = {
        "core": [("DO", None), ("A", None)],
        "first": [("X", 0), ("X", 1), ("Z", 0), ("DX", 0), ("DX", 1), ("DZ", 0)],
        "second": [("B", 0), ("B", 1), ("Z", 1), ("C", 0)],
        "last": [("C", 1), ("DZ", 1)],
    }

    def chunk_of(key):
        slot, p = key
        if slot in ("B", "C"):
            return (got["V" if slot == "B" else "F"], cuts[p][0] * stored, got[key])
        return (got[key],)

    x0 = left[cuts[0][0] * stored : cuts[0][1] * stored]
    got["DO", None] = send(left, "core")
    got["A", None] = send(left, "cross")
    got["X", 0] = send(x0, "pair")
    got["p2"] = send(pattern, "far")
    got["p1"] = send(pattern, "pair")
    wait("p1", "p2", ("DO", None))
    columns = jnp.stack([pattern, got["p1"], got["p2"]])
    got["W"] = send(left, "wrap_back")
    got["p3"] = send(columns, "core")
    got["p4"] = send(columns, "beside")
    got["x1"] = after(left)[cuts[1][0] * stored : cuts[1][1] * stored]
    own_codes = codes_of(after(pattern), here * held + jnp.arange(held), jnp.arange(held) * stored)
    got["own"] = listing(own_codes)
    wait("own")
    got["acc"] = accumulate("own", flag[0], *got["own"], left, [(left,)], None)
    owners = after(owner).reshape(items)
    number = jnp.arange(items, dtype=jnp.int32)
    earlier = (owners[:, None] == owners[None, :]) & (number[None, :] < number[:, None])
    rank = jnp.sum(earlier.astype(jnp.int32), axis=1)
    capacity = max(2, items // devices + 1)
    target = owners * capacity + rank
    landed = target[None, :] == jnp.arange(devices * capacity, dtype=jnp.int32)[:, None]
    got["inverse"] = jnp.sum(jnp.where(landed, number[None, :] + 1, 0), axis=1) - 1
    outgoing_ids = jnp.where(got["inverse"] >= 0, here * items + got["inverse"], -1)
    got["ids"] = lax.all_to_all(
        after(outgoing_ids).reshape(devices, capacity), AXES, split_axis=0, concat_axis=0, tiled=True
    )
    wait("acc", "W", ("A", None), "x1", "inverse", "p3", "p4")
    lists = {}
    core, near = got["p3"], got["p4"]
    patterns = {
        "O": pattern,
        "X": got["p1"],
        "Z": got["p2"],
        "DO": core[0],
        "DX": core[1],
        "DZ": core[2],
        "A": jnp.where(wrap, near[1], near[0]),
        "B": jnp.where(wrap, near[0], near[1]),
        "C": near[2],
    }
    pats, ids, first, bounds = [], [], [], [0]
    for names in calls.values():
        block = 0
        for key in names:
            for s, k in rows_of(key):
                pats.append(patterns[s][k : k + 1])
                ids.append(holders[s] * held + k)
                first.append(block)
                block += stored
        bounds.append(len(first))
    codes = codes_of(after(jnp.concatenate(pats)), jnp.stack(ids), jnp.asarray(first, jnp.int32))
    for name, lo, hi in zip(calls, bounds[:-1], bounds[1:]):
        lists[name] = listing(codes[lo:hi])

    for name in calls:
        lists[name] = tuple(after(x) for x in lists[name])
    wait(("X", 0))


    def run(name):
        chunks = [chunk_of(key) for key in calls[name]]
        got["acc"] = accumulate(name, flag[0], *lists[name], left, chunks, got["acc"])

    got["DX", 0] = send(got["X", 0], "core")
    got["F"] = send(got["W"], "wrap_cross")
    got["B", 0] = send(got["X", 0], "inner_beside")
    got["X", 1] = send(got["x1"], "pair")
    got["Z", 0] = send(got["X", 0], "along")
    run("core")
    wait("acc", ("Z", 0), ("X", 1), ("B", 0), "F", ("DX", 0))
    got["DX", 1] = send(got["X", 1], "core")
    got["B", 1] = send(got["X", 1], "inner_beside")
    got["V"] = send(got["A", None], "wrap_pair")
    got["C", 0] = send(got["Z", 0], "inner_beside")
    got["Z", 1] = send(got["X", 1], "along")
    wait(("DX", 1))
    got["DZ", 0] = send(got["Z", 0], "core")
    wait(("DZ", 0))
    run("first")
    wait("acc", "V", ("Z", 1), ("C", 0), ("B", 1), "ids")
    got["DZ", 1] = send(got["Z", 1], "core")
    got["C", 1] = send(got["Z", 1], "inner_beside")
    run("second")
    wait("acc", ("C", 1), ("DZ", 1))
    outgoing = finish(
        "last", flag[0], *lists["last"], left, [chunk_of(key) for key in calls["last"]], got["acc"], got["inverse"]
    )
    arrived_ids = got["ids"].reshape(devices * capacity)
    outgoing, arrived_ids = lax.optimization_barrier((outgoing, arrived_ids))
    arrived = lax.all_to_all(outgoing.reshape(-1, order), AXES, split_axis=0, concat_axis=0, tiled=True)
    arrived = arrived.reshape(outgoing.shape)
    return arrived, arrived_ids


def solution(mesh):
    in_specs = (P(AXES, None, None, None), P(AXES, None), P(AXES, None))
    out_specs = (P(AXES, None, None), P(AXES))
    return jax.shard_map(shards, mesh=mesh, in_specs=in_specs, out_specs=out_specs, check_vma=False)
```

time: 399 us -> 336 us (0.84); the launches traced: 392 us -> 335 us
  waiting for transfers between devices: 192 us -> 80.9 us
  blocking collectives: 0 us -> 109 us
  other arithmetic: 30.3 us -> 13.6 us
  starting transfers between devices: 52.1 us -> 35.6 us
  Pallas kernels: 75.6 us -> 64.7 us
  local copies, waits for them, and re-layouts: 39.6 us -> 29.8 us
    all_to_all x0 -> x1, blocking collectives: none -> 109 us  [shards(): lax.all_to_all(outgoing.reshape(-1, order), AXES, split_axis=0, concat_ax...]
    all_to_all x2 -> x1, waiting for transfers between devices: 99.9 us -> 6.4 us  [shards(): lax.all_to_all(after(outgoing_ids).reshape(devices, capacity), AXES, spli...]
    pallas_call x10 -> x0, Pallas kernels: 20.5 us -> none  [pick(): pl.pallas_call(body, out_shape=jax.ShapeDtypeStruct(a.shape, a.dtype), in...]
    ppermute x40 -> x21, waiting for transfers between devices: 91.9 us -> 74.5 us  [send(): return lax.ppermute(after(x), AXES, perms[which])]
    all_to_all x2 -> x1, starting transfers between devices: 15.6 us -> 7.35 us  [shards(): lax.all_to_all(after(outgoing_ids).reshape(devices, capacity), AXES, spli...]
    ppermute x40 -> x21, starting transfers between devices: 36.5 us -> 28.3 us  [send(): return lax.ppermute(after(x), AXES, perms[which])]
    shift_left x13 -> x0, local copies, waits for them, and re-layouts: 7.76 us -> none  [tables(): block_number + n * stored << 7]
    pallas_call x5 -> x4, Pallas kernels: 45.7 us -> 53.3 us  [accumulate(): pl.pallas_call(body, out_shape=jax.ShapeDtypeStruct((slots, order, order)...]
  transfers between devices with their start and end apart: 42 -> 22, of which waited for: 15 -> 7; matrix products, arithmetic and copies ran while one was open for 13% -> 7% of each run, Pallas kernels for 19% -> 16%
where the time goes in v2:
time: 336 us; the launch traced here: 335 us
  blocking collectives  109 us (32%)
  waiting for transfers between devices  80.9 us (24%)
  Pallas kernels  64.7 us (19%)
  starting transfers between devices  35.6 us (11%)
  local copies, waits for them, and re-layouts  29.8 us (9%)
  other arithmetic  13.6 us (4%)
    all_to_all x1, blocking collectives, shards(): lax.all_to_all(outgoing.reshape(-1, order), AXES, split_axis=0, concat_ax...  109 us
    ppermute x21, waiting for transfers between devices, send(): return lax.ppermute(after(x), AXES, perms[which])  74.5 us
    pallas_call x4, Pallas kernels, accumulate(): pl.pallas_call(body, out_shape=jax.ShapeDtypeStruct((slots, order, order)...  53.3 us
    ppermute x21, starting transfers between devices, send(): return lax.ppermute(after(x), AXES, perms[which])  28.3 us
    unnamed x17, local copies, waits for them, and re-layouts  19.6 us
    pallas_call x1, Pallas kernels, finish(): pl.pallas_call(body, out_shape=jax.ShapeDtypeStruct((slots, order, order)...  11.3 us
    all_to_all x1, starting transfers between devices, shards(): lax.all_to_all(after(outgoing_ids).reshape(devices, capacity), AXES, spli...  7.35 us
  transfers between devices with their start and end apart: 22, of which 7 were waited for; matrix products, arithmetic and copies ran while one was open for 7% of the time, Pallas kernels for 16%

profile of v2, /device:TPU:0, one launch (start us, length us, event | category | flops | bytes accessed | tf_op | source)
XLA Modules:
  0.0 335.1 jit_solution(5420562772736112203)
XLA Ops:
  0.8 1.9 slice.253
  2.7 1.7 collective-permute-start
  4.4 4.0 %collective-permute-start.1 = (s32[5,24]{1,0:T(8,128)S(1)}, s32[5,24]{1,0:T(8,128)S(1)}, u32[]{:S(2)}, u32[]{:S(2)}) collective-permute-start(s32[5,24]{1,0:T(8,128)S(1)} %copy-done.5), channel_id=1, source_target_pairs={{0,7},{1,2},{2,1},{3,4},{4,3},{5,6},{6,5},{7,0},{8,15},{9,10},{10,... | collective-permute-start | bytes 1448 | tf_op jit(solution)/shard_map/ppermute | solution.py:227
  8.4 2.6 collective-permute-start.3
  11.0 2.3 collective-permute-start.5
  13.9 2.3 collective-permute-start.4
  16.4 0.6 select_reduce_fusion.6
  17.0 0.7 convert_reduce_fusion.4
  18.9 0.6 fusion.6.refs_2_
  19.6 2.7 collective-permute-start.7
  22.6 7.5 %own.1.refs_6_ = f32[128,128,128]{2,1,0:T(8,128)S(1)} custom-call(s32[1]{0:T(128)} %bitcast.3.refs_0_, s32[1]{0:T(128)} %bitcast.6.refs_1_, s32[600]{0:T(1024)S(1)} %fusion.6.refs_2_, bf16[120,128,128]{2,1,0:T(8,128)(2,1)} %bitcast.refs_3_.refs_4_, bf16[120,128,128]{2,1,0:T(8,128)(2,1)} %bitcast.refs_3_.refs_4_), custom_call_target="tpu_custom_call" | custom-call | flops 8589934592 | bytes 33554432 | tf_op jit(solution)/shard_map/own/pallas_call | solution.py:123
  30.1 3.4 %copy-done = f32[128,128,128]{2,1,0:T(8,128)} copy-done((f32[128,128,128]{2,1,0:T(8,128)}, f32[128,128,128]{2,1,0:T(8,128)S(1)}, u32[]{:S(2)}) %copy-start) | copy-done | bytes 8388632
  33.5 2.8 slice.255
  36.2 25.6 %collective-permute-done.4 = bf16[120,128,128]{2,1,0:T(8,128)(2,1)} collective-permute-done((bf16[120,128,128]{2,1,0:T(8,128)(2,1)}, bf16[120,128,128]{2,1,0:T(8,128)(2,1)}, u32[]{:S(2)}, u32[]{:S(2)}) %collective-permute-start.4) | collective-permute-done | bytes 3932192 | tf_op jit(solution)/shard_map/ppermute | solution.py:227
  61.9 4.5 %collective-permute-done.7 = s32[3,5,24]{2,1,0:T(8,128)S(1)} collective-permute-done((s32[3,5,24]{2,1,0:T(8,128)S(1)}, s32[3,5,24]{2,1,0:T(8,128)S(1)}, u32[]{:S(2)}, u32[]{:S(2)}) %collective-permute-start.7) | collective-permute-done | bytes 1472 | tf_op jit(solution)/shard_map/ppermute | solution.py:227
  67.3 0.7 convert_reduce_fusion
  68.1 0.8 fusion.8
  70.0 0.7 select_reduce_fusion.1
  70.7 0.7 fusion.5.refs_2_
  72.9 1.5 select_reduce_fusion
  74.4 0.7 fusion.4.refs_2_
  76.2 0.7 select_reduce_fusion.2
  77.5 0.8 convert_reduce_fusion.2
  79.5 0.6 fusion.7.refs_2_
  80.2 3.1 collective-permute-start.11
  83.4 1.0 collective-permute-start.12
  84.6 14.9 %core.1.refs_10_ = f32[128,128,128]{2,1,0:T(8,128)} custom-call(s32[1]{0:T(128)} %bitcast.3.refs_0_, s32[1]{0:T(128)} %bitcast.82.refs_1_, s32[1200]{0:T(1024)S(1)} %fusion.5.refs_2_, bf16[120,128,128]{2,1,0:T(8,128)(2,1)} %bitcast.refs_3_.refs_4_, bf16[120,128,128]{2,1,0:T(8,128)(2,1)} %collective-permute-done.2.refs_4_, ...), custom_call_target="tpu_custom_call", output_to_operand_aliasing={{}: (6, {})} | custom-call | flops 8589934592 | bytes 33554432 | tf_op jit(solution)/shard_map/core/pallas_call | solution.py:123
  99.5 25.9 %collective-permute-done.9.refs_6_ = bf16[72,128,128]{2,1,0:T(8,128)(2,1)} collective-permute-done((bf16[72,128,128]{2,1,0:T(8,128)(2,1)}, bf16[72,128,128]{2,1,0:T(8,128)(2,1)}, u32[]{:S(2)}, u32[]{:S(2)}) %collective-permute-start.9) | collective-permute-done | bytes 2359328 | tf_op jit(solution)/shard_map/ppermute | solution.py:227
  125.4 5.5 %collective-permute-done.11.refs_9_.refs_5_ = bf16[120,128,128]{2,1,0:T(8,128)(2,1)} collective-permute-done((bf16[120,128,128]{2,1,0:T(8,128)(2,1)}, bf16[120,128,128]{2,1,0:T(8,128)(2,1)}, u32[]{:S(2)}, u32[]{:S(2)}) %collective-permute-start.11) | collective-permute-done | bytes 3932192 | tf_op jit(solution)/shard_map/ppermute | solution.py:227
  130.8 1.4 copy-done.1
  132.2 1.9 collective-permute-start.14
  134.2 1.7 collective-permute-done.15.refs_8_
  135.9 1.2 copy-done.3
  137.2 2.1 collective-permute-start.18
  139.3 1.9 collective-permute-start.17
  141.1 0.8 all_to_all.14
  141.9 7.3 %all-to-all-start = ((s32[128,1,2]{2,1,0:T(1,128)}), s32[128,1,2]{2,1,0:T(1,128)S(1)}, u32[]{:S(2)}, u32[]{:S(2)}) async-start(s32[128,1,2]{2,1,0:T(1,128)} %bitcast.83), calls=%async_computation | async-start | bytes 131072 | tf_op jit(solution)/shard_map/all_to_all | solution.py:311
  149.3 1.7 copy-done.2
  150.9 1.4 copy-done.4
  152.3 16.8 %first.1.refs_11_ = f32[128,128,128]{2,1,0:T(8,128)} custom-call(s32[1]{0:T(128)} %bitcast.3.refs_0_, s32[1]{0:T(128)} %bitcast.79.refs_1_, s32[1920]{0:T(1024)S(1)} %fusion.4.refs_2_, bf16[120,128,128]{2,1,0:T(8,128)(2,1)} %bitcast.refs_3_.refs_4_, bf16[72,128,128]{2,1,0:T(8,128)(2,1)} %collective-permute-done.5.refs_4_, ...), custom_call_target="tpu_custom_call", output_to_operand_aliasing={{}: (10, {})} | custom-call | flops 8589934592 | bytes 33554432 | tf_op jit(solution)/shard_map/first/pallas_call | solution.py:123
  169.2 11.3 %collective-permute-done.14.refs_4_.refs_6_ = bf16[120,128,128]{2,1,0:T(8,128)(2,1)} collective-permute-done((bf16[120,128,128]{2,1,0:T(8,128)(2,1)}, bf16[120,128,128]{2,1,0:T(8,128)(2,1)}, u32[]{:S(2)}, u32[]{:S(2)}) %collective-permute-start.14) | collective-permute-done | bytes 3932192 | tf_op jit(solution)/shard_map/ppermute | solution.py:227
  180.5 6.4 %all-to-all-done = s32[128,1,2]{2,1,0:T(1,128)S(1)} async-done(((s32[128,1,2]{2,1,0:T(1,128)}), s32[128,1,2]{2,1,0:T(1,128)S(1)}, u32[]{:S(2)}, u32[]{:S(2)}) %all-to-all-start) | async-done | bytes 1056 | tf_op jit(solution)/shard_map/all_to_all | solution.py:311
  186.9 1.8 collective-permute-start.20
  189.0 14.1 %second.1.refs_8_ = f32[128,128,128]{2,1,0:T(8,128)} custom-call(s32[1]{0:T(128)} %bitcast.3.refs_0_, s32[1]{0:T(128)} %bitcast.77.refs_1_, s32[1200]{0:T(1024)S(1)} %fusion.3.refs_2_, bf16[120,128,128]{2,1,0:T(8,128)(2,1)} %bitcast.refs_3_.refs_4_, bf16[120,128,128]{2,1,0:T(8,128)(2,1)} %collective-permute-done.14.refs_4_.refs_6_, ...), custom_call_target="tpu_custom_call", output_to_operand_aliasing={{}: (11, {})} | custom-call | flops 8589934592 | bytes 33554432 | tf_op jit(solution)/shard_map/second/pallas_call | solution.py:123
  203.2 0.7 reshape.376
  203.9 11.3 %last.1 = bf16[256,128,128]{2,1,0:T(8,128)(2,1)} custom-call(s32[1]{0:T(128)} %bitcast.3.refs_0_, s32[1]{0:T(128)} %bitcast.74.refs_1_, s32[480]{0:T(512)S(1)} %fusion.7.refs_2_, s32[256]{0:T(256)S(1)} %get-tuple-element.251.refs_3_, bf16[120,128,128]{2,1,0:T(8,128)(2,1)} %bitcast.refs_3_.refs_4_, ...), custom_call_target="tpu_custom_call" | custom-call | bytes 262144 | tf_op jit(solution)/shard_map/last/pallas_call | solution.py:184
  215.2 109.4 %all_to_all.21 = bf16[128,256,128]{2,1,0:T(8,128)(2,1)} all-to-all(bf16[128,256,128]{2,1,0:T(8,128)(2,1)} %bitcast.119), channel_id=1, replica_groups=mesh['row'=16,'col'=8] {'row','col'}, dimensions={0} | all-to-all | bytes 16777216 | tf_op jit(solution)/shard_map/all_to_all | solution.py:377
  324.6 10.5 %copy.22 = bf16[256,128,128]{2,1,0:T(8,128)(2,1)} copy(bf16[256,128,128]{2,1,0:T(8,128)(2,1)} %bitcast.120) | data formatting | bytes 16777216
  (114 shorter events, 9.4 us)
Async XLA Ops:
  0.6 15.7 %copy-start.6 = (s32[40]{0:T(128)S(1)}, s32[40]{0:T(128)}, u32[]{:S(2)}) copy-start(s32[40]{0:T(128)} %constant.114.clone) | copy-start | bytes 484
  0.6 2.1 copy-start.5
  0.7 21.6 %copy-start.7 = (s32[120,1]{0,1:T(1,128)S(1)}, s32[120,1]{0,1:T(1,128)}, u32[]{:S(2)}) copy-start(s32[120,1]{0,1:T(1,128)} %param.6) | copy-start | bytes 1444
  0.7 13.3 %collective-permute-start.2 = (bf16[120,128,128]{2,1,0:T(8,128)(2,1)}, bf16[120,128,128]{2,1,0:T(8,128)(2,1)}, u32[]{:S(2)}, u32[]{:S(2)}) collective-permute-start(bf16[120,128,128]{2,1,0:T(8,128)(2,1)} %bitcast.refs_3_.refs_4_), channel_id=1, source_target_pairs={{0,8},{1,9},{2,10},{3,11},{4,12},{5,13},{6,14},{7,15},{8,0},{9,1},... | collective-permute-start | bytes 11796488 | tf_op jit(solution)/shard_map/ppermute | solution.py:227
  2.7 11.2 %collective-permute-start = (s32[5,24]{1,0:T(8,128)S(1)}, s32[5,24]{1,0:T(8,128)S(1)}, u32[]{:S(2)}, u32[]{:S(2)}) collective-permute-start(s32[5,24]{1,0:T(8,128)S(1)} %copy-done.5), channel_id=1, source_target_pairs={{0,1},{1,0},{2,3},{3,2},{4,5},{5,4},{6,7},{7,6},{8,9},{9,8},{10,11... | collective-permute-start | bytes 1448 | tf_op jit(solution)/shard_map/ppermute | solution.py:227
  4.4 9.5 %collective-permute-start.1 = (s32[5,24]{1,0:T(8,128)S(1)}, s32[5,24]{1,0:T(8,128)S(1)}, u32[]{:S(2)}, u32[]{:S(2)}) collective-permute-start(s32[5,24]{1,0:T(8,128)S(1)} %copy-done.5), channel_id=1, source_target_pairs={{0,7},{1,2},{2,1},{3,4},{4,3},{5,6},{6,5},{7,0},{8,15},{9,10},{10,... | collective-permute-start | bytes 1448 | tf_op jit(solution)/shard_map/ppermute | solution.py:227
  8.4 53.5 %collective-permute-start.3 = (bf16[120,128,128]{2,1,0:T(8,128)(2,1)}, bf16[120,128,128]{2,1,0:T(8,128)(2,1)}, u32[]{:S(2)}, u32[]{:S(2)}) collective-permute-start(bf16[120,128,128]{2,1,0:T(8,128)(2,1)} %bitcast.refs_3_.refs_4_), channel_id=1, source_target_pairs={{0,121},{1,120},{2,123},{3,122},{4,125},{5,124},{6,127},{7,126},{8... | collective-permute-start | bytes 11796488 | tf_op jit(solution)/shard_map/ppermute | solution.py:227
  11.0 69.1 %collective-permute-start.5 = (bf16[72,128,128]{2,1,0:T(8,128)(2,1)S(1)}, bf16[72,128,128]{2,1,0:T(8,128)(2,1)}, u32[]{:S(2)}, u32[]{:S(2)}) collective-permute-start(bf16[72,128,128]{2,1,0:T(8,128)(2,1)S(1)} %bitcast.121), channel_id=1, source_target_pairs={{0,1},{1,0},{2,3},{3,2},{4,5},{5,4},{6,7},{7,6},{8,9},{9,8},{10,11... | collective-permute-start | bytes 7077896 | tf_op jit(solution)/shard_map/ppermute | solution.py:227
  13.9 47.9 %collective-permute-start.4 = (bf16[120,128,128]{2,1,0:T(8,128)(2,1)}, bf16[120,128,128]{2,1,0:T(8,128)(2,1)}, u32[]{:S(2)}, u32[]{:S(2)}) collective-permute-start(bf16[120,128,128]{2,1,0:T(8,128)(2,1)} %bitcast.refs_3_.refs_4_), channel_id=1, source_target_pairs={{0,6},{1,3},{2,0},{3,5},{4,2},{5,7},{6,4},{7,1},{56,62},{57,59},{5... | collective-permute-start | bytes 11796488 | tf_op jit(solution)/shard_map/ppermute | solution.py:227
  19.5 42.3 %collective-permute-start.6 = (s32[3,5,24]{2,1,0:T(8,128)S(1)}, s32[3,5,24]{2,1,0:T(8,128)S(1)}, u32[]{:S(2)}, u32[]{:S(2)}) collective-permute-start(s32[3,5,24]{2,1,0:T(8,128)S(1)} %pad_add_fusion), channel_id=1, source_target_pairs={{0,8},{1,9},{2,10},{3,11},{4,12},{5,13},{6,14},{7,15},{8,0},{9,1},... | collective-permute-start | bytes 4328 | tf_op jit(solution)/shard_map/ppermute | solution.py:227
  19.6 46.8 %collective-permute-start.7 = (s32[3,5,24]{2,1,0:T(8,128)S(1)}, s32[3,5,24]{2,1,0:T(8,128)S(1)}, u32[]{:S(2)}, u32[]{:S(2)}) collective-permute-start(s32[3,5,24]{2,1,0:T(8,128)S(1)} %pad_add_fusion), channel_id=1, source_target_pairs={{0,120},{1,121},{2,122},{3,123},{4,124},{5,125},{6,126},{7,127},{8... | collective-permute-start | bytes 4328 | tf_op jit(solution)/shard_map/ppermute | solution.py:227
  30.0 3.4 %copy-start = (f32[128,128,128]{2,1,0:T(8,128)}, f32[128,128,128]{2,1,0:T(8,128)S(1)}, u32[]{:S(2)}) copy-start(f32[128,128,128]{2,1,0:T(8,128)S(1)} %own.1.refs_6_) | copy-start | bytes 25165828
  80.2 50.7 %collective-permute-start.11 = (bf16[120,128,128]{2,1,0:T(8,128)(2,1)}, bf16[120,128,128]{2,1,0:T(8,128)(2,1)}, u32[]{:S(2)}, u32[]{:S(2)}) collective-permute-start(bf16[120,128,128]{2,1,0:T(8,128)(2,1)} %collective-permute-done.4), channel_id=1, source_target_pairs={{0,121},{1,120},{2,123},{3,122},{4,125},{5,124},{6,127},{7,126},{5... | collective-permute-start | bytes 11796488 | tf_op jit(solution)/shard_map/ppermute | solution.py:227
  83.3 42.1 %collective-permute-start.9 = (bf16[72,128,128]{2,1,0:T(8,128)(2,1)}, bf16[72,128,128]{2,1,0:T(8,128)(2,1)}, u32[]{:S(2)}, u32[]{:S(2)}) collective-permute-start(bf16[72,128,128]{2,1,0:T(8,128)(2,1)} %collective-permute-done.5.refs_4_), channel_id=1, source_target_pairs={{0,2},{1,7},{2,4},{3,1},{4,6},{5,3},{6,0},{7,5},{8,10},{9,15},{10,... | collective-permute-start | bytes 7077896 | tf_op jit(solution)/shard_map/ppermute | solution.py:227
  83.4 42.0 %collective-permute-start.12 = (bf16[72,128,128]{2,1,0:T(8,128)(2,1)}, bf16[72,128,128]{2,1,0:T(8,128)(2,1)S(1)}, u32[]{:S(2)}, u32[]{:S(2)}) collective-permute-start(bf16[72,128,128]{2,1,0:T(8,128)(2,1)} %collective-permute-done.5.refs_4_), channel_id=1, source_target_pairs={{8,16},{9,17},{10,18},{11,19},{12,20},{13,21},{14,22},{15,23},{16,... | collective-permute-start | bytes 7077896 | tf_op jit(solution)/shard_map/ppermute | solution.py:227
  84.4 46.5 %collective-permute-start.10 = (bf16[72,128,128]{2,1,0:T(8,128)(2,1)}, bf16[72,128,128]{2,1,0:T(8,128)(2,1)S(1)}, u32[]{:S(2)}, u32[]{:S(2)}) collective-permute-start(bf16[72,128,128]{2,1,0:T(8,128)(2,1)} %collective-permute-done.5.refs_4_), channel_id=1, source_target_pairs={{0,8},{1,9},{2,10},{3,11},{4,12},{5,13},{6,14},{7,15},{8,0},{9,1},... | collective-permute-start | bytes 7077896 | tf_op jit(solution)/shard_map/ppermute | solution.py:227
  84.5 40.9 %collective-permute-start.8 = (bf16[48,128,128]{2,1,0:T(8,128)(2,1)}, bf16[48,128,128]{2,1,0:T(8,128)(2,1)}, u32[]{:S(2)}, u32[]{:S(2)}) collective-permute-start(bf16[48,128,128]{2,1,0:T(8,128)(2,1)} %slice.255), channel_id=1, source_target_pairs={{0,1},{1,0},{2,3},{3,2},{4,5},{5,4},{6,7},{7,6},{8,9},{9,8},{10,11... | collective-permute-start | bytes 4718600 | tf_op jit(solution)/shard_map/ppermute | solution.py:227
  130.8 1.4 copy-start.1
  132.2 3.6 %collective-permute-start.15 = (bf16[48,128,128]{2,1,0:T(8,128)(2,1)}, bf16[48,128,128]{2,1,0:T(8,128)(2,1)S(1)}, u32[]{:S(2)}, u32[]{:S(2)}) collective-permute-start(bf16[48,128,128]{2,1,0:T(8,128)(2,1)} %collective-permute-done.8.refs_5_), channel_id=1, source_target_pairs={{0,8},{1,9},{2,10},{3,11},{4,12},{5,13},{6,14},{7,15},{8,0},{9,1},... | collective-permute-start | bytes 4718600 | tf_op jit(solution)/shard_map/ppermute | solution.py:227
  132.2 48.2 %collective-permute-start.14 = (bf16[120,128,128]{2,1,0:T(8,128)(2,1)}, bf16[120,128,128]{2,1,0:T(8,128)(2,1)}, u32[]{:S(2)}, u32[]{:S(2)}) collective-permute-start(bf16[120,128,128]{2,1,0:T(8,128)(2,1)} %collective-permute-done.3.refs_5_), channel_id=1, source_target_pairs={{0,1},{1,0},{2,3},{3,2},{4,5},{5,4},{6,7},{7,6},{56,57},{57,56},{5... | collective-permute-start | bytes 11796488 | tf_op jit(solution)/shard_map/ppermute | solution.py:227
  135.9 1.2 copy-start.3
  137.1 12.2 %collective-permute-start.16 = (bf16[72,128,128]{2,1,0:T(8,128)(2,1)}, bf16[72,128,128]{2,1,0:T(8,128)(2,1)}, u32[]{:S(2)}, u32[]{:S(2)}) collective-permute-start(bf16[72,128,128]{2,1,0:T(8,128)(2,1)} %collective-permute-done.9.refs_6_), channel_id=1, source_target_pairs={{0,8},{1,9},{2,10},{3,11},{4,12},{5,13},{6,14},{7,15},{8,0},{9,1},... | collective-permute-start | bytes 7077896 | tf_op jit(solution)/shard_map/ppermute | solution.py:227
  137.2 43.3 %collective-permute-start.18 = (bf16[72,128,128]{2,1,0:T(8,128)(2,1)}, bf16[72,128,128]{2,1,0:T(8,128)(2,1)}, u32[]{:S(2)}, u32[]{:S(2)}) collective-permute-start(bf16[72,128,128]{2,1,0:T(8,128)(2,1)} %collective-permute-done.9.refs_6_), channel_id=1, source_target_pairs={{8,16},{9,17},{10,18},{11,19},{12,20},{13,21},{14,22},{15,23},{16,... | collective-permute-start | bytes 7077896 | tf_op jit(solution)/shard_map/ppermute | solution.py:227
  139.3 41.2 %collective-permute-start.13 = (bf16[48,128,128]{2,1,0:T(8,128)(2,1)}, bf16[48,128,128]{2,1,0:T(8,128)(2,1)}, u32[]{:S(2)}, u32[]{:S(2)}) collective-permute-start(bf16[48,128,128]{2,1,0:T(8,128)(2,1)} %collective-permute-done.8.refs_5_), channel_id=1, source_target_pairs={{0,2},{1,7},{2,4},{3,1},{4,6},{5,3},{6,0},{7,5},{8,10},{9,15},{10,... | collective-permute-start | bytes 4718600 | tf_op jit(solution)/shard_map/ppermute | solution.py:227
  139.3 41.2 %collective-permute-start.17 = (bf16[48,128,128]{2,1,0:T(8,128)(2,1)}, bf16[48,128,128]{2,1,0:T(8,128)(2,1)}, u32[]{:S(2)}, u32[]{:S(2)}) collective-permute-start(bf16[48,128,128]{2,1,0:T(8,128)(2,1)} %collective-permute-done.8.refs_5_), channel_id=1, source_target_pairs={{8,16},{9,17},{10,18},{11,19},{12,20},{13,21},{14,22},{15,23},{16,... | collective-permute-start | bytes 4718600 | tf_op jit(solution)/shard_map/ppermute | solution.py:227
  141.9 45.0 %all-to-all-start = ((s32[128,1,2]{2,1,0:T(1,128)}), s32[128,1,2]{2,1,0:T(1,128)S(1)}, u32[]{:S(2)}, u32[]{:S(2)}) async-start(s32[128,1,2]{2,1,0:T(1,128)} %bitcast.83), calls=%async_computation | async-start | bytes 131072 | tf_op jit(solution)/shard_map/all_to_all | solution.py:311
  149.3 1.7 copy-start.2
  150.9 1.4 copy-start.4
  186.9 17.0 %collective-permute-start.20 = (bf16[48,128,128]{2,1,0:T(8,128)(2,1)}, bf16[48,128,128]{2,1,0:T(8,128)(2,1)}, u32[]{:S(2)}, u32[]{:S(2)}) collective-permute-start(bf16[48,128,128]{2,1,0:T(8,128)(2,1)} %collective-permute-done.13.refs_8_), channel_id=1, source_target_pairs={{8,16},{9,17},{10,18},{11,19},{12,20},{13,21},{14,22},{15,23},{16,... | collective-permute-start | bytes 4718600 | tf_op jit(solution)/shard_map/ppermute | solution.py:227
  188.7 15.2 %collective-permute-start.19 = (bf16[48,128,128]{2,1,0:T(8,128)(2,1)}, bf16[48,128,128]{2,1,0:T(8,128)(2,1)}, u32[]{:S(2)}, u32[]{:S(2)}) collective-permute-start(bf16[48,128,128]{2,1,0:T(8,128)(2,1)} %collective-permute-done.13.refs_8_), channel_id=1, source_target_pairs={{0,8},{1,9},{2,10},{3,11},{4,12},{5,13},{6,14},{7,15},{8,0},{9,1},... | collective-permute-start | bytes 4718600 | tf_op jit(solution)/shard_map/ppermute | solution.py:227

commit v3 on v2

--- a/solution.py
+++ b/solution.py
@@ -272,9 +272,9 @@
 
     calls = {
         "core": [("DO", None), ("A", None)],
-        "first": [("X", 0), ("X", 1), ("Z", 0), ("DX", 0), ("DX", 1), ("DZ", 0)],
-        "second": [("B", 0), ("B", 1), ("Z", 1), ("C", 0)],
-        "last": [("C", 1), ("DZ", 1)],
+        "first": [("X", 0), ("X", 1), ("Z", 0), ("DX", 0)],
+        "second": [("B", 0), ("B", 1), ("Z", 1), ("C", 0), ("DZ", 0)],
+        "last": [("C", 1), ("DZ", 1), ("DX", 1)],
     }
 
     def chunk_of(key):
@@ -336,11 +336,18 @@
                 block += stored
         bounds.append(len(first))
     codes = codes_of(after(jnp.concatenate(pats)), jnp.stack(ids), jnp.asarray(first, jnp.int32))
-    for name, lo, hi in zip(calls, bounds[:-1], bounds[1:]):
-        lists[name] = listing(codes[lo:hi])
-
-    for name in calls:
-        lists[name] = tuple(after(x) for x in lists[name])
+    ranges = dict(zip(calls, zip(bounds[:-1], bounds[1:])))
+    got["codes"] = codes
+
+    def make_lists(names):
+        for name in names:
+            lo, hi = ranges[name]
+            lists[name] = listing(got["codes"][lo:hi])
+        for name in names:
+            lists[name] = tuple(after(x) for x in lists[name])
+
+    wait("codes")
+    make_lists(["core"])
     wait(("X", 0))
 
 
@@ -354,21 +361,20 @@
     got["X", 1] = send(got["x1"], "pair")
     got["Z", 0] = send(got["X", 0], "along")
     run("core")
+    make_lists(["first", "second", "last"])
     wait("acc", ("Z", 0), ("X", 1), ("B", 0), "F", ("DX", 0))
+    got["DZ", 0] = send(got["Z", 0], "core")
+    got["V"] = send(got["A", None], "wrap_pair")
+    got["Z", 1] = send(got["X", 1], "along")
+    got["B", 1] = send(got["X", 1], "inner_beside")
+    got["C", 0] = send(got["Z", 0], "inner_beside")
+    run("first")
+    wait("acc", ("C", 0), ("B", 1), ("Z", 1), "V", ("DZ", 0), "ids")
     got["DX", 1] = send(got["X", 1], "core")
-    got["B", 1] = send(got["X", 1], "inner_beside")
-    got["V"] = send(got["A", None], "wrap_pair")
-    got["C", 0] = send(got["Z", 0], "inner_beside")
-    got["Z", 1] = send(got["X", 1], "along")
-    wait(("DX", 1))
-    got["DZ", 0] = send(got["Z", 0], "core")
-    wait(("DZ", 0))
-    run("first")
-    wait("acc", "V", ("Z", 1), ("C", 0), ("B", 1), "ids")
     got["DZ", 1] = send(got["Z", 1], "core")
     got["C", 1] = send(got["Z", 1], "inner_beside")
     run("second")
-    wait("acc", ("C", 1), ("DZ", 1))
+    wait("acc", ("C", 1), ("DZ", 1), ("DX", 1))
     outgoing = finish(
         "last", flag[0], *lists["last"], left, [chunk_of(key) for key in calls["last"]], got["acc"], got["inverse"]
     )

time: 336 us -> 326 us (0.970)
  local copies, waits for them, and re-layouts: 29.8 us -> 22.5 us
  waiting for transfers between devices: 80.9 us -> 74.9 us
  Pallas kernels: 64.7 us -> 68.1 us
    unnamed x17 -> x9, local copies, waits for them, and re-layouts: 19.6 us -> 13.9 us
    all_to_all x1, waiting for transfers between devices: 6.4 us -> 2.31 us  [shards(): lax.all_to_all(after(outgoing_ids).reshape(devices, capacity), AXES, spli...]
  transfers between devices with their start and end apart: 22 -> 22, of which waited for: 7 -> 8; matrix products, arithmetic and copies ran while one was open for 7% -> 6% of each run, Pallas kernels for 16% -> 17%
where the time goes in v3:
time: 326 us; the launch traced here: 325 us
  blocking collectives  107 us (33%)
  waiting for transfers between devices  74.9 us (23%)
  Pallas kernels  68.1 us (21%)
  starting transfers between devices  38.2 us (12%)
  local copies, waits for them, and re-layouts  22.5 us (7%)
  other arithmetic  13.8 us (4%)
    all_to_all x1, blocking collectives, shards(): lax.all_to_all(outgoing.reshape(-1, order), AXES, split_axis=0, concat_ax...  107 us
    ppermute x21, waiting for transfers between devices, send(): return lax.ppermute(after(x), AXES, perms[which])  72.6 us
    pallas_call x4, Pallas kernels, accumulate(): pl.pallas_call(body, out_shape=jax.ShapeDtypeStruct((slots, order, order)...  55.8 us
    ppermute x21, starting transfers between devices, send(): return lax.ppermute(after(x), AXES, perms[which])  31 us
    unnamed x9, local copies, waits for them, and re-layouts  13.9 us
    pallas_call x1, Pallas kernels, finish(): pl.pallas_call(body, out_shape=jax.ShapeDtypeStruct((slots, order, order)...  12.3 us
    all_to_all x1, starting transfers between devices, shards(): lax.all_to_all(after(outgoing_ids).reshape(devices, capacity), AXES, spli...  7.18 us
  transfers between devices with their start and end apart: 22, of which 8 were waited for; matrix products, arithmetic and copies ran while one was open for 6% of the time, Pallas kernels for 17%

profile of v3, /device:TPU:0, one launch (start us, length us, event | category | flops | bytes accessed | tf_op | source)
XLA Modules:
  0.0 325.4 jit_solution(15620835229349501700)
XLA Ops:
  0.8 1.9 slice.252
  2.7 1.7 collective-permute-start
  4.4 4.0 %collective-permute-start.1 = (s32[5,24]{1,0:T(8,128)S(1)}, s32[5,24]{1,0:T(8,128)S(1)}, u32[]{:S(2)}, u32[]{:S(2)}) collective-permute-start(s32[5,24]{1,0:T(8,128)S(1)} %copy-done.1), channel_id=1, source_target_pairs={{0,7},{1,2},{2,1},{3,4},{4,3},{5,6},{6,5},{7,0},{8,15},{9,10},{10,... | collective-permute-start | bytes 1448 | tf_op jit(solution)/shard_map/ppermute | solution.py:227
  8.4 5.3 %collective-permute-start.3 = (bf16[120,128,128]{2,1,0:T(8,128)(2,1)}, bf16[120,128,128]{2,1,0:T(8,128)(2,1)}, u32[]{:S(2)}, u32[]{:S(2)}) collective-permute-start(bf16[120,128,128]{2,1,0:T(8,128)(2,1)} %bitcast.refs_3_.refs_4_), channel_id=1, source_target_pairs={{0,121},{1,120},{2,123},{3,122},{4,125},{5,124},{6,127},{7,126},{8... | collective-permute-start | bytes 11796488 | tf_op jit(solution)/shard_map/ppermute | solution.py:227
  14.3 2.3 collective-permute-start.4
  16.7 2.3 collective-permute-start.7
  19.1 0.6 select_reduce_fusion.6
  19.7 0.7 convert_reduce_fusion.5
  21.5 0.6 fusion.7.refs_2_
  22.5 8.6 %own.1.refs_6_ = f32[128,128,128]{2,1,0:T(8,128)S(1)} custom-call(s32[1]{0:T(128)} %bitcast.3.refs_0_, s32[1]{0:T(128)} %bitcast.6.refs_1_, s32[600]{0:T(1024)S(1)} %fusion.7.refs_2_, bf16[120,128,128]{2,1,0:T(8,128)(2,1)} %bitcast.refs_3_.refs_4_, bf16[120,128,128]{2,1,0:T(8,128)(2,1)} %bitcast.refs_3_.refs_4_), custom_call_target="tpu_custom_call" | custom-call | flops 8589934592 | bytes 33554432 | tf_op jit(solution)/shard_map/own/pallas_call | solution.py:123
  31.1 3.4 %copy-done = f32[128,128,128]{2,1,0:T(8,128)} copy-done((f32[128,128,128]{2,1,0:T(8,128)}, f32[128,128,128]{2,1,0:T(8,128)S(1)}, u32[]{:S(2)}) %copy-start) | copy-done | bytes 8388632
  34.5 2.8 slice.254
  37.3 24.9 %collective-permute-done.4 = bf16[120,128,128]{2,1,0:T(8,128)(2,1)} collective-permute-done((bf16[120,128,128]{2,1,0:T(8,128)(2,1)}, bf16[120,128,128]{2,1,0:T(8,128)(2,1)}, u32[]{:S(2)}, u32[]{:S(2)}) %collective-permute-start.4) | collective-permute-done | bytes 3932192 | tf_op jit(solution)/shard_map/ppermute | solution.py:227
  62.2 2.7 collective-permute-done.7
  65.3 0.5 select_reduce_fusion.5
  65.8 0.7 convert_reduce_fusion.3
  67.3 0.7 select_reduce_fusion.2
  68.0 0.6 fusion.4.refs_2_
  68.7 0.7 convert_reduce_fusion.2
  69.4 0.7 convert_reduce_fusion.1
  70.1 0.7 convert_reduce_fusion
  72.6 0.8 collective-permute-start.12
  73.5 2.7 collective-permute-start.11
  76.4 0.9 select_reduce_fusion.1
  77.3 0.7 fusion.6.refs_2_
  78.4 1.1 select_reduce_fusion
  79.6 0.6 fusion.5.refs_2_
  80.8 0.6 fusion.8.refs_2_
  81.4 14.9 %core.1.refs_8_ = f32[128,128,128]{2,1,0:T(8,128)} custom-call(s32[1]{0:T(128)} %bitcast.3.refs_0_, s32[1]{0:T(128)} %bitcast.74.refs_1_, s32[1200]{0:T(1024)S(1)} %fusion.4.refs_2_, bf16[120,128,128]{2,1,0:T(8,128)(2,1)} %bitcast.refs_3_.refs_4_, bf16[120,128,128]{2,1,0:T(8,128)(2,1)} %collective-permute-done.2.refs_4_, ...), custom_call_target="tpu_custom_call", output_to_operand_aliasing={{}: (6, {})} | custom-call | flops 8589934592 | bytes 33554432 | tf_op jit(solution)/shard_map/core/pallas_call | solution.py:123
  96.3 20.5 %collective-permute-done.9.refs_6_ = bf16[72,128,128]{2,1,0:T(8,128)(2,1)} collective-permute-done((bf16[72,128,128]{2,1,0:T(8,128)(2,1)}, bf16[72,128,128]{2,1,0:T(8,128)(2,1)}, u32[]{:S(2)}, u32[]{:S(2)}) %collective-permute-start.9) | collective-permute-done | bytes 2359328 | tf_op jit(solution)/shard_map/ppermute | solution.py:227
  117.3 6.9 %collective-permute-done.11.refs_9_.refs_5_ = bf16[120,128,128]{2,1,0:T(8,128)(2,1)} collective-permute-done((bf16[120,128,128]{2,1,0:T(8,128)(2,1)}, bf16[120,128,128]{2,1,0:T(8,128)(2,1)}, u32[]{:S(2)}, u32[]{:S(2)}) %collective-permute-start.11) | collective-permute-done | bytes 3932192 | tf_op jit(solution)/shard_map/ppermute | solution.py:227
  124.2 1.9 collective-permute-start.14
  126.1 2.1 collective-permute-start.17
  128.2 1.9 collective-permute-start.16
  130.1 1.6 collective-permute-start.15
  131.7 0.8 all_to_all.14
  132.5 7.2 %all-to-all-start = ((s32[128,1,2]{2,1,0:T(1,128)}), s32[128,1,2]{2,1,0:T(1,128)S(1)}, u32[]{:S(2)}, u32[]{:S(2)}) async-start(s32[128,1,2]{2,1,0:T(1,128)} %bitcast.84), calls=%async_computation | async-start | bytes 131072 | tf_op jit(solution)/shard_map/all_to_all | solution.py:311
  139.6 15.6 %first.1.refs_12_ = f32[128,128,128]{2,1,0:T(8,128)} custom-call(s32[1]{0:T(128)} %bitcast.3.refs_0_, s32[1]{0:T(128)} %bitcast.83.refs_1_, s32[1320]{0:T(1024)S(1)} %fusion.6.refs_2_, bf16[120,128,128]{2,1,0:T(8,128)(2,1)} %bitcast.refs_3_.refs_4_, bf16[72,128,128]{2,1,0:T(8,128)(2,1)} %collective-permute-done.5.refs_4_, ...), custom_call_target="tpu_custom_call", output_to_operand_aliasing={{}: (8, {})} | custom-call | flops 8589934592 | bytes 33554432 | tf_op jit(solution)/shard_map/first/pallas_call | solution.py:123
  155.2 13.8 %collective-permute-done.15.refs_8_ = bf16[48,128,128]{2,1,0:T(8,128)(2,1)} collective-permute-done((bf16[48,128,128]{2,1,0:T(8,128)(2,1)}, bf16[48,128,128]{2,1,0:T(8,128)(2,1)}, u32[]{:S(2)}, u32[]{:S(2)}) %collective-permute-start.15) | collective-permute-done | bytes 1572896 | tf_op jit(solution)/shard_map/ppermute | solution.py:227
  169.0 3.4 %collective-permute-done.14.refs_4_.refs_6_ = bf16[120,128,128]{2,1,0:T(8,128)(2,1)} collective-permute-done((bf16[120,128,128]{2,1,0:T(8,128)(2,1)}, bf16[120,128,128]{2,1,0:T(8,128)(2,1)}, u32[]{:S(2)}, u32[]{:S(2)}) %collective-permute-start.14) | collective-permute-done | bytes 3932192 | tf_op jit(solution)/shard_map/ppermute | solution.py:227
  172.4 2.3 all-to-all-done
  174.7 1.8 collective-permute-start.20
  176.5 1.8 collective-permute-start.19
  178.5 0.7 reshape.356
  179.2 16.7 %second.1.refs_9_ = f32[128,128,128]{2,1,0:T(8,128)} custom-call(s32[1]{0:T(128)} %bitcast.3.refs_0_, s32[1]{0:T(128)} %bitcast.80.refs_1_, s32[1560]{0:T(1024)S(1)} %fusion.5.refs_2_, bf16[120,128,128]{2,1,0:T(8,128)(2,1)} %bitcast.refs_3_.refs_4_, bf16[120,128,128]{2,1,0:T(8,128)(2,1)} %collective-permute-done.14.refs_4_.refs_6_, ...), custom_call_target="tpu_custom_call", output_to_operand_aliasing={{}: (12, {})} | custom-call | flops 8589934592 | bytes 33554432 | tf_op jit(solution)/shard_map/second/pallas_call | solution.py:123
  196.0 12.3 %last.1 = bf16[256,128,128]{2,1,0:T(8,128)(2,1)} custom-call(s32[1]{0:T(128)} %bitcast.3.refs_0_, s32[1]{0:T(128)} %bitcast.77.refs_1_, s32[720]{0:T(1024)S(1)} %fusion.8.refs_2_, s32[256]{0:T(256)S(1)} %get-tuple-element.254.refs_3_, bf16[120,128,128]{2,1,0:T(8,128)(2,1)} %bitcast.refs_3_.refs_4_, ...), custom_call_target="tpu_custom_call" | custom-call | bytes 262144 | tf_op jit(solution)/shard_map/last/pallas_call | solution.py:184
  208.2 106.6 %all_to_all.21 = bf16[128,256,128]{2,1,0:T(8,128)(2,1)} all-to-all(bf16[128,256,128]{2,1,0:T(8,128)(2,1)} %bitcast.124), channel_id=1, replica_groups=mesh['row'=16,'col'=8] {'row','col'}, dimensions={0} | all-to-all | bytes 16777216 | tf_op jit(solution)/shard_map/all_to_all | solution.py:383
  314.8 10.5 %copy.29 = bf16[256,128,128]{2,1,0:T(8,128)(2,1)} copy(bf16[256,128,128]{2,1,0:T(8,128)(2,1)} %bitcast.123) | data formatting | bytes 16777216
  (108 shorter events, 7.1 us)
Async XLA Ops:
  0.6 2.1 copy-start.1
  0.7 16.0 %copy-start.2 = (s32[40]{0:T(128)S(1)}, s32[40]{0:T(128)}, u32[]{:S(2)}) copy-start(s32[40]{0:T(128)} %constant.118.clone) | copy-start | bytes 484
  0.7 21.5 %copy-start.3 = (s32[120,1]{0,1:T(1,128)S(1)}, s32[120,1]{0,1:T(1,128)}, u32[]{:S(2)}) copy-start(s32[120,1]{0,1:T(1,128)} %param.6) | copy-start | bytes 1444
  0.7 13.6 %collective-permute-start.2 = (bf16[120,128,128]{2,1,0:T(8,128)(2,1)}, bf16[120,128,128]{2,1,0:T(8,128)(2,1)}, u32[]{:S(2)}, u32[]{:S(2)}) collective-permute-start(bf16[120,128,128]{2,1,0:T(8,128)(2,1)} %bitcast.refs_3_.refs_4_), channel_id=1, source_target_pairs={{0,8},{1,9},{2,10},{3,11},{4,12},{5,13},{6,14},{7,15},{8,0},{9,1},... | collective-permute-start | bytes 11796488 | tf_op jit(solution)/shard_map/ppermute | solution.py:227
  2.7 11.5 %collective-permute-start = (s32[5,24]{1,0:T(8,128)S(1)}, s32[5,24]{1,0:T(8,128)S(1)}, u32[]{:S(2)}, u32[]{:S(2)}) collective-permute-start(s32[5,24]{1,0:T(8,128)S(1)} %copy-done.1), channel_id=1, source_target_pairs={{0,1},{1,0},{2,3},{3,2},{4,5},{5,4},{6,7},{7,6},{8,9},{9,8},{10,11... | collective-permute-start | bytes 1448 | tf_op jit(solution)/shard_map/ppermute | solution.py:227
  4.4 9.9 %collective-permute-start.1 = (s32[5,24]{1,0:T(8,128)S(1)}, s32[5,24]{1,0:T(8,128)S(1)}, u32[]{:S(2)}, u32[]{:S(2)}) collective-permute-start(s32[5,24]{1,0:T(8,128)S(1)} %copy-done.1), channel_id=1, source_target_pairs={{0,7},{1,2},{2,1},{3,4},{4,3},{5,6},{6,5},{7,0},{8,15},{9,10},{10,... | collective-permute-start | bytes 1448 | tf_op jit(solution)/shard_map/ppermute | solution.py:227
  8.4 62.4 %collective-permute-start.5 = (bf16[72,128,128]{2,1,0:T(8,128)(2,1)S(1)}, bf16[72,128,128]{2,1,0:T(8,128)(2,1)}, u32[]{:S(2)}, u32[]{:S(2)}) collective-permute-start(bf16[72,128,128]{2,1,0:T(8,128)(2,1)S(1)} %bitcast.125), channel_id=1, source_target_pairs={{0,1},{1,0},{2,3},{3,2},{4,5},{5,4},{6,7},{7,6},{8,9},{9,8},{10,11... | collective-permute-start | bytes 7077896 | tf_op jit(solution)/shard_map/ppermute | solution.py:227
  8.4 53.8 %collective-permute-start.3 = (bf16[120,128,128]{2,1,0:T(8,128)(2,1)}, bf16[120,128,128]{2,1,0:T(8,128)(2,1)}, u32[]{:S(2)}, u32[]{:S(2)}) collective-permute-start(bf16[120,128,128]{2,1,0:T(8,128)(2,1)} %bitcast.refs_3_.refs_4_), channel_id=1, source_target_pairs={{0,121},{1,120},{2,123},{3,122},{4,125},{5,124},{6,127},{7,126},{8... | collective-permute-start | bytes 11796488 | tf_op jit(solution)/shard_map/ppermute | solution.py:227
  14.3 47.9 %collective-permute-start.4 = (bf16[120,128,128]{2,1,0:T(8,128)(2,1)}, bf16[120,128,128]{2,1,0:T(8,128)(2,1)}, u32[]{:S(2)}, u32[]{:S(2)}) collective-permute-start(bf16[120,128,128]{2,1,0:T(8,128)(2,1)} %bitcast.refs_3_.refs_4_), channel_id=1, source_target_pairs={{0,6},{1,3},{2,0},{3,5},{4,2},{5,7},{6,4},{7,1},{56,62},{57,59},{5... | collective-permute-start | bytes 11796488 | tf_op jit(solution)/shard_map/ppermute | solution.py:227
  16.7 48.1 %collective-permute-start.7 = (s32[3,5,24]{2,1,0:T(8,128)S(1)}, s32[3,5,24]{2,1,0:T(8,128)S(1)}, u32[]{:S(2)}, u32[]{:S(2)}) collective-permute-start(s32[3,5,24]{2,1,0:T(8,128)S(1)} %pad_add_fusion), channel_id=1, source_target_pairs={{0,120},{1,121},{2,122},{3,123},{4,124},{5,125},{6,126},{7,127},{8... | collective-permute-start | bytes 4328 | tf_op jit(solution)/shard_map/ppermute | solution.py:227
  19.1 43.1 %collective-permute-start.6 = (s32[3,5,24]{2,1,0:T(8,128)S(1)}, s32[3,5,24]{2,1,0:T(8,128)S(1)}, u32[]{:S(2)}, u32[]{:S(2)}) collective-permute-start(s32[3,5,24]{2,1,0:T(8,128)S(1)} %pad_add_fusion), channel_id=1, source_target_pairs={{0,8},{1,9},{2,10},{3,11},{4,12},{5,13},{6,14},{7,15},{8,0},{9,1},... | collective-permute-start | bytes 4328 | tf_op jit(solution)/shard_map/ppermute | solution.py:227
  31.1 3.4 %copy-start = (f32[128,128,128]{2,1,0:T(8,128)}, f32[128,128,128]{2,1,0:T(8,128)S(1)}, u32[]{:S(2)}) copy-start(f32[128,128,128]{2,1,0:T(8,128)S(1)} %own.1.refs_6_) | copy-start | bytes 25165828
  72.3 44.6 %collective-permute-start.9 = (bf16[72,128,128]{2,1,0:T(8,128)(2,1)}, bf16[72,128,128]{2,1,0:T(8,128)(2,1)}, u32[]{:S(2)}, u32[]{:S(2)}) collective-permute-start(bf16[72,128,128]{2,1,0:T(8,128)(2,1)} %collective-permute-done.5.refs_4_), channel_id=1, source_target_pairs={{0,2},{1,7},{2,4},{3,1},{4,6},{5,3},{6,0},{7,5},{8,10},{9,15},{10,... | collective-permute-start | bytes 7077896 | tf_op jit(solution)/shard_map/ppermute | solution.py:227
  72.6 44.7 %collective-permute-start.12 = (bf16[72,128,128]{2,1,0:T(8,128)(2,1)}, bf16[72,128,128]{2,1,0:T(8,128)(2,1)S(1)}, u32[]{:S(2)}, u32[]{:S(2)}) collective-permute-start(bf16[72,128,128]{2,1,0:T(8,128)(2,1)} %collective-permute-done.5.refs_4_), channel_id=1, source_target_pairs={{8,16},{9,17},{10,18},{11,19},{12,20},{13,21},{14,22},{15,23},{16,... | collective-permute-start | bytes 7077896 | tf_op jit(solution)/shard_map/ppermute | solution.py:227
  73.4 50.7 %collective-permute-start.10 = (bf16[72,128,128]{2,1,0:T(8,128)(2,1)}, bf16[72,128,128]{2,1,0:T(8,128)(2,1)}, u32[]{:S(2)}, u32[]{:S(2)}) collective-permute-start(bf16[72,128,128]{2,1,0:T(8,128)(2,1)} %collective-permute-done.5.refs_4_), channel_id=1, source_target_pairs={{0,8},{1,9},{2,10},{3,11},{4,12},{5,13},{6,14},{7,15},{8,0},{9,1},... | collective-permute-start | bytes 7077896 | tf_op jit(solution)/shard_map/ppermute | solution.py:227
  73.5 50.7 %collective-permute-start.11 = (bf16[120,128,128]{2,1,0:T(8,128)(2,1)}, bf16[120,128,128]{2,1,0:T(8,128)(2,1)}, u32[]{:S(2)}, u32[]{:S(2)}) collective-permute-start(bf16[120,128,128]{2,1,0:T(8,128)(2,1)} %collective-permute-done.4), channel_id=1, source_target_pairs={{0,121},{1,120},{2,123},{3,122},{4,125},{5,124},{6,127},{7,126},{5... | collective-permute-start | bytes 11796488 | tf_op jit(solution)/shard_map/ppermute | solution.py:227
  80.2 37.1 %collective-permute-start.8 = (bf16[48,128,128]{2,1,0:T(8,128)(2,1)}, bf16[48,128,128]{2,1,0:T(8,128)(2,1)}, u32[]{:S(2)}, u32[]{:S(2)}) collective-permute-start(bf16[48,128,128]{2,1,0:T(8,128)(2,1)} %slice.254), channel_id=1, source_target_pairs={{0,1},{1,0},{2,3},{3,2},{4,5},{5,4},{6,7},{7,6},{8,9},{9,8},{10,11... | collective-permute-start | bytes 4718600 | tf_op jit(solution)/shard_map/ppermute | solution.py:227
  124.2 48.2 %collective-permute-start.14 = (bf16[120,128,128]{2,1,0:T(8,128)(2,1)}, bf16[120,128,128]{2,1,0:T(8,128)(2,1)}, u32[]{:S(2)}, u32[]{:S(2)}) collective-permute-start(bf16[120,128,128]{2,1,0:T(8,128)(2,1)} %collective-permute-done.3.refs_5_), channel_id=1, source_target_pairs={{0,1},{1,0},{2,3},{3,2},{4,5},{5,4},{6,7},{7,6},{56,57},{57,56},{5... | collective-permute-start | bytes 11796488 | tf_op jit(solution)/shard_map/ppermute | solution.py:227
  126.1 29.1 %collective-permute-start.17 = (bf16[72,128,128]{2,1,0:T(8,128)(2,1)}, bf16[72,128,128]{2,1,0:T(8,128)(2,1)}, u32[]{:S(2)}, u32[]{:S(2)}) collective-permute-start(bf16[72,128,128]{2,1,0:T(8,128)(2,1)} %collective-permute-done.9.refs_6_), channel_id=1, source_target_pairs={{8,16},{9,17},{10,18},{11,19},{12,20},{13,21},{14,22},{15,23},{16,... | collective-permute-start | bytes 7077896 | tf_op jit(solution)/shard_map/ppermute | solution.py:227
  128.2 44.3 %collective-permute-start.13 = (bf16[72,128,128]{2,1,0:T(8,128)(2,1)}, bf16[72,128,128]{2,1,0:T(8,128)(2,1)}, u32[]{:S(2)}, u32[]{:S(2)}) collective-permute-start(bf16[72,128,128]{2,1,0:T(8,128)(2,1)} %collective-permute-done.9.refs_6_), channel_id=1, source_target_pairs={{0,8},{1,9},{2,10},{3,11},{4,12},{5,13},{6,14},{7,15},{8,0},{9,1},... | collective-permute-start | bytes 7077896 | tf_op jit(solution)/shard_map/ppermute | solution.py:227
  128.2 27.0 %collective-permute-start.16 = (bf16[48,128,128]{2,1,0:T(8,128)(2,1)}, bf16[48,128,128]{2,1,0:T(8,128)(2,1)}, u32[]{:S(2)}, u32[]{:S(2)}) collective-permute-start(bf16[48,128,128]{2,1,0:T(8,128)(2,1)} %collective-permute-done.8.refs_5_), channel_id=1, source_target_pairs={{8,16},{9,17},{10,18},{11,19},{12,20},{13,21},{14,22},{15,23},{16,... | collective-permute-start | bytes 4718600 | tf_op jit(solution)/shard_map/ppermute | solution.py:227
  130.1 39.0 %collective-permute-start.15 = (bf16[48,128,128]{2,1,0:T(8,128)(2,1)}, bf16[48,128,128]{2,1,0:T(8,128)(2,1)}, u32[]{:S(2)}, u32[]{:S(2)}) collective-permute-start(bf16[48,128,128]{2,1,0:T(8,128)(2,1)} %collective-permute-done.8.refs_5_), channel_id=1, source_target_pairs={{0,2},{1,7},{2,4},{3,1},{4,6},{5,3},{6,0},{7,5},{8,10},{9,15},{10,... | collective-permute-start | bytes 4718600 | tf_op jit(solution)/shard_map/ppermute | solution.py:227
  132.5 42.3 %all-to-all-start = ((s32[128,1,2]{2,1,0:T(1,128)}), s32[128,1,2]{2,1,0:T(1,128)S(1)}, u32[]{:S(2)}, u32[]{:S(2)}) async-start(s32[128,1,2]{2,1,0:T(1,128)} %bitcast.84), calls=%async_computation | async-start | bytes 131072 | tf_op jit(solution)/shard_map/all_to_all | solution.py:311
  174.7 21.2 %collective-permute-start.20 = (bf16[48,128,128]{2,1,0:T(8,128)(2,1)}, bf16[48,128,128]{2,1,0:T(8,128)(2,1)}, u32[]{:S(2)}, u32[]{:S(2)}) collective-permute-start(bf16[48,128,128]{2,1,0:T(8,128)(2,1)} %collective-permute-done.15.refs_8_), channel_id=1, source_target_pairs={{8,16},{9,17},{10,18},{11,19},{12,20},{13,21},{14,22},{15,23},{16,... | collective-permute-start | bytes 4718600 | tf_op jit(solution)/shard_map/ppermute | solution.py:227
  176.5 19.4 %collective-permute-start.19 = (bf16[48,128,128]{2,1,0:T(8,128)(2,1)}, bf16[48,128,128]{2,1,0:T(8,128)(2,1)}, u32[]{:S(2)}, u32[]{:S(2)}) collective-permute-start(bf16[48,128,128]{2,1,0:T(8,128)(2,1)} %collective-permute-done.15.refs_8_), channel_id=1, source_target_pairs={{0,8},{1,9},{2,10},{3,11},{4,12},{5,13},{6,14},{7,15},{8,0},{9,1},... | collective-permute-start | bytes 4718600 | tf_op jit(solution)/shard_map/ppermute | solution.py:227
  178.4 17.6 %collective-permute-start.18 = (bf16[48,128,128]{2,1,0:T(8,128)(2,1)}, bf16[48,128,128]{2,1,0:T(8,128)(2,1)}, u32[]{:S(2)}, u32[]{:S(2)}) collective-permute-start(bf16[48,128,128]{2,1,0:T(8,128)(2,1)} %collective-permute-done.8.refs_5_), channel_id=1, source_target_pairs={{0,8},{1,9},{2,10},{3,11},{4,12},{5,13},{6,14},{7,15},{8,0},{9,1},... | collective-permute-start | bytes 4718600 | tf_op jit(solution)/shard_map/ppermute | solution.py:227

commit v4 on v3

--- a/solution.py
+++ b/solution.py
@@ -132,7 +132,7 @@
             pltpu.SemaphoreType.DMA((n + 2,)),
         ],
         input_output_aliases={} if fresh else {4 + n: 0},
-        compiler_params=pltpu.CompilerParams(vmem_limit_bytes=36 << 20),
+        compiler_params=pltpu.CompilerParams(vmem_limit_bytes=58 << 20),
         cost_estimate=pl.CostEstimate(flops=8 << 30, bytes_accessed=32 << 20, transcendentals=0),
         name=name,
     )(*args)
@@ -194,10 +194,44 @@
             pltpu.SemaphoreType.DMA((n + 2,)),
             pltpu.SemaphoreType.DMA((slots // part,)),
         ],
-        compiler_params=pltpu.CompilerParams(vmem_limit_bytes=40 << 20),
+        compiler_params=pltpu.CompilerParams(vmem_limit_bytes=58 << 20),
         cost_estimate=pl.CostEstimate(flops=0, bytes_accessed=1 << 18, transcendentals=0),
         name=name,
     )(flag, count, entries, inverse, left, *arrays, acc)
+
+
+def copied(x):
+    pieces = 16
+    size = x.shape[0] // pieces
+
+    def body(x_ref, out, held, in_sems, out_sems):
+        def part(p):
+            return pl.ds(p * size, size)
+
+        ins = [pltpu.make_async_copy(x_ref.at[part(p)], held.at[part(p)], in_sems.at[p]) for p in range(pieces)]
+        outs = [pltpu.make_async_copy(held.at[part(p)], out.at[part(p)], out_sems.at[p]) for p in range(pieces)]
+        for copy in ins:
+            copy.start()
+        for copy, onward in zip(ins, outs):
+            copy.wait()
+            onward.start()
+        for onward in outs:
+            onward.wait()
+
+    anywhere = pl.BlockSpec(memory_space=pl.ANY)
+    return pl.pallas_call(
+        body,
+        out_shape=jax.ShapeDtypeStruct(x.shape, x.dtype),
+        in_specs=[anywhere],
+        out_specs=anywhere,
+        scratch_shapes=[
+            pltpu.VMEM(x.shape, x.dtype),
+            pltpu.SemaphoreType.DMA((pieces,)),
+            pltpu.SemaphoreType.DMA((pieces,)),
+        ],
+        compiler_params=pltpu.CompilerParams(vmem_limit_bytes=20 << 20),
+        name="copied",
+    )(x)
 
 
 def shards(blocks, pattern, owner):
@@ -348,7 +382,7 @@
 
     wait("codes")
     make_lists(["core"])
-    wait(("X", 0))
+    wait("ids", ("X", 0))
 
 
     def run(name):
@@ -369,7 +403,7 @@
     got["B", 1] = send(got["X", 1], "inner_beside")
     got["C", 0] = send(got["Z", 0], "inner_beside")
     run("first")
-    wait("acc", ("C", 0), ("B", 1), ("Z", 1), "V", ("DZ", 0), "ids")
+    wait("acc", ("C", 0), ("B", 1), ("Z", 1), "V", ("DZ", 0))
     got["DX", 1] = send(got["X", 1], "core")
     got["DZ", 1] = send(got["Z", 1], "core")
     got["C", 1] = send(got["Z", 1], "inner_beside")
@@ -381,7 +415,7 @@
     arrived_ids = got["ids"].reshape(devices * capacity)
     outgoing, arrived_ids = lax.optimization_barrier((outgoing, arrived_ids))
     arrived = lax.all_to_all(outgoing.reshape(-1, order), AXES, split_axis=0, concat_axis=0, tiled=True)
-    arrived = arrived.reshape(outgoing.shape)
+    arrived = copied(arrived.reshape(outgoing.shape))
     return arrived, arrived_ids
 
 

time: 326 us -> 320 us (0.982)
  local copies, waits for them, and re-layouts: 22.5 us -> 12.2 us
  Pallas kernels: 68.1 us -> 74.7 us
  waiting for transfers between devices: 74.9 us -> 69.8 us
  other arithmetic: 13.8 us -> 17.2 us
    unnamed x9 -> x14, local copies, waits for them, and re-layouts: 13.9 us -> 3.8 us
    pallas_call x0 -> x1, Pallas kernels: none -> 4.13 us  [copied(): pl.pallas_call(body, out_shape=jax.ShapeDtypeStruct(x.shape, x.dtype), in...]
  transfers between devices with their start and end apart: 22 -> 22, of which waited for: 8 -> 5; matrix products, arithmetic and copies ran while one was open for 6% -> 7% of each run, Pallas kernels for 17% -> 18%
where the time goes in v4:
time: 320 us; the launch traced here: 319 us
  blocking collectives  104 us (32%)
  Pallas kernels  74.7 us (23%)
  waiting for transfers between devices  69.8 us (22%)
  starting transfers between devices  40 us (12%)
  other arithmetic  17.2 us (5%)
  local copies, waits for them, and re-layouts  12.2 us (4%)
    all_to_all x1, blocking collectives, shards(): lax.all_to_all(outgoing.reshape(-1, order), AXES, split_axis=0, concat_ax...  104 us
    ppermute x21, waiting for transfers between devices, send(): return lax.ppermute(after(x), AXES, perms[which])  69.8 us
    pallas_call x4, Pallas kernels, accumulate(): pl.pallas_call(body, out_shape=jax.ShapeDtypeStruct((slots, order, order)...  57.9 us
    ppermute x21, starting transfers between devices, send(): return lax.ppermute(after(x), AXES, perms[which])  33.6 us
    pallas_call x1, Pallas kernels, finish(): pl.pallas_call(body, out_shape=jax.ShapeDtypeStruct((slots, order, order)...  12.6 us
  transfers between devices with their start and end apart: 22, of which 5 were waited for; matrix products, arithmetic and copies ran while one was open for 7% of the time, Pallas kernels for 18%

profile of v4, /device:TPU:0, one launch (start us, length us, event | category | flops | bytes accessed | tf_op | source)
XLA Modules:
  0.0 319.1 jit_solution(16208239095921082144)
XLA Ops:
  0.8 1.8 slice.252
  2.6 1.7 collective-permute-start
  4.3 4.0 %collective-permute-start.1 = (s32[5,24]{1,0:T(8,128)S(1)}, s32[5,24]{1,0:T(8,128)S(1)}, u32[]{:S(2)}, u32[]{:S(2)}) collective-permute-start(s32[5,24]{1,0:T(8,128)S(1)} %copy-done.3), channel_id=1, source_target_pairs={{0,7},{1,2},{2,1},{3,4},{4,3},{5,6},{6,5},{7,0},{8,15},{9,10},{10,... | collective-permute-start | bytes 1448 | tf_op jit(solution)/shard_map/ppermute | solution.py:261
  8.3 5.3 %collective-permute-start.3 = (bf16[120,128,128]{2,1,0:T(8,128)(2,1)}, bf16[120,128,128]{2,1,0:T(8,128)(2,1)}, u32[]{:S(2)}, u32[]{:S(2)}) collective-permute-start(bf16[120,128,128]{2,1,0:T(8,128)(2,1)} %bitcast.refs_3_.refs_4_), channel_id=1, source_target_pairs={{0,121},{1,120},{2,123},{3,122},{4,125},{5,124},{6,127},{7,126},{8... | collective-permute-start | bytes 11796488 | tf_op jit(solution)/shard_map/ppermute | solution.py:261
  14.1 2.3 collective-permute-start.4
  16.6 2.5 collective-permute-start.7
  19.1 0.6 select_reduce_fusion.6
  19.7 0.7 convert_reduce_fusion.5
  21.5 1.2 fusion.7.refs_2_
  23.1 0.5 broadcast_add_fusion
  23.6 0.8 all_to_all.14
  24.4 6.4 %all-to-all-start = ((s32[128,1,2]{2,1,0:T(1,128)}), s32[128,1,2]{2,1,0:T(1,128)S(1)}, u32[]{:S(2)}, u32[]{:S(2)}) async-start(s32[128,1,2]{2,1,0:T(1,128)} %bitcast.10), calls=%async_computation | async-start | bytes 131072 | tf_op jit(solution)/shard_map/all_to_all | solution.py:345
  30.8 11.5 %own.1.refs_6_ = f32[128,128,128]{2,1,0:T(8,128)} custom-call(s32[1]{0:T(128)} %bitcast.3.refs_0_, s32[1]{0:T(128)} %bitcast.6.refs_1_, s32[600]{0:T(1024)} %fusion.7.refs_2_, bf16[120,128,128]{2,1,0:T(8,128)(2,1)} %bitcast.refs_3_.refs_4_, bf16[120,128,128]{2,1,0:T(8,128)(2,1)} %bitcast.refs_3_.refs_4_), custom_call_target="tpu_custom_call" | custom-call | flops 8589934592 | bytes 33554432 | tf_op jit(solution)/shard_map/own/pallas_call | solution.py:123
  42.3 2.7 slice.254
  45.0 17.5 %collective-permute-done.4 = bf16[120,128,128]{2,1,0:T(8,128)(2,1)} collective-permute-done((bf16[120,128,128]{2,1,0:T(8,128)(2,1)}, bf16[120,128,128]{2,1,0:T(8,128)(2,1)}, u32[]{:S(2)}, u32[]{:S(2)}) %collective-permute-start.4) | collective-permute-done | bytes 3932192 | tf_op jit(solution)/shard_map/ppermute | solution.py:261
  62.5 2.2 collective-permute-done.7
  65.7 0.7 convert_reduce_fusion.3
  67.1 0.7 select_reduce_fusion.2
  67.9 1.2 fusion.4.refs_2_
  69.1 0.7 convert_reduce_fusion.2
  69.8 0.7 convert_reduce_fusion.1
  70.5 0.7 convert_reduce_fusion
  73.0 0.8 collective-permute-start.12
  74.3 3.8 %collective-permute-start.11 = (bf16[120,128,128]{2,1,0:T(8,128)(2,1)}, bf16[120,128,128]{2,1,0:T(8,128)(2,1)}, u32[]{:S(2)}, u32[]{:S(2)}) collective-permute-start(bf16[120,128,128]{2,1,0:T(8,128)(2,1)} %collective-permute-done.4), channel_id=1, source_target_pairs={{0,121},{1,120},{2,123},{3,122},{4,125},{5,124},{6,127},{7,126},{5... | collective-permute-start | bytes 11796488 | tf_op jit(solution)/shard_map/ppermute | solution.py:261
  78.3 0.9 select_reduce_fusion.1
  79.1 1.2 fusion.6.refs_2_
  80.8 1.1 select_reduce_fusion
  82.0 1.1 fusion.5.refs_2_
  83.7 1.1 fusion.8.refs_2_
  84.8 14.7 %core.1.refs_8_ = f32[128,128,128]{2,1,0:T(8,128)} custom-call(s32[1]{0:T(128)} %bitcast.3.refs_0_, s32[1]{0:T(128)} %bitcast.76.refs_1_, s32[1200]{0:T(1024)} %fusion.4.refs_2_, bf16[120,128,128]{2,1,0:T(8,128)(2,1)} %bitcast.refs_3_.refs_4_, bf16[120,128,128]{2,1,0:T(8,128)(2,1)} %collective-permute-done.2.refs_4_, ...), custom_call_target="tpu_custom_call", output_to_operand_aliasing={{}: (6, {})} | custom-call | flops 8589934592 | bytes 33554432 | tf_op jit(solution)/shard_map/core/pallas_call | solution.py:123
  99.5 26.3 %collective-permute-done.9.refs_6_ = bf16[72,128,128]{2,1,0:T(8,128)(2,1)} collective-permute-done((bf16[72,128,128]{2,1,0:T(8,128)(2,1)}, bf16[72,128,128]{2,1,0:T(8,128)(2,1)}, u32[]{:S(2)}, u32[]{:S(2)}) %collective-permute-start.9) | collective-permute-done | bytes 2359328 | tf_op jit(solution)/shard_map/ppermute | solution.py:261
  125.8 1.2 copy-done.6
  126.9 1.9 collective-permute-start.14
  128.9 0.8 collective-permute-start.17
  129.7 2.7 collective-permute-start.13
  132.4 1.9 collective-permute-start.16
  134.3 15.3 %first.1.refs_12_ = f32[128,128,128]{2,1,0:T(8,128)} custom-call(s32[1]{0:T(128)} %bitcast.3.refs_0_, s32[1]{0:T(128)} %bitcast.85.refs_1_, s32[1320]{0:T(1024)} %fusion.6.refs_2_, bf16[120,128,128]{2,1,0:T(8,128)(2,1)} %bitcast.refs_3_.refs_4_, bf16[72,128,128]{2,1,0:T(8,128)(2,1)} %collective-permute-done.5.refs_4_, ...), custom_call_target="tpu_custom_call", output_to_operand_aliasing={{}: (8, {})} | custom-call | flops 8589934592 | bytes 33554432 | tf_op jit(solution)/shard_map/first/pallas_call | solution.py:123
  149.6 1.4 copy-done.1
  151.0 21.9 %collective-permute-done.15.refs_8_ = bf16[48,128,128]{2,1,0:T(8,128)(2,1)} collective-permute-done((bf16[48,128,128]{2,1,0:T(8,128)(2,1)}, bf16[48,128,128]{2,1,0:T(8,128)(2,1)}, u32[]{:S(2)}, u32[]{:S(2)}) %collective-permute-start.15) | collective-permute-done | bytes 1572896 | tf_op jit(solution)/shard_map/ppermute | solution.py:261
  173.0 1.9 collective-permute-done.14.refs_4_.refs_6_
  174.8 0.8 collective-permute-start.20
  175.6 4.1 %collective-permute-start.19 = (bf16[48,128,128]{2,1,0:T(8,128)(2,1)}, bf16[48,128,128]{2,1,0:T(8,128)(2,1)}, u32[]{:S(2)}, u32[]{:S(2)}) collective-permute-start(bf16[48,128,128]{2,1,0:T(8,128)(2,1)} %collective-permute-done.15.refs_8_), channel_id=1, source_target_pairs={{0,8},{1,9},{2,10},{3,11},{4,12},{5,13},{6,14},{7,15},{8,0},{9,1},... | collective-permute-start | bytes 4718600 | tf_op jit(solution)/shard_map/ppermute | solution.py:261
  179.8 0.7 reshape.356
  180.5 16.5 %second.1.refs_9_ = f32[128,128,128]{2,1,0:T(8,128)} custom-call(s32[1]{0:T(128)} %bitcast.3.refs_0_, s32[1]{0:T(128)} %bitcast.82.refs_1_, s32[1560]{0:T(1024)} %fusion.5.refs_2_, bf16[120,128,128]{2,1,0:T(8,128)(2,1)} %bitcast.refs_3_.refs_4_, bf16[120,128,128]{2,1,0:T(8,128)(2,1)} %collective-permute-done.14.refs_4_.refs_6_, ...), custom_call_target="tpu_custom_call", output_to_operand_aliasing={{}: (12, {})} | custom-call | flops 8589934592 | bytes 33554432 | tf_op jit(solution)/shard_map/second/pallas_call | solution.py:123
  197.1 1.2 copy-done.2
  198.3 12.6 %last.1 = bf16[256,128,128]{2,1,0:T(8,128)(2,1)} custom-call(s32[1]{0:T(128)} %bitcast.3.refs_0_, s32[1]{0:T(128)} %bitcast.79.refs_1_, s32[720]{0:T(1024)} %fusion.8.refs_2_, s32[256]{0:T(256)} %get-tuple-element.254.refs_3_, bf16[120,128,128]{2,1,0:T(8,128)(2,1)} %bitcast.refs_3_.refs_4_, bf16[120,128,128]{2,1,0:T(8,128)(2,1)} %collective-permute-done.11.refs_9_.refs_5_, ...), custom_call_target="tpu_custom_call" | custom-call | bytes 262144 | tf_op jit(solution)/shard_map/last/pallas_call | solution.py:184
  210.9 103.9 %all_to_all.21 = bf16[128,256,128]{2,1,0:T(8,128)(2,1)S(1)} all-to-all(bf16[128,256,128]{2,1,0:T(8,128)(2,1)} %bitcast.124), channel_id=1, replica_groups=mesh['row'=16,'col'=8] {'row','col'}, dimensions={0} | all-to-all | bytes 16777216 | tf_op jit(solution)/shard_map/all_to_all | solution.py:417
  314.8 4.1 %copied.1 = bf16[256,128,128]{2,1,0:T(8,128)(2,1)} custom-call(bf16[256,128,128]{2,1,0:T(8,128)(2,1)S(1)} %bitcast.123), custom_call_target="tpu_custom_call" | custom-call | tf_op jit(solution)/shard_map/copied/pallas_call | solution.py:222
  (114 shorter events, 7.4 us)
Async XLA Ops:
  0.6 2.0 copy-start.3
  0.7 15.9 %copy-start.4 = (s32[40]{0:T(128)S(1)}, s32[40]{0:T(128)}, u32[]{:S(2)}) copy-start(s32[40]{0:T(128)} %constant.118.clone) | copy-start | bytes 484
  0.7 22.1 %copy-start.5 = (s32[120,1]{0,1:T(1,128)S(1)}, s32[120,1]{0,1:T(1,128)}, u32[]{:S(2)}) copy-start(s32[120,1]{0,1:T(1,128)} %param.6) | copy-start | bytes 1444
  0.7 13.5 %collective-permute-start.2 = (bf16[120,128,128]{2,1,0:T(8,128)(2,1)}, bf16[120,128,128]{2,1,0:T(8,128)(2,1)}, u32[]{:S(2)}, u32[]{:S(2)}) collective-permute-start(bf16[120,128,128]{2,1,0:T(8,128)(2,1)} %bitcast.refs_3_.refs_4_), channel_id=1, source_target_pairs={{0,8},{1,9},{2,10},{3,11},{4,12},{5,13},{6,14},{7,15},{8,0},{9,1},... | collective-permute-start | bytes 11796488 | tf_op jit(solution)/shard_map/ppermute | solution.py:261
  2.6 11.5 %collective-permute-start = (s32[5,24]{1,0:T(8,128)S(1)}, s32[5,24]{1,0:T(8,128)S(1)}, u32[]{:S(2)}, u32[]{:S(2)}) collective-permute-start(s32[5,24]{1,0:T(8,128)S(1)} %copy-done.3), channel_id=1, source_target_pairs={{0,1},{1,0},{2,3},{3,2},{4,5},{5,4},{6,7},{7,6},{8,9},{9,8},{10,11... | collective-permute-start | bytes 1448 | tf_op jit(solution)/shard_map/ppermute | solution.py:261
  4.3 9.9 %collective-permute-start.1 = (s32[5,24]{1,0:T(8,128)S(1)}, s32[5,24]{1,0:T(8,128)S(1)}, u32[]{:S(2)}, u32[]{:S(2)}) collective-permute-start(s32[5,24]{1,0:T(8,128)S(1)} %copy-done.3), channel_id=1, source_target_pairs={{0,7},{1,2},{2,1},{3,4},{4,3},{5,6},{6,5},{7,0},{8,15},{9,10},{10,... | collective-permute-start | bytes 1448 | tf_op jit(solution)/shard_map/ppermute | solution.py:261
  8.3 62.9 %collective-permute-start.5 = (bf16[72,128,128]{2,1,0:T(8,128)(2,1)S(1)}, bf16[72,128,128]{2,1,0:T(8,128)(2,1)}, u32[]{:S(2)}, u32[]{:S(2)}) collective-permute-start(bf16[72,128,128]{2,1,0:T(8,128)(2,1)S(1)} %bitcast.125), channel_id=1, source_target_pairs={{0,1},{1,0},{2,3},{3,2},{4,5},{5,4},{6,7},{7,6},{8,9},{9,8},{10,11... | collective-permute-start | bytes 7077896 | tf_op jit(solution)/shard_map/ppermute | solution.py:261
  8.3 54.2 %collective-permute-start.3 = (bf16[120,128,128]{2,1,0:T(8,128)(2,1)}, bf16[120,128,128]{2,1,0:T(8,128)(2,1)}, u32[]{:S(2)}, u32[]{:S(2)}) collective-permute-start(bf16[120,128,128]{2,1,0:T(8,128)(2,1)} %bitcast.refs_3_.refs_4_), channel_id=1, source_target_pairs={{0,121},{1,120},{2,123},{3,122},{4,125},{5,124},{6,127},{7,126},{8... | collective-permute-start | bytes 11796488 | tf_op jit(solution)/shard_map/ppermute | solution.py:261
  14.1 48.3 %collective-permute-start.4 = (bf16[120,128,128]{2,1,0:T(8,128)(2,1)}, bf16[120,128,128]{2,1,0:T(8,128)(2,1)}, u32[]{:S(2)}, u32[]{:S(2)}) collective-permute-start(bf16[120,128,128]{2,1,0:T(8,128)(2,1)} %bitcast.refs_3_.refs_4_), channel_id=1, source_target_pairs={{0,6},{1,3},{2,0},{3,5},{4,2},{5,7},{6,4},{7,1},{56,62},{57,59},{5... | collective-permute-start | bytes 11796488 | tf_op jit(solution)/shard_map/ppermute | solution.py:261
  16.6 48.1 %collective-permute-start.7 = (s32[3,5,24]{2,1,0:T(8,128)S(1)}, s32[3,5,24]{2,1,0:T(8,128)S(1)}, u32[]{:S(2)}, u32[]{:S(2)}) collective-permute-start(s32[3,5,24]{2,1,0:T(8,128)S(1)} %pad_add_fusion), channel_id=1, source_target_pairs={{0,120},{1,121},{2,122},{3,123},{4,124},{5,125},{6,126},{7,127},{8... | collective-permute-start | bytes 4328 | tf_op jit(solution)/shard_map/ppermute | solution.py:261
  19.1 43.4 %collective-permute-start.6 = (s32[3,5,24]{2,1,0:T(8,128)S(1)}, s32[3,5,24]{2,1,0:T(8,128)S(1)}, u32[]{:S(2)}, u32[]{:S(2)}) collective-permute-start(s32[3,5,24]{2,1,0:T(8,128)S(1)} %pad_add_fusion), channel_id=1, source_target_pairs={{0,8},{1,9},{2,10},{3,11},{4,12},{5,13},{6,14},{7,15},{8,0},{9,1},... | collective-permute-start | bytes 4328 | tf_op jit(solution)/shard_map/ppermute | solution.py:261
  24.4 44.7 %all-to-all-start = ((s32[128,1,2]{2,1,0:T(1,128)}), s32[128,1,2]{2,1,0:T(1,128)S(1)}, u32[]{:S(2)}, u32[]{:S(2)}) async-start(s32[128,1,2]{2,1,0:T(1,128)} %bitcast.10), calls=%async_computation | async-start | bytes 131072 | tf_op jit(solution)/shard_map/all_to_all | solution.py:345
  72.7 53.1 %collective-permute-start.9 = (bf16[72,128,128]{2,1,0:T(8,128)(2,1)}, bf16[72,128,128]{2,1,0:T(8,128)(2,1)}, u32[]{:S(2)}, u32[]{:S(2)}) collective-permute-start(bf16[72,128,128]{2,1,0:T(8,128)(2,1)} %collective-permute-done.5.refs_4_), channel_id=1, source_target_pairs={{0,2},{1,7},{2,4},{3,1},{4,6},{5,3},{6,0},{7,5},{8,10},{9,15},{10,... | collective-permute-start | bytes 7077896 | tf_op jit(solution)/shard_map/ppermute | solution.py:261
  73.0 52.7 %collective-permute-start.12 = (bf16[72,128,128]{2,1,0:T(8,128)(2,1)}, bf16[72,128,128]{2,1,0:T(8,128)(2,1)S(1)}, u32[]{:S(2)}, u32[]{:S(2)}) collective-permute-start(bf16[72,128,128]{2,1,0:T(8,128)(2,1)} %collective-permute-done.5.refs_4_), channel_id=1, source_target_pairs={{8,16},{9,17},{10,18},{11,19},{12,20},{13,21},{14,22},{15,23},{16,... | collective-permute-start | bytes 7077896 | tf_op jit(solution)/shard_map/ppermute | solution.py:261
  73.9 51.9 %collective-permute-start.10 = (bf16[72,128,128]{2,1,0:T(8,128)(2,1)}, bf16[72,128,128]{2,1,0:T(8,128)(2,1)}, u32[]{:S(2)}, u32[]{:S(2)}) collective-permute-start(bf16[72,128,128]{2,1,0:T(8,128)(2,1)} %collective-permute-done.5.refs_4_), channel_id=1, source_target_pairs={{0,8},{1,9},{2,10},{3,11},{4,12},{5,13},{6,14},{7,15},{8,0},{9,1},... | collective-permute-start | bytes 7077896 | tf_op jit(solution)/shard_map/ppermute | solution.py:261
  74.3 51.5 %collective-permute-start.11 = (bf16[120,128,128]{2,1,0:T(8,128)(2,1)}, bf16[120,128,128]{2,1,0:T(8,128)(2,1)}, u32[]{:S(2)}, u32[]{:S(2)}) collective-permute-start(bf16[120,128,128]{2,1,0:T(8,128)(2,1)} %collective-permute-done.4), channel_id=1, source_target_pairs={{0,121},{1,120},{2,123},{3,122},{4,125},{5,124},{6,127},{7,126},{5... | collective-permute-start | bytes 11796488 | tf_op jit(solution)/shard_map/ppermute | solution.py:261
  83.1 42.6 %collective-permute-start.8 = (bf16[48,128,128]{2,1,0:T(8,128)(2,1)}, bf16[48,128,128]{2,1,0:T(8,128)(2,1)S(1)}, u32[]{:S(2)}, u32[]{:S(2)}) collective-permute-start(bf16[48,128,128]{2,1,0:T(8,128)(2,1)} %slice.254), channel_id=1, source_target_pairs={{0,1},{1,0},{2,3},{3,2},{4,5},{5,4},{6,7},{7,6},{8,9},{9,8},{10,11... | collective-permute-start | bytes 4718600 | tf_op jit(solution)/shard_map/ppermute | solution.py:261
  125.7 1.2 copy-start.6
  125.8 23.9 %copy-start = (bf16[72,128,128]{2,1,0:T(8,128)(2,1)}, bf16[72,128,128]{2,1,0:T(8,128)(2,1)S(1)}, u32[]{:S(2)}) copy-start(bf16[72,128,128]{2,1,0:T(8,128)(2,1)S(1)} %collective-permute-done.12.refs_5_) | copy-start | bytes 7077892
  126.9 47.9 %collective-permute-start.14 = (bf16[120,128,128]{2,1,0:T(8,128)(2,1)}, bf16[120,128,128]{2,1,0:T(8,128)(2,1)}, u32[]{:S(2)}, u32[]{:S(2)}) collective-permute-start(bf16[120,128,128]{2,1,0:T(8,128)(2,1)} %collective-permute-done.3.refs_5_), channel_id=1, source_target_pairs={{0,1},{1,0},{2,3},{3,2},{4,5},{5,4},{6,7},{7,6},{56,57},{57,56},{5... | collective-permute-start | bytes 11796488 | tf_op jit(solution)/shard_map/ppermute | solution.py:261
  128.9 20.8 %collective-permute-start.17 = (bf16[72,128,128]{2,1,0:T(8,128)(2,1)}, bf16[72,128,128]{2,1,0:T(8,128)(2,1)S(1)}, u32[]{:S(2)}, u32[]{:S(2)}) collective-permute-start(bf16[72,128,128]{2,1,0:T(8,128)(2,1)} %collective-permute-done.9.refs_6_), channel_id=1, source_target_pairs={{8,16},{9,17},{10,18},{11,19},{12,20},{13,21},{14,22},{15,23},{16,... | collective-permute-start | bytes 7077896 | tf_op jit(solution)/shard_map/ppermute | solution.py:261
  129.7 45.2 %collective-permute-start.13 = (bf16[72,128,128]{2,1,0:T(8,128)(2,1)}, bf16[72,128,128]{2,1,0:T(8,128)(2,1)}, u32[]{:S(2)}, u32[]{:S(2)}) collective-permute-start(bf16[72,128,128]{2,1,0:T(8,128)(2,1)} %collective-permute-done.9.refs_6_), channel_id=1, source_target_pairs={{0,8},{1,9},{2,10},{3,11},{4,12},{5,13},{6,14},{7,15},{8,0},{9,1},... | collective-permute-start | bytes 7077896 | tf_op jit(solution)/shard_map/ppermute | solution.py:261
  132.4 18.6 %collective-permute-start.16 = (bf16[48,128,128]{2,1,0:T(8,128)(2,1)}, bf16[48,128,128]{2,1,0:T(8,128)(2,1)}, u32[]{:S(2)}, u32[]{:S(2)}) collective-permute-start(bf16[48,128,128]{2,1,0:T(8,128)(2,1)} %copy-done.6), channel_id=1, source_target_pairs={{8,16},{9,17},{10,18},{11,19},{12,20},{13,21},{14,22},{15,23},{16,... | collective-permute-start | bytes 4718600 | tf_op jit(solution)/shard_map/ppermute | solution.py:261
  134.3 38.7 %collective-permute-start.15 = (bf16[48,128,128]{2,1,0:T(8,128)(2,1)}, bf16[48,128,128]{2,1,0:T(8,128)(2,1)}, u32[]{:S(2)}, u32[]{:S(2)}) collective-permute-start(bf16[48,128,128]{2,1,0:T(8,128)(2,1)} %copy-done.6), channel_id=1, source_target_pairs={{0,2},{1,7},{2,4},{3,1},{4,6},{5,3},{6,0},{7,5},{8,10},{9,15},{10,... | collective-permute-start | bytes 4718600 | tf_op jit(solution)/shard_map/ppermute | solution.py:261
  149.6 1.4 copy-start.1
  174.8 22.2 %collective-permute-start.20 = (bf16[48,128,128]{2,1,0:T(8,128)(2,1)}, bf16[48,128,128]{2,1,0:T(8,128)(2,1)S(1)}, u32[]{:S(2)}, u32[]{:S(2)}) collective-permute-start(bf16[48,128,128]{2,1,0:T(8,128)(2,1)} %collective-permute-done.15.refs_8_), channel_id=1, source_target_pairs={{8,16},{9,17},{10,18},{11,19},{12,20},{13,21},{14,22},{15,23},{16,... | collective-permute-start | bytes 4718600 | tf_op jit(solution)/shard_map/ppermute | solution.py:261
  175.6 21.4 %collective-permute-start.19 = (bf16[48,128,128]{2,1,0:T(8,128)(2,1)}, bf16[48,128,128]{2,1,0:T(8,128)(2,1)}, u32[]{:S(2)}, u32[]{:S(2)}) collective-permute-start(bf16[48,128,128]{2,1,0:T(8,128)(2,1)} %collective-permute-done.15.refs_8_), channel_id=1, source_target_pairs={{0,8},{1,9},{2,10},{3,11},{4,12},{5,13},{6,14},{7,15},{8,0},{9,1},... | collective-permute-start | bytes 4718600 | tf_op jit(solution)/shard_map/ppermute | solution.py:261
  179.7 17.3 %collective-permute-start.18 = (bf16[48,128,128]{2,1,0:T(8,128)(2,1)}, bf16[48,128,128]{2,1,0:T(8,128)(2,1)}, u32[]{:S(2)}, u32[]{:S(2)}) collective-permute-start(bf16[48,128,128]{2,1,0:T(8,128)(2,1)} %copy-done.6), channel_id=1, source_target_pairs={{0,8},{1,9},{2,10},{3,11},{4,12},{5,13},{6,14},{7,15},{8,0},{9,1},... | collective-permute-start | bytes 4718600 | tf_op jit(solution)/shard_map/ppermute | solution.py:261
  197.0 1.2 copy-start.2

commit v5 on v4

--- a/solution.py
+++ b/solution.py
@@ -6,7 +6,7 @@
 from jax.sharding import PartitionSpec as P
 
 AXES = ("row", "col")
-UNROLL = 24
+UNROLL = 32
 
 
 def at_wrap(r, rows):

time: 320 us -> 320 us (level)
  no operation moved by 1% of the time
where the time goes in v5:
time: 320 us; the launch traced here: 319 us
  blocking collectives  105 us (33%)
  Pallas kernels  73.6 us (23%)
  waiting for transfers between devices  69.4 us (22%)
  starting transfers between devices  39.9 us (12%)
  other arithmetic  17.5 us (5%)
  local copies, waits for them, and re-layouts  12.2 us (4%)
    all_to_all x1, blocking collectives, shards(): lax.all_to_all(outgoing.reshape(-1, order), AXES, split_axis=0, concat_ax...  105 us
    ppermute x21, waiting for transfers between devices, send(): return lax.ppermute(after(x), AXES, perms[which])  69.3 us
    pallas_call x4, Pallas kernels, accumulate(): pl.pallas_call(body, out_shape=jax.ShapeDtypeStruct((slots, order, order)...  57.2 us
    ppermute x21, starting transfers between devices, send(): return lax.ppermute(after(x), AXES, perms[which])  33.5 us
    pallas_call x1, Pallas kernels, finish(): pl.pallas_call(body, out_shape=jax.ShapeDtypeStruct((slots, order, order)...  12.2 us
  transfers between devices with their start and end apart: 22, of which 5 were waited for; matrix products, arithmetic and copies ran while one was open for 7% of the time, Pallas kernels for 18%

profile of v5, /device:TPU:0, one launch (start us, length us, event | category | flops | bytes accessed | tf_op | source)
XLA Modules:
  0.0 319.1 jit_solution(1346961507073810167)
XLA Ops:
  0.8 1.8 slice.252
  2.6 1.7 collective-permute-start
  4.3 4.0 %collective-permute-start.1 = (s32[5,24]{1,0:T(8,128)S(1)}, s32[5,24]{1,0:T(8,128)S(1)}, u32[]{:S(2)}, u32[]{:S(2)}) collective-permute-start(s32[5,24]{1,0:T(8,128)S(1)} %copy-done.3), channel_id=1, source_target_pairs={{0,7},{1,2},{2,1},{3,4},{4,3},{5,6},{6,5},{7,0},{8,15},{9,10},{10,... | collective-permute-start | bytes 1448 | tf_op jit(solution)/shard_map/ppermute | solution.py:261
  8.3 5.3 %collective-permute-start.3 = (bf16[120,128,128]{2,1,0:T(8,128)(2,1)}, bf16[120,128,128]{2,1,0:T(8,128)(2,1)}, u32[]{:S(2)}, u32[]{:S(2)}) collective-permute-start(bf16[120,128,128]{2,1,0:T(8,128)(2,1)} %bitcast.refs_3_.refs_4_), channel_id=1, source_target_pairs={{0,121},{1,120},{2,123},{3,122},{4,125},{5,124},{6,127},{7,126},{8... | collective-permute-start | bytes 11796488 | tf_op jit(solution)/shard_map/ppermute | solution.py:261
  14.1 2.3 collective-permute-start.4
  16.6 2.5 collective-permute-start.7
  19.1 0.6 select_reduce_fusion.6
  19.7 0.7 convert_reduce_fusion.5
  21.5 1.2 fusion.7.refs_2_
  23.1 0.5 broadcast_add_fusion
  23.6 0.8 all_to_all.14
  24.4 6.4 %all-to-all-start = ((s32[128,1,2]{2,1,0:T(1,128)}), s32[128,1,2]{2,1,0:T(1,128)S(1)}, u32[]{:S(2)}, u32[]{:S(2)}) async-start(s32[128,1,2]{2,1,0:T(1,128)} %bitcast.10), calls=%async_computation | async-start | bytes 131072 | tf_op jit(solution)/shard_map/all_to_all | solution.py:345
  30.8 11.4 %own.1.refs_6_ = f32[128,128,128]{2,1,0:T(8,128)} custom-call(s32[1]{0:T(128)} %bitcast.3.refs_0_, s32[1]{0:T(128)} %bitcast.6.refs_1_, s32[608]{0:T(1024)} %fusion.7.refs_2_, bf16[120,128,128]{2,1,0:T(8,128)(2,1)} %bitcast.refs_3_.refs_4_, bf16[120,128,128]{2,1,0:T(8,128)(2,1)} %bitcast.refs_3_.refs_4_), custom_call_target="tpu_custom_call" | custom-call | flops 8589934592 | bytes 33554432 | tf_op jit(solution)/shard_map/own/pallas_call | solution.py:123
  42.2 2.7 slice.254
  44.9 17.6 %collective-permute-done.4 = bf16[120,128,128]{2,1,0:T(8,128)(2,1)} collective-permute-done((bf16[120,128,128]{2,1,0:T(8,128)(2,1)}, bf16[120,128,128]{2,1,0:T(8,128)(2,1)}, u32[]{:S(2)}, u32[]{:S(2)}) %collective-permute-start.4) | collective-permute-done | bytes 3932192 | tf_op jit(solution)/shard_map/ppermute | solution.py:261
  62.5 2.2 collective-permute-done.7
  65.7 0.7 convert_reduce_fusion.3
  67.1 0.8 select_reduce_fusion.2
  68.0 1.2 fusion.4.refs_2_
  69.2 0.7 convert_reduce_fusion.2
  69.9 0.7 convert_reduce_fusion.1
  70.6 0.7 convert_reduce_fusion
  73.1 0.8 collective-permute-start.12
  74.3 3.8 %collective-permute-start.11 = (bf16[120,128,128]{2,1,0:T(8,128)(2,1)}, bf16[120,128,128]{2,1,0:T(8,128)(2,1)}, u32[]{:S(2)}, u32[]{:S(2)}) collective-permute-start(bf16[120,128,128]{2,1,0:T(8,128)(2,1)} %collective-permute-done.4), channel_id=1, source_target_pairs={{0,121},{1,120},{2,123},{3,122},{4,125},{5,124},{6,127},{7,126},{5... | collective-permute-start | bytes 11796488 | tf_op jit(solution)/shard_map/ppermute | solution.py:261
  78.3 0.9 select_reduce_fusion.1
  79.2 1.2 fusion.6.refs_2_
  80.9 1.3 select_reduce_fusion
  82.2 1.1 fusion.5.refs_2_
  83.9 1.1 fusion.8.refs_2_
  85.1 15.0 %core.1.refs_8_ = f32[128,128,128]{2,1,0:T(8,128)} custom-call(s32[1]{0:T(128)} %bitcast.3.refs_0_, s32[1]{0:T(128)} %bitcast.76.refs_1_, s32[1216]{0:T(1024)} %fusion.4.refs_2_, bf16[120,128,128]{2,1,0:T(8,128)(2,1)} %bitcast.refs_3_.refs_4_, bf16[120,128,128]{2,1,0:T(8,128)(2,1)} %collective-permute-done.2.refs_4_, ...), custom_call_target="tpu_custom_call", output_to_operand_aliasing={{}: (6, {})} | custom-call | flops 8589934592 | bytes 33554432 | tf_op jit(solution)/shard_map/core/pallas_call | solution.py:123
  100.1 25.7 %collective-permute-done.9.refs_6_ = bf16[72,128,128]{2,1,0:T(8,128)(2,1)} collective-permute-done((bf16[72,128,128]{2,1,0:T(8,128)(2,1)}, bf16[72,128,128]{2,1,0:T(8,128)(2,1)}, u32[]{:S(2)}, u32[]{:S(2)}) %collective-permute-start.9) | collective-permute-done | bytes 2359328 | tf_op jit(solution)/shard_map/ppermute | solution.py:261
  125.8 1.2 copy-done.6
  126.9 1.9 collective-permute-start.14
  128.9 0.8 collective-permute-start.17
  129.7 2.7 collective-permute-start.13
  132.4 1.9 collective-permute-start.16
  134.3 15.2 %first.1.refs_12_ = f32[128,128,128]{2,1,0:T(8,128)} custom-call(s32[1]{0:T(128)} %bitcast.3.refs_0_, s32[1]{0:T(128)} %bitcast.85.refs_1_, s32[1344]{0:T(1024)} %fusion.6.refs_2_, bf16[120,128,128]{2,1,0:T(8,128)(2,1)} %bitcast.refs_3_.refs_4_, bf16[72,128,128]{2,1,0:T(8,128)(2,1)} %collective-permute-done.5.refs_4_, ...), custom_call_target="tpu_custom_call", output_to_operand_aliasing={{}: (8, {})} | custom-call | flops 8589934592 | bytes 33554432 | tf_op jit(solution)/shard_map/first/pallas_call | solution.py:123
  149.6 1.4 copy-done.1
  151.0 22.0 %collective-permute-done.15.refs_8_ = bf16[48,128,128]{2,1,0:T(8,128)(2,1)} collective-permute-done((bf16[48,128,128]{2,1,0:T(8,128)(2,1)}, bf16[48,128,128]{2,1,0:T(8,128)(2,1)}, u32[]{:S(2)}, u32[]{:S(2)}) %collective-permute-start.15) | collective-permute-done | bytes 1572896 | tf_op jit(solution)/shard_map/ppermute | solution.py:261
  173.0 1.8 collective-permute-done.14.refs_4_.refs_6_
  174.8 0.8 collective-permute-start.20
  175.6 4.1 %collective-permute-start.19 = (bf16[48,128,128]{2,1,0:T(8,128)(2,1)}, bf16[48,128,128]{2,1,0:T(8,128)(2,1)}, u32[]{:S(2)}, u32[]{:S(2)}) collective-permute-start(bf16[48,128,128]{2,1,0:T(8,128)(2,1)} %collective-permute-done.15.refs_8_), channel_id=1, source_target_pairs={{0,8},{1,9},{2,10},{3,11},{4,12},{5,13},{6,14},{7,15},{8,0},{9,1},... | collective-permute-start | bytes 4718600 | tf_op jit(solution)/shard_map/ppermute | solution.py:261
  179.8 0.7 reshape.356
  180.5 15.6 %second.1.refs_9_ = f32[128,128,128]{2,1,0:T(8,128)} custom-call(s32[1]{0:T(128)} %bitcast.3.refs_0_, s32[1]{0:T(128)} %bitcast.82.refs_1_, s32[1568]{0:T(1024)} %fusion.5.refs_2_, bf16[120,128,128]{2,1,0:T(8,128)(2,1)} %bitcast.refs_3_.refs_4_, bf16[120,128,128]{2,1,0:T(8,128)(2,1)} %collective-permute-done.14.refs_4_.refs_6_, ...), custom_call_target="tpu_custom_call", output_to_operand_aliasing={{}: (12, {})} | custom-call | flops 8589934592 | bytes 33554432 | tf_op jit(solution)/shard_map/second/pallas_call | solution.py:123
  196.2 1.2 copy-done.2
  197.4 12.2 %last.1 = bf16[256,128,128]{2,1,0:T(8,128)(2,1)} custom-call(s32[1]{0:T(128)} %bitcast.3.refs_0_, s32[1]{0:T(128)} %bitcast.79.refs_1_, s32[736]{0:T(1024)} %fusion.8.refs_2_, s32[256]{0:T(256)} %get-tuple-element.254.refs_3_, bf16[120,128,128]{2,1,0:T(8,128)(2,1)} %bitcast.refs_3_.refs_4_, bf16[120,128,128]{2,1,0:T(8,128)(2,1)} %collective-permute-done.11.refs_9_.refs_5_, ...), custom_call_target="tpu_custom_call" | custom-call | bytes 262144 | tf_op jit(solution)/shard_map/last/pallas_call | solution.py:184
  209.6 105.2 %all_to_all.21 = bf16[128,256,128]{2,1,0:T(8,128)(2,1)S(1)} all-to-all(bf16[128,256,128]{2,1,0:T(8,128)(2,1)} %bitcast.124), channel_id=1, replica_groups=mesh['row'=16,'col'=8] {'row','col'}, dimensions={0} | all-to-all | bytes 16777216 | tf_op jit(solution)/shard_map/all_to_all | solution.py:417
  314.8 4.1 %copied.1 = bf16[256,128,128]{2,1,0:T(8,128)(2,1)} custom-call(bf16[256,128,128]{2,1,0:T(8,128)(2,1)S(1)} %bitcast.123), custom_call_target="tpu_custom_call" | custom-call | tf_op jit(solution)/shard_map/copied/pallas_call | solution.py:222
  (114 shorter events, 7.3 us)
Async XLA Ops:
  0.6 2.0 copy-start.3
  0.7 15.9 %copy-start.4 = (s32[40]{0:T(128)S(1)}, s32[40]{0:T(128)}, u32[]{:S(2)}) copy-start(s32[40]{0:T(128)} %constant.118.clone) | copy-start | bytes 484
  0.7 22.1 %copy-start.5 = (s32[120,1]{0,1:T(1,128)S(1)}, s32[120,1]{0,1:T(1,128)}, u32[]{:S(2)}) copy-start(s32[120,1]{0,1:T(1,128)} %param.6) | copy-start | bytes 1444
  0.7 13.5 %collective-permute-start.2 = (bf16[120,128,128]{2,1,0:T(8,128)(2,1)}, bf16[120,128,128]{2,1,0:T(8,128)(2,1)}, u32[]{:S(2)}, u32[]{:S(2)}) collective-permute-start(bf16[120,128,128]{2,1,0:T(8,128)(2,1)} %bitcast.refs_3_.refs_4_), channel_id=1, source_target_pairs={{0,8},{1,9},{2,10},{3,11},{4,12},{5,13},{6,14},{7,15},{8,0},{9,1},... | collective-permute-start | bytes 11796488 | tf_op jit(solution)/shard_map/ppermute | solution.py:261
  2.6 11.5 %collective-permute-start = (s32[5,24]{1,0:T(8,128)S(1)}, s32[5,24]{1,0:T(8,128)S(1)}, u32[]{:S(2)}, u32[]{:S(2)}) collective-permute-start(s32[5,24]{1,0:T(8,128)S(1)} %copy-done.3), channel_id=1, source_target_pairs={{0,1},{1,0},{2,3},{3,2},{4,5},{5,4},{6,7},{7,6},{8,9},{9,8},{10,11... | collective-permute-start | bytes 1448 | tf_op jit(solution)/shard_map/ppermute | solution.py:261
  4.3 9.9 %collective-permute-start.1 = (s32[5,24]{1,0:T(8,128)S(1)}, s32[5,24]{1,0:T(8,128)S(1)}, u32[]{:S(2)}, u32[]{:S(2)}) collective-permute-start(s32[5,24]{1,0:T(8,128)S(1)} %copy-done.3), channel_id=1, source_target_pairs={{0,7},{1,2},{2,1},{3,4},{4,3},{5,6},{6,5},{7,0},{8,15},{9,10},{10,... | collective-permute-start | bytes 1448 | tf_op jit(solution)/shard_map/ppermute | solution.py:261
  8.3 63.0 %collective-permute-start.5 = (bf16[72,128,128]{2,1,0:T(8,128)(2,1)S(1)}, bf16[72,128,128]{2,1,0:T(8,128)(2,1)}, u32[]{:S(2)}, u32[]{:S(2)}) collective-permute-start(bf16[72,128,128]{2,1,0:T(8,128)(2,1)S(1)} %bitcast.125), channel_id=1, source_target_pairs={{0,1},{1,0},{2,3},{3,2},{4,5},{5,4},{6,7},{7,6},{8,9},{9,8},{10,11... | collective-permute-start | bytes 7077896 | tf_op jit(solution)/shard_map/ppermute | solution.py:261
  8.3 54.2 %collective-permute-start.3 = (bf16[120,128,128]{2,1,0:T(8,128)(2,1)}, bf16[120,128,128]{2,1,0:T(8,128)(2,1)}, u32[]{:S(2)}, u32[]{:S(2)}) collective-permute-start(bf16[120,128,128]{2,1,0:T(8,128)(2,1)} %bitcast.refs_3_.refs_4_), channel_id=1, source_target_pairs={{0,121},{1,120},{2,123},{3,122},{4,125},{5,124},{6,127},{7,126},{8... | collective-permute-start | bytes 11796488 | tf_op jit(solution)/shard_map/ppermute | solution.py:261
  14.1 48.3 %collective-permute-start.4 = (bf16[120,128,128]{2,1,0:T(8,128)(2,1)}, bf16[120,128,128]{2,1,0:T(8,128)(2,1)}, u32[]{:S(2)}, u32[]{:S(2)}) collective-permute-start(bf16[120,128,128]{2,1,0:T(8,128)(2,1)} %bitcast.refs_3_.refs_4_), channel_id=1, source_target_pairs={{0,6},{1,3},{2,0},{3,5},{4,2},{5,7},{6,4},{7,1},{56,62},{57,59},{5... | collective-permute-start | bytes 11796488 | tf_op jit(solution)/shard_map/ppermute | solution.py:261
  16.6 48.1 %collective-permute-start.7 = (s32[3,5,24]{2,1,0:T(8,128)S(1)}, s32[3,5,24]{2,1,0:T(8,128)S(1)}, u32[]{:S(2)}, u32[]{:S(2)}) collective-permute-start(s32[3,5,24]{2,1,0:T(8,128)S(1)} %pad_add_fusion), channel_id=1, source_target_pairs={{0,120},{1,121},{2,122},{3,123},{4,124},{5,125},{6,126},{7,127},{8... | collective-permute-start | bytes 4328 | tf_op jit(solution)/shard_map/ppermute | solution.py:261
  19.1 43.4 %collective-permute-start.6 = (s32[3,5,24]{2,1,0:T(8,128)S(1)}, s32[3,5,24]{2,1,0:T(8,128)S(1)}, u32[]{:S(2)}, u32[]{:S(2)}) collective-permute-start(s32[3,5,24]{2,1,0:T(8,128)S(1)} %pad_add_fusion), channel_id=1, source_target_pairs={{0,8},{1,9},{2,10},{3,11},{4,12},{5,13},{6,14},{7,15},{8,0},{9,1},... | collective-permute-start | bytes 4328 | tf_op jit(solution)/shard_map/ppermute | solution.py:261
  24.4 44.8 %all-to-all-start = ((s32[128,1,2]{2,1,0:T(1,128)}), s32[128,1,2]{2,1,0:T(1,128)S(1)}, u32[]{:S(2)}, u32[]{:S(2)}) async-start(s32[128,1,2]{2,1,0:T(1,128)} %bitcast.10), calls=%async_computation | async-start | bytes 131072 | tf_op jit(solution)/shard_map/all_to_all | solution.py:345
  72.8 53.0 %collective-permute-start.9 = (bf16[72,128,128]{2,1,0:T(8,128)(2,1)}, bf16[72,128,128]{2,1,0:T(8,128)(2,1)}, u32[]{:S(2)}, u32[]{:S(2)}) collective-permute-start(bf16[72,128,128]{2,1,0:T(8,128)(2,1)} %collective-permute-done.5.refs_4_), channel_id=1, source_target_pairs={{0,2},{1,7},{2,4},{3,1},{4,6},{5,3},{6,0},{7,5},{8,10},{9,15},{10,... | collective-permute-start | bytes 7077896 | tf_op jit(solution)/shard_map/ppermute | solution.py:261
  73.1 52.6 %collective-permute-start.12 = (bf16[72,128,128]{2,1,0:T(8,128)(2,1)}, bf16[72,128,128]{2,1,0:T(8,128)(2,1)S(1)}, u32[]{:S(2)}, u32[]{:S(2)}) collective-permute-start(bf16[72,128,128]{2,1,0:T(8,128)(2,1)} %collective-permute-done.5.refs_4_), channel_id=1, source_target_pairs={{8,16},{9,17},{10,18},{11,19},{12,20},{13,21},{14,22},{15,23},{16,... | collective-permute-start | bytes 7077896 | tf_op jit(solution)/shard_map/ppermute | solution.py:261
  73.9 51.8 %collective-permute-start.10 = (bf16[72,128,128]{2,1,0:T(8,128)(2,1)}, bf16[72,128,128]{2,1,0:T(8,128)(2,1)}, u32[]{:S(2)}, u32[]{:S(2)}) collective-permute-start(bf16[72,128,128]{2,1,0:T(8,128)(2,1)} %collective-permute-done.5.refs_4_), channel_id=1, source_target_pairs={{0,8},{1,9},{2,10},{3,11},{4,12},{5,13},{6,14},{7,15},{8,0},{9,1},... | collective-permute-start | bytes 7077896 | tf_op jit(solution)/shard_map/ppermute | solution.py:261
  74.3 51.5 %collective-permute-start.11 = (bf16[120,128,128]{2,1,0:T(8,128)(2,1)}, bf16[120,128,128]{2,1,0:T(8,128)(2,1)}, u32[]{:S(2)}, u32[]{:S(2)}) collective-permute-start(bf16[120,128,128]{2,1,0:T(8,128)(2,1)} %collective-permute-done.4), channel_id=1, source_target_pairs={{0,121},{1,120},{2,123},{3,122},{4,125},{5,124},{6,127},{7,126},{5... | collective-permute-start | bytes 11796488 | tf_op jit(solution)/shard_map/ppermute | solution.py:261
  83.4 42.4 %collective-permute-start.8 = (bf16[48,128,128]{2,1,0:T(8,128)(2,1)}, bf16[48,128,128]{2,1,0:T(8,128)(2,1)S(1)}, u32[]{:S(2)}, u32[]{:S(2)}) collective-permute-start(bf16[48,128,128]{2,1,0:T(8,128)(2,1)} %slice.254), channel_id=1, source_target_pairs={{0,1},{1,0},{2,3},{3,2},{4,5},{5,4},{6,7},{7,6},{8,9},{9,8},{10,11... | collective-permute-start | bytes 4718600 | tf_op jit(solution)/shard_map/ppermute | solution.py:261
  125.7 1.2 copy-start.6
  125.8 23.8 %copy-start = (bf16[72,128,128]{2,1,0:T(8,128)(2,1)}, bf16[72,128,128]{2,1,0:T(8,128)(2,1)S(1)}, u32[]{:S(2)}) copy-start(bf16[72,128,128]{2,1,0:T(8,128)(2,1)S(1)} %collective-permute-done.12.refs_5_) | copy-start | bytes 7077892
  126.9 47.9 %collective-permute-start.14 = (bf16[120,128,128]{2,1,0:T(8,128)(2,1)}, bf16[120,128,128]{2,1,0:T(8,128)(2,1)}, u32[]{:S(2)}, u32[]{:S(2)}) collective-permute-start(bf16[120,128,128]{2,1,0:T(8,128)(2,1)} %collective-permute-done.3.refs_5_), channel_id=1, source_target_pairs={{0,1},{1,0},{2,3},{3,2},{4,5},{5,4},{6,7},{7,6},{56,57},{57,56},{5... | collective-permute-start | bytes 11796488 | tf_op jit(solution)/shard_map/ppermute | solution.py:261
  128.9 20.7 %collective-permute-start.17 = (bf16[72,128,128]{2,1,0:T(8,128)(2,1)}, bf16[72,128,128]{2,1,0:T(8,128)(2,1)S(1)}, u32[]{:S(2)}, u32[]{:S(2)}) collective-permute-start(bf16[72,128,128]{2,1,0:T(8,128)(2,1)} %collective-permute-done.9.refs_6_), channel_id=1, source_target_pairs={{8,16},{9,17},{10,18},{11,19},{12,20},{13,21},{14,22},{15,23},{16,... | collective-permute-start | bytes 7077896 | tf_op jit(solution)/shard_map/ppermute | solution.py:261
  129.7 45.2 %collective-permute-start.13 = (bf16[72,128,128]{2,1,0:T(8,128)(2,1)}, bf16[72,128,128]{2,1,0:T(8,128)(2,1)}, u32[]{:S(2)}, u32[]{:S(2)}) collective-permute-start(bf16[72,128,128]{2,1,0:T(8,128)(2,1)} %collective-permute-done.9.refs_6_), channel_id=1, source_target_pairs={{0,8},{1,9},{2,10},{3,11},{4,12},{5,13},{6,14},{7,15},{8,0},{9,1},... | collective-permute-start | bytes 7077896 | tf_op jit(solution)/shard_map/ppermute | solution.py:261
  132.4 18.6 %collective-permute-start.16 = (bf16[48,128,128]{2,1,0:T(8,128)(2,1)}, bf16[48,128,128]{2,1,0:T(8,128)(2,1)}, u32[]{:S(2)}, u32[]{:S(2)}) collective-permute-start(bf16[48,128,128]{2,1,0:T(8,128)(2,1)} %copy-done.6), channel_id=1, source_target_pairs={{8,16},{9,17},{10,18},{11,19},{12,20},{13,21},{14,22},{15,23},{16,... | collective-permute-start | bytes 4718600 | tf_op jit(solution)/shard_map/ppermute | solution.py:261
  134.3 38.7 %collective-permute-start.15 = (bf16[48,128,128]{2,1,0:T(8,128)(2,1)}, bf16[48,128,128]{2,1,0:T(8,128)(2,1)}, u32[]{:S(2)}, u32[]{:S(2)}) collective-permute-start(bf16[48,128,128]{2,1,0:T(8,128)(2,1)} %copy-done.6), channel_id=1, source_target_pairs={{0,2},{1,7},{2,4},{3,1},{4,6},{5,3},{6,0},{7,5},{8,10},{9,15},{10,... | collective-permute-start | bytes 4718600 | tf_op jit(solution)/shard_map/ppermute | solution.py:261
  149.5 1.4 copy-start.1
  174.8 21.3 %collective-permute-start.20 = (bf16[48,128,128]{2,1,0:T(8,128)(2,1)}, bf16[48,128,128]{2,1,0:T(8,128)(2,1)S(1)}, u32[]{:S(2)}, u32[]{:S(2)}) collective-permute-start(bf16[48,128,128]{2,1,0:T(8,128)(2,1)} %collective-permute-done.15.refs_8_), channel_id=1, source_target_pairs={{8,16},{9,17},{10,18},{11,19},{12,20},{13,21},{14,22},{15,23},{16,... | collective-permute-start | bytes 4718600 | tf_op jit(solution)/shard_map/ppermute | solution.py:261
  175.6 20.6 %collective-permute-start.19 = (bf16[48,128,128]{2,1,0:T(8,128)(2,1)}, bf16[48,128,128]{2,1,0:T(8,128)(2,1)}, u32[]{:S(2)}, u32[]{:S(2)}) collective-permute-start(bf16[48,128,128]{2,1,0:T(8,128)(2,1)} %collective-permute-done.15.refs_8_), channel_id=1, source_target_pairs={{0,8},{1,9},{2,10},{3,11},{4,12},{5,13},{6,14},{7,15},{8,0},{9,1},... | collective-permute-start | bytes 4718600 | tf_op jit(solution)/shard_map/ppermute | solution.py:261
  179.7 16.5 %collective-permute-start.18 = (bf16[48,128,128]{2,1,0:T(8,128)(2,1)}, bf16[48,128,128]{2,1,0:T(8,128)(2,1)}, u32[]{:S(2)}, u32[]{:S(2)}) collective-permute-start(bf16[48,128,128]{2,1,0:T(8,128)(2,1)} %copy-done.6), channel_id=1, source_target_pairs={{0,8},{1,9},{2,10},{3,11},{4,12},{5,13},{6,14},{7,15},{8,0},{9,1},... | collective-permute-start | bytes 4718600 | tf_op jit(solution)/shard_map/ppermute | solution.py:261
  196.2 1.2 copy-start.2
